TPU v7x, 32 devices: a whole 2x2x4 slice. The times are simulated.
32 devices in a mesh: dp: 8 (over y, x, core), mp: 4 (over z).
Axes of the slice: x: 2, y: 2, z: 4, core: 2. Of those that a mesh axis runs over, the one named last changes fastest.
Arguments:
- inputs: bfloat16 [8704, 1536], P(('dp', 'mp')), may hold values from -6 to 6
- cotangent: bfloat16 [8704, 1536], P(('dp', 'mp')), may hold values from -6 to 6
- token_mask: int32 [8704], P(('dp', 'mp')), may hold values 0 or 1
- order: int32 [8, 1088], P('dp'), may hold values from 0 to 1087, each once within a row
- lengths: int32 [8, 4], P('dp'), may hold values from 1 to 1024, 1088 in all within a row
- gains: bfloat16 [2, 1536], replicated, may hold values from 0.5 to 1.5
- w_in: bfloat16 [1536, 2048], P('dp', 'mp'), may hold values from -0.15625 to 0.15625
- w_gate: bfloat16 [1536, 2048], P('dp', 'mp'), may hold values from -0.15625 to 0.15625
- w_out: bfloat16 [2048, 1536], P('mp', 'dp'), may hold values from -0.5 to 0.5
- conv_weight: bfloat16 [4, 16, 128], P(None, 'mp', 'dp'), may hold values from -3 to 3
- chan_bias: bfloat16 [3, 16, 128], P(None, 'mp', 'dp'), may hold values from -3 to 3
- decay: bfloat16 [16, 128], P('mp', 'dp'), may hold values from -9 to -3
- gate_blocks: bfloat16 [2, 16, 128, 128], P(None, 'mp', 'dp'), may hold values from -0.5 to 0.5
- w_up: bfloat16 [1536, 4608], P('dp', 'mp'), may hold values from -0.15625 to 0.15625
- w_gate_ff: bfloat16 [1536, 4608], P('dp', 'mp'), may hold values from -0.15625 to 0.15625
- w_down: bfloat16 [4608, 1536], P('mp', 'dp'), may hold values from -0.1875 to 0.1875
Outputs:
- output: bfloat16 [8704, 1536], P(('dp', 'mp'))
- grad_inputs: bfloat16 [8704, 1536], P(('dp', 'mp'))
- grad_gains: float32 [2, 1536], P(None, ('dp', 'mp'))
- grad_w_in: float32 [1536, 2048], P('dp', 'mp')
- grad_w_gate: float32 [1536, 2048], P('dp', 'mp')
- grad_w_out: float32 [2048, 1536], P('mp', 'dp')
- grad_conv: float32 [4, 16, 128], P(None, 'mp', 'dp')
- grad_bias: float32 [3, 16, 128], P(None, 'mp', 'dp')
- grad_decay: float32 [16, 128], P('mp', 'dp')
- grad_gate_blocks: float32 [2, 16, 128, 128], P(None, 'mp', 'dp')
- grad_w_up: float32 [1536, 4608], P('dp', 'mp')
- grad_w_gate_ff: float32 [1536, 4608], P('dp', 'mp')
- grad_w_down: float32 [4608, 1536], P('mp', 'dp')
Inputs may be any that keep to these rules, and one draw needn't show every extreme that they name: Each row of order holds each of 0 to 1087 once. `lengths`: each row sums to 1088; its largest entry is 1024.
All inputs are finite; a program needn't handle non-finite values. No bound on the sum of `token_mask` on one device may be relied on, other than what follows from the above.
Results may differ from a plain program's by a relative error of at most 0.02.
Values may be sent and summed in bfloat16 or wider, within the bound.
A program may use at most 256 MiB of HBM per device.

v0:
```python
import functools

import jax
import jax.numpy as jnp
from jax import lax
from jax.experimental import pallas as pl
from jax.experimental.pallas import tpu as pltpu
from jax.sharding import PartitionSpec as P

epsilon = 1e-06
LANE = 128
SUB = 8
TAIL = 24
ROWS = 272
VMEM_MB = 60
f32 = jnp.float32
bf16 = jnp.bfloat16
GELU_C = 0.7978845608028654
GELU_A = 0.044715


def rms_scale(values):
    return lax.rsqrt(jnp.mean(values * values, axis=-1, keepdims=True) + epsilon)


def dot(left, right):
    return lax.dot_general(left, right, (((1,), (0,)), ((), ())), preferred_element_type=f32)


def dot_last(left, right):
    return lax.dot_general(left, right, (((1,), (1,)), ((), ())), preferred_element_type=f32)


def dot_first(left, right):
    return lax.dot_general(left, right, (((0,), (0,)), ((), ())), preferred_element_type=f32)


def gelu_of(v):
    return 0.5 * v * (1.0 + jnp.tanh(GELU_C * (v + GELU_A * v * v * v)))


def gelu_both(v):
    square = v * v
    th = jnp.tanh(GELU_C * (v + GELU_A * v * square))
    half = 0.5 * (1.0 + th)
    slope = half + 0.5 * v * (1.0 - th * th) * (GELU_C * (1.0 + 3.0 * GELU_A * square))
    return v * half, slope


def sigmoid(v):
    return 0.5 * jnp.tanh(0.5 * v) + 0.5


def split(values):
    high = values.astype(bf16)
    return high, (values - high.astype(f32)).astype(bf16)


def rows_of(index, rows):
    return pl.ds(pl.multiple_of(index * rows, rows), rows)


def pick_rows(order_col, count):
    places = lax.broadcasted_iota(jnp.int32, (order_col.shape[0], count), 1)
    return (places == order_col).astype(f32).astype(bf16)


def put_rows(order_row, first, rows):
    places = lax.broadcasted_iota(jnp.int32, (rows, order_row.shape[1]), 0) + first
    return (places == order_row).astype(f32).astype(bf16)


def mixer_forward(
    tokens,
    ocol,
    orow,
    pos,
    w_in,
    w_gate,
    w_out,
    chan,
    blocks,
    gate_ref,
    branch_ref,
    conv_ref,
    gin_ref,
    grec_ref,
    state_ref,
    mixed_ref,
    out_ref,
    packed,
    rate,
    prod,
    before,
    low,
):
    count, _ = tokens.shape
    width = w_in.shape[1]
    steps = count // SUB
    heads = width // LANE

    def project(b, carry):
        at = rows_of(b, ROWS)
        packed[...] = dot(pick_rows(ocol[at, :], count), tokens[...]).astype(bf16)
        branch_ref[at, :] = dot(packed[...], w_in[...])
        gate_ref[at, :] = dot(packed[...], w_gate[...])
        return carry

    lax.fori_loop(0, count // ROWS, project, 0)

    for k in range(TAIL // SUB):
        last = branch_ref[pl.ds(count - TAIL + k * SUB, SUB), :]
        before[pl.ds(k * SUB, SUB), :] = pltpu.roll(last, 1, 0)
    before[pl.ds(TAIL, ROWS), :] = branch_ref[pl.ds(0, ROWS), :]

    def gates(b, carry):
        at = rows_of(b, ROWS)

        @pl.when(b > 0)
        def _():
            before[...] = branch_ref[pl.ds(pl.multiple_of(b * ROWS - TAIL, SUB), ROWS + TAIL), :]

        place = pos[at, :]
        for h in range(heads):
            lanes = pl.ds(h * LANE, LANE)
            par = chan[:, lanes]
            conv = par[4:5] + par[0:1] * before[pl.ds(TAIL, ROWS), lanes]
            for k in range(1, 4):
                earlier = before[pl.ds(TAIL - SUB * k, ROWS), lanes]
                conv = conv + par[k : k + 1] * jnp.where(place >= k, earlier, 0.0)
            high, rest = split(conv)
            pre = dot(jnp.concatenate([high, rest], axis=1), blocks[h])
            gate_in = sigmoid(pre[:, :LANE] + par[5:6])
            gate_rec = sigmoid(pre[:, LANE:] + par[6:7])
            kept = jnp.exp(-8.0 * gate_rec * par[7:8])
            drive = jnp.sqrt(1.0 - kept * kept + 0.01) * gate_in * conv
            conv_ref[at, lanes] = conv
            gin_ref[at, lanes] = gate_in
            grec_ref[at, lanes] = gate_rec
            rate[at, lanes] = jnp.where(place >= 1, kept, 0.0)
            state_ref[at, lanes] = drive
        return carry

    lax.fori_loop(0, count // ROWS, gates, 0)

    def scan(i, carry):
        held, passed = carry
        at = rows_of(i, SUB)
        a = rate[at, :]
        held = a * held + state_ref[at, :]
        passed = a * passed
        state_ref[at, :] = held
        prod[at, :] = passed
        return held, passed

    ends = lax.fori_loop(
        0, steps, scan, (jnp.zeros((SUB, width), f32), jnp.ones((SUB, width), f32)), unroll=8
    )
    first = lax.broadcasted_iota(jnp.int32, (SUB, width), 0) == 0
    carry_in = jnp.zeros((SUB, width), f32)
    for _ in range(SUB - 1):
        carry_in = jnp.where(first, 0.0, pltpu.roll(ends[0] + ends[1] * carry_in, 1, 0))

    def finish(i, carry):
        at = rows_of(i, 2 * SUB)
        twice = jnp.concatenate([carry_in, carry_in], axis=0)
        value = state_ref[at, :] + prod[at, :] * twice
        state_ref[at, :] = value
        low[at, :] = (gelu_of(gate_ref[at, :]) * value).astype(bf16)
        return carry

    lax.fori_loop(0, steps // 2, finish, 0, unroll=2)

    def leave(b, carry):
        at = rows_of(b, ROWS)
        mixed = dot(put_rows(orow[...], b * ROWS, ROWS), low[...]).astype(bf16)
        mixed_ref[at, :] = mixed
        out_ref[at, :] = dot(mixed, w_out[...]).astype(bf16)
        return carry

    lax.fori_loop(0, count // ROWS, leave, 0)


def ffn(
    tokens, cot, w_up, w_gate, w_down, part_ref, dnorm_ref, hidden_ref, dup_ref, dgate_ref
):
    def block(b, carry):
        at = rows_of(b, ROWS)
        up = dot(tokens[at, :], w_up[...])
        value, slope = gelu_both(dot(tokens[at, :], w_gate[...]))
        hidden = (value * up).astype(bf16)
        hidden_ref[at, :] = hidden
        d_hidden = dot_last(cot[at, :], w_down[...])
        d_up = (d_hidden * value).astype(bf16)
        d_gate = (d_hidden * up * slope).astype(bf16)
        dup_ref[at, :] = d_up
        dgate_ref[at, :] = d_gate
        dnorm_ref[at, :] = (dot_last(d_up, w_up[...]) + dot_last(d_gate, w_gate[...])).astype(bf16)
        part_ref[at, :] = dot(hidden, w_down[...]).astype(bf16)
        return carry

    lax.fori_loop(0, tokens.shape[0] // ROWS, block, 0)


def mixer_backward(
    back,
    norm,
    ocol,
    orow,
    pos,
    gain,
    w_in,
    w_gate,
    w_out,
    chan,
    blocks,
    gate_ref,
    branch_ref,
    conv_ref,
    gin_ref,
    grec_ref,
    state_ref,
    dcat_ref,
    dnorm_ref,
    small_ref,
    dblocks_ref,
    dgain_ref,
    dmix_arr,
    dmix,
    adj,
    prod,
    after,
    before,
    low,
):
    count, _ = back.shape
    width = w_in.shape[1]
    steps = count // SUB
    heads = width // LANE
    blocks_of = count // ROWS

    def enter(b, carry):
        at = rows_of(b, ROWS)
        dmix_arr[at, :] = dot_last(back[at, :], w_out[...]).astype(bf16)
        return carry

    lax.fori_loop(0, blocks_of, enter, 0)

    def pack(b, carry):
        at = rows_of(b, ROWS)
        d_mixed = dot(pick_rows(ocol[at, :], count), dmix_arr[...])
        value, slope = gelu_both(gate_ref[at, :])
        adj[at, :] = d_mixed * value
        low[at, pl.ds(width, width)] = (d_mixed * state_ref[at, :] * slope).astype(bf16)
        kept = jnp.exp(-8.0 * grec_ref[at, :] * chan[7:8, :])
        dmix[at, :] = jnp.where(pos[at, :] >= 1, kept, 0.0)
        return carry

    lax.fori_loop(0, blocks_of, pack, 0)

    def scan(i, carry):
        held, passed, following = carry
        at = rows_of(steps - 1 - i, SUB)
        held = following * held + adj[at, :]
        passed = following * passed
        adj[at, :] = held
        prod[at, :] = passed
        return held, passed, dmix[at, :]

    last = lax.broadcasted_iota(jnp.int32, (SUB, width), 0) == SUB - 1
    wrapped = jnp.where(last, 0.0, pltpu.roll(dmix[pl.ds(0, SUB), :], SUB - 1, 0))
    ends = lax.fori_loop(
        0,
        steps,
        scan,
        (jnp.zeros((SUB, width), f32), jnp.ones((SUB, width), f32), wrapped),
        unroll=8,
    )
    carry_in = jnp.zeros((SUB, width), f32)
    for _ in range(SUB - 1):
        carry_in = jnp.where(last, 0.0, pltpu.roll(ends[0] + ends[1] * carry_in, SUB - 1, 0))

    small_ref[...] = jnp.zeros_like(small_ref)
    dblocks_ref[...] = jnp.zeros_like(dblocks_ref)
    first = lax.broadcasted_iota(jnp.int32, (SUB, width), 0) == 0
    state_last = state_ref[pl.ds(count - SUB, SUB), :]
    before[pl.ds(TAIL - SUB, SUB), :] = jnp.where(first, 0.0, pltpu.roll(state_last, 1, 0))
    before[pl.ds(TAIL, ROWS), :] = state_ref[pl.ds(0, ROWS), :]
    wide_carry = jnp.concatenate([carry_in] * (ROWS // SUB), axis=0)

    def point(b, carry):
        at = rows_of(b, ROWS)

        @pl.when(b > 0)
        def _():
            before[...] = state_ref[pl.ds(pl.multiple_of(b * ROWS - TAIL, SUB), ROWS + TAIL), :]

        place = pos[at, :]
        for h in range(heads):
            lanes = pl.ds(h * LANE, LANE)
            par = chan[:, lanes]
            adjoint = adj[at, lanes] + prod[at, lanes] * wide_carry[:, h * LANE : (h + 1) * LANE]
            conv = conv_ref[at, lanes]
            gate_in = gin_ref[at, lanes]
            gate_rec = grec_ref[at, lanes]
            kept = jnp.exp(-8.0 * gate_rec * par[7:8])
            square = kept * kept
            inside = 1.0 - square + 0.01
            inverse = lax.rsqrt(inside)
            root = inside * inverse
            previous = before[pl.ds(TAIL - SUB, ROWS), lanes]
            d_log = adjoint * previous * dmix[at, lanes]
            scaled = adjoint * gate_in
            d_log = d_log - scaled * conv * square * inverse
            d_in = adjoint * root * conv * gate_in * (1.0 - gate_in)
            d_rec = d_log * (-8.0 * par[7:8]) * gate_rec * (1.0 - gate_rec)
            both = jnp.concatenate([d_in, d_rec], axis=1)
            high, rest = split(both)
            d_conv = scaled * root + dot_last(high, blocks[h]) + dot_last(rest, blocks[h])
            dblocks_ref[h] += dot_first(conv.astype(bf16), high)
            after[at, lanes] = d_conv
            small_ref[4:5, lanes] += jnp.sum(d_conv, axis=0, keepdims=True)
            small_ref[5:6, lanes] += jnp.sum(d_in, axis=0, keepdims=True)
            small_ref[6:7, lanes] += jnp.sum(d_rec, axis=0, keepdims=True)
            small_ref[7:8, lanes] += (
                jnp.sum(d_log * gate_rec, axis=0, keepdims=True) * (-8.0) * par[8:9]
            )
        return carry

    lax.fori_loop(0, blocks_of, point, 0)

    for k in range(TAIL // SUB):
        head = after[pl.ds(k * SUB, SUB), :]
        after[pl.ds(count + k * SUB, SUB), :] = pltpu.roll(head, SUB - 1, 0)
        tail = branch_ref[pl.ds(count - TAIL + k * SUB, SUB), :]
        before[pl.ds(k * SUB, SUB), :] = pltpu.roll(tail, 1, 0)
    before[pl.ds(TAIL, ROWS), :] = branch_ref[pl.ds(0, ROWS), :]

    def unmix(b, carry):
        at = rows_of(b, ROWS)

        @pl.when(b > 0)
        def _():
            before[...] = branch_ref[pl.ds(pl.multiple_of(b * ROWS - TAIL, SUB), ROWS + TAIL), :]

        place = pos[at, :]
        for h in range(heads):
            lanes = pl.ds(h * LANE, LANE)
            par = chan[:, lanes]
            d_conv = after[at, lanes]
            d_branch = par[0:1] * d_conv
            small_ref[0:1, lanes] += jnp.sum(
                d_conv * before[pl.ds(TAIL, ROWS), lanes], axis=0, keepdims=True
            )
            for k in range(1, 4):
                later = pl.ds(pl.multiple_of(b * ROWS + SUB * k, SUB), ROWS)
                d_branch = d_branch + par[k : k + 1] * jnp.where(
                    pos[later, :] >= k, after[later, lanes], 0.0
                )
                earlier = before[pl.ds(TAIL - SUB * k, ROWS), lanes]
                small_ref[k : k + 1, lanes] += jnp.sum(
                    jnp.where(place >= k, d_conv * earlier, 0.0), axis=0, keepdims=True
                )
            low[at, lanes] = d_branch.astype(bf16)
        return carry

    lax.fori_loop(0, blocks_of, unmix, 0)
    dgain_ref[...] = jnp.zeros_like(dgain_ref)

    def leave(b, carry):
        at = rows_of(b, ROWS)
        cat = dot(put_rows(orow[...], b * ROWS, ROWS), low[...]).astype(bf16)
        dcat_ref[at, :] = cat
        d_norm = dot_last(cat[:, :width], w_in[...]) + dot_last(cat[:, width:], w_gate[...])
        dgain_ref[...] += jnp.sum(d_norm * norm[at, :].astype(f32), axis=0, keepdims=True)
        dnorm_ref[at, :] = d_norm.astype(bf16)
        return carry

    lax.fori_loop(0, blocks_of, leave, 0)
    dgain_ref[...] = dgain_ref[...] / gain[...]


def local_call(body, outs, scratch, flops, args):
    whole = pl.BlockSpec(memory_space=pltpu.VMEM)
    moved = sum(a.size * a.dtype.itemsize for a in args)
    moved += sum(o.size * o.dtype.itemsize for o in outs)
    return pl.pallas_call(
        body,
        out_shape=outs,
        in_specs=[whole] * len(args),
        out_specs=[whole] * len(outs),
        scratch_shapes=scratch,
        compiler_params=pltpu.CompilerParams(vmem_limit_bytes=VMEM_MB << 20),
        cost_estimate=pl.CostEstimate(flops=flops, bytes_accessed=moved, transcendentals=0),
    )(*args)


def shape_of(dtype, *shape):
    return jax.ShapeDtypeStruct(shape, dtype)


def shards(
    inputs,
    cotangent,
    token_mask,
    order,
    lengths,
    gains,
    w_in,
    w_gate,
    w_out,
    conv_weight,
    chan_bias,
    decay,
    gate_blocks,
    w_up,
    w_gate_ff,
    w_down,
):
    n_dp = lax.axis_size("dp")
    local_rows, model = inputs.shape
    count = local_rows * lax.axis_size("mp")
    heads, piece = decay.shape
    width = heads * piece * n_dp
    hidden_width = w_up.shape[1]

    flat = jnp.concatenate(
        [conv_weight.reshape(-1, piece), chan_bias.reshape(-1, piece), decay]
        + [gate_blocks.transpose(0, 1, 3, 2).reshape(-1, piece)],
        axis=0,
    )
    small_all = lax.all_gather(flat, "dp", axis=1, tiled=True)
    full_in = lax.all_gather(w_in, "dp", axis=0, tiled=True)
    full_gate = lax.all_gather(w_gate, "dp", axis=0, tiled=True)
    full_out = lax.all_gather(w_out, "dp", axis=1, tiled=True)
    full_up = lax.all_gather(w_up, "dp", axis=0, tiled=True)
    full_gate_ff = lax.all_gather(w_gate_ff, "dp", axis=0, tiled=True)
    full_down = lax.all_gather(w_down, "dp", axis=1, tiled=True)

    params = small_all[: 8 * heads].astype(f32).reshape(8, width)
    decay_row = params[7:8]
    chan = jnp.concatenate(
        [params[:7], jax.nn.softplus(decay_row), jax.nn.sigmoid(decay_row), jnp.zeros((7, width), f32)],
        axis=0,
    )
    blocks = small_all[8 * heads :].reshape(2, heads, LANE, LANE)
    blocks = blocks.transpose(1, 3, 0, 2).reshape(heads, LANE, 2 * LANE)
    blocks_twice = jnp.concatenate([blocks, blocks], axis=1)

    steps = count // SUB
    ends = jnp.cumsum(lengths[0], dtype=jnp.int32)
    starts = ends - lengths[0]
    places = jnp.arange(count, dtype=jnp.int32)
    own_start = jnp.max(
        jnp.where(places[:, None] >= starts[None, :], starts[None, :], 0), axis=1
    )
    pos = (places - own_start).reshape(SUB, steps).T
    wrap = jnp.concatenate([pos[: TAIL // SUB, 1:], jnp.full((TAIL // SUB, 1), -1, jnp.int32)], axis=1)
    pos_col = jnp.concatenate([pos, wrap], axis=0).reshape(count + TAIL, 1)
    order_int = order[0].reshape(SUB, steps).T.reshape(count)
    ocol, orow = order_int.reshape(count, 1), order_int.reshape(1, count)

    gain_f = gains.astype(f32)
    x_local = inputs.astype(f32)
    norm_in = (x_local * rms_scale(x_local) * gain_f[0]).astype(bf16)
    norm_group = lax.all_gather(norm_in, "mp", axis=0, tiled=True)
    cot = cotangent.astype(f32) * token_mask.astype(f32)[:, None]
    cot_group = lax.all_gather(cot.astype(bf16), "mp", axis=0, tiled=True)

    wide = pltpu.VMEM((count, width), f32)
    saved = [shape_of(f32, count, width)] * 6
    *kept, mixed, back_part = local_call(
        mixer_forward,
        saved + [shape_of(bf16, count, width), shape_of(bf16, count, model)],
        [
            pltpu.VMEM((ROWS, model), bf16),
            wide,
            wide,
            pltpu.VMEM((ROWS + TAIL, width), f32),
            pltpu.VMEM((count, width), bf16),
        ],
        2 * count * (count * model + 3 * model * width),
        (norm_group, ocol, orow, pos_col, full_in, full_gate, full_out, chan, blocks_twice),
    )
    resid = x_local + lax.psum_scatter(back_part, "mp", scatter_dimension=0, tiled=True).astype(f32)
    rms_mid = rms_scale(resid)
    norm_mid = (resid * rms_mid * gain_f[1]).astype(bf16)
    norm_mid_group = lax.all_gather(norm_mid, "mp", axis=0, tiled=True)

    hid = shape_of(bf16, count, hidden_width)
    tok = shape_of(bf16, count, model)
    ffn_part, d_norm_part, hidden, d_up, d_gate_ff = local_call(
        ffn,
        [tok, tok, hid, hid, hid],
        [],
        12 * count * model * hidden_width,
        (norm_mid_group, cot_group, full_up, full_gate_ff, full_down),
    )
    d_norm_mid = lax.psum_scatter(d_norm_part, "mp", scatter_dimension=0, tiled=True).astype(f32)
    scaled = gain_f[1] * d_norm_mid
    gain_mid = jnp.sum(d_norm_mid * resid * rms_mid, axis=0)
    d_resid = (
        cot
        + rms_mid * scaled
        - resid * (rms_mid * rms_mid * rms_mid) * jnp.mean(resid * scaled, axis=-1, keepdims=True)
    )
    back_group = lax.all_gather(d_resid.astype(bf16), "mp", axis=0, tiled=True)
    output = (
        resid + lax.psum_scatter(ffn_part, "mp", scatter_dimension=0, tiled=True).astype(f32)
    ).astype(bf16)

    def reduced(grad, dimension):
        return lax.psum_scatter(grad.astype(bf16), "dp", scatter_dimension=dimension, tiled=True).astype(f32)

    grad_down = reduced(dot_first(hidden, cot_group), 1)
    grad_up = reduced(dot_first(norm_mid_group, d_up), 0)
    grad_gate_ff = reduced(dot_first(norm_mid_group, d_gate_ff), 0)

    d_cat, d_norm_back, small, d_blocks, gain_in = local_call(
        mixer_backward,
        [
            shape_of(bf16, count, 2 * width),
            tok,
            shape_of(f32, 8, width),
            shape_of(f32, heads, LANE, 2 * LANE),
            shape_of(f32, 1, model),
        ],
        [
            pltpu.VMEM((count, width), bf16),
            wide,
            wide,
            wide,
            pltpu.VMEM((count + TAIL, width), f32),
            pltpu.VMEM((ROWS + TAIL, width), f32),
            pltpu.VMEM((count, 2 * width), bf16),
        ],
        2 * count * (3 * count * width + 3 * model * width),
        (
            back_group,
            norm_group,
            ocol,
            orow,
            pos_col,
            gain_f[0:1],
            full_in,
            full_gate,
            full_out,
            chan,
            blocks,
            *kept,
        ),
    )
    d_norm_in = lax.psum_scatter(d_norm_back, "mp", scatter_dimension=0, tiled=True).astype(f32)
    grad_out = reduced(dot_first(mixed, back_group), 1)
    grad_cat = dot_first(norm_group, d_cat)
    grad_in = reduced(grad_cat[:, :width], 0)
    grad_gate = reduced(grad_cat[:, width:], 0)

    d_blocks_rows = d_blocks.reshape(heads, n_dp, piece, 2, LANE).transpose(1, 3, 0, 2, 4)
    small_rows = small.reshape(8 * heads, n_dp, piece).transpose(1, 0, 2)
    packed_small = jnp.concatenate(
        [small_rows.reshape(n_dp, -1), d_blocks_rows.reshape(n_dp, -1)], axis=1
    )
    small_own = lax.psum_scatter(packed_small, "dp", scatter_dimension=0, tiled=True)[0]
    split_at = 8 * heads * piece
    rows = small_own[:split_at].reshape(8, heads, piece)
    grad_blocks = small_own[split_at:].reshape(2, heads, piece, LANE)

    rms_in = rms_scale(x_local)
    e_in = gain_f[0] * d_norm_in
    grad_inputs = (
        d_resid
        + rms_in * e_in
        - x_local * (rms_in * rms_in * rms_in) * jnp.mean(x_local * e_in, axis=-1, keepdims=True)
    ).astype(bf16)
    grad_gains = lax.psum_scatter(
        jnp.stack([gain_in[0], gain_mid]), ("dp", "mp"), scatter_dimension=1, tiled=True
    )
    return (
        output,
        grad_inputs,
        grad_gains,
        grad_in,
        grad_gate,
        grad_out,
        rows[0:4],
        rows[4:7],
        rows[7],
        grad_blocks,
        grad_up,
        grad_gate_ff,
        grad_down,
    )


def solution(mesh):
    row, col = P("dp", "mp"), P("mp", "dp")
    tok = P(("dp", "mp"), None)
    chan = P(None, "mp", "dp")
    gate = P(None, "mp", "dp", None)
    return jax.shard_map(
        shards,
        mesh=mesh,
        in_specs=(
            tok, tok, P(("dp", "mp")), P("dp", None), P("dp", None), P(),
            row, row, col, chan, chan, col, gate, row, row, col,
        ),
        out_specs=(
            tok, tok, P(None, ("dp", "mp")), row, row, col, chan, chan, col, gate, row, row, col,
        ),
        check_vma=False,
    )
```

profile of v0, /device:TPU:0, one launch (start us, length us, event | category | flops | bytes accessed | tf_op | source)
XLA Modules:
  0.0 1247.6 jit_solution(6607764393217644918)
XLA Ops:
  15.9 10.9 all_gather.37
  31.0 7.9 all-gather.17.cloned.1.call-done
  41.5 25.0 %all-gather.13.cloned.1.call-done.w_in = bf16[1536,512]{1,0:T(8,128)(2,1)} async-done(((bf16[192,512]{1,0:T(8,128)(2,1)}), bf16[1536,512]{1,0:T(8,128)(2,1)}) %all-gather.13.cloned.1.call-update) | async-done | bytes 1572880 | tf_op jit(solution)/shard_map/all_gather | solution.py:433
  66.5 27.6 %all-gather.15.cloned.1.call-done.w_gate = bf16[1536,512]{1,0:T(8,128)(2,1)} async-done(((bf16[192,512]{1,0:T(8,128)(2,1)}), bf16[1536,512]{1,0:T(8,128)(2,1)}) %all-gather.15.cloned.1.call-update) | async-done | bytes 1572880 | tf_op jit(solution)/shard_map/all_gather | solution.py:434
  94.1 68.8 %all-gather.11.cloned.1.call-done.tokens.norm = bf16[1088,1536]{1,0:T(8,128)(2,1)} async-done(((bf16[272,1536]{1,0:T(8,128)(2,1)}), bf16[1088,1536]{1,0:T(8,128)(2,1)}) %all-gather.11.cloned.1.call-update) | async-done | bytes 3342352 | tf_op jit(solution)/shard_map/all_gather | solution.py:466
  162.9 27.2 %shard_map.255 = (f32[1088,512]{1,0:T(8,128)}, f32[1088,512]{1,0:T(8,128)}, f32[1088,512]{1,0:T(8,128)}, f32[1088,512]{1,0:T(8,128)}, f32[1088,512]{1,0:T(8,128)...) custom-call(bf16[1088,1536]{1,0:T(8,128)(2,1)} %all-gather.11.cloned.1.call-done.tokens.norm, ...), custom_call_target="tpu_custom_call" | custom-call | flops 8770289664 | bytes 26456928 | tf_op jit(solution)/shard_map/pallas_call | solution.py:387
  194.0 58.3 %reduce-scatter.14.cloned.1.call-done = bf16[272,1536]{1,0:T(8,128)(2,1)} async-done(((bf16[1088,1536]{1,0:T(8,128)(2,1)}), bf16[272,1536]{1,0:T(8,128)(2,1)}) %reduce-scatter.14.cloned.1.call-update) | async-done | bytes 835600 | tf_op jit(solution)/shard_map/reduce_scatter | solution.py:485
  255.3 33.0 %all-gather.27.cloned.1.call-done = bf16[1152,1536]{0,1:T(8,128)(2,1)} async-done(((bf16[1152,192]{0,1:T(8,128)(2,1)}), bf16[1152,1536]{0,1:T(8,128)(2,1)}) %all-gather.27.cloned.1.call-update) | async-done | bytes 3538960 | tf_op jit(solution)/shard_map/all_gather | solution.py:438
  288.3 5.8 copy.102.w_down
  294.1 63.2 %all-gather.21.cloned.1.call-done.cot = bf16[1088,1536]{1,0:T(8,128)(2,1)} async-done(((bf16[272,1536]{1,0:T(8,128)(2,1)}), bf16[1088,1536]{1,0:T(8,128)(2,1)}) %all-gather.21.cloned.1.call-update) | async-done | bytes 3342352 | tf_op jit(solution)/shard_map/all_gather | solution.py:468
  357.3 34.7 %all-gather.23.cloned.1.call-done.w_up = bf16[1536,1152]{1,0:T(8,128)(2,1)} async-done(((bf16[192,1152]{1,0:T(8,128)(2,1)}), bf16[1536,1152]{1,0:T(8,128)(2,1)}) %all-gather.23.cloned.1.call-update) | async-done | bytes 3538960 | tf_op jit(solution)/shard_map/all_gather | solution.py:436
  392.0 36.0 %all-gather.25.cloned.1.call-done.w_gate = bf16[1536,1152]{1,0:T(8,128)(2,1)} async-done(((bf16[192,1152]{1,0:T(8,128)(2,1)}), bf16[1536,1152]{1,0:T(8,128)(2,1)}) %all-gather.25.cloned.1.call-update) | async-done | bytes 3538960 | tf_op jit(solution)/shard_map/all_gather | solution.py:437
  428.0 68.9 %all-gather.19.cloned.1.call-done.tokens = bf16[1088,1536]{1,0:T(8,128)(2,1)} async-done(((bf16[272,1536]{1,0:T(8,128)(2,1)}), bf16[1088,1536]{1,0:T(8,128)(2,1)}) %all-gather.19.cloned.1.call-update) | async-done | bytes 3342352 | tf_op jit(solution)/shard_map/all_gather | solution.py:488
  496.9 38.2 %shard_map.256 = (bf16[1088,1536]{1,0:T(8,128)(2,1)}, bf16[1088,1536]{1,0:T(8,128)(2,1)}, bf16[1088,1152]{1,0:T(8,128)(2,1)}, bf16[1088,1152]{1,0:T(8,128)(2,1)}, bf16[1088,1152]{1,0:T(8,128)(2,1)}) custom-call(bf16[1088,1536]{1,0:T(8,128)(2,1)} %all-gather.19.cloned.1.call-done.tokens, bf16[1088,1536]{1,0:T(8,128)(2,1)} %all-gather.21.cloned.1.call-done.cot, ...), custom_call_target="tpu_custom_call" | custom-call | flops 23102226432 | bytes 31506432 | tf_op jit(solution)/shard_map/pallas_call | solution.py:387
  535.7 61.5 %reduce-scatter.18.cloned.1.call-done = bf16[272,1536]{1,0:T(8,128)(2,1)} async-done(((bf16[1088,1536]{1,0:T(8,128)(2,1)}), bf16[272,1536]{1,0:T(8,128)(2,1)}) %reduce-scatter.18.cloned.1.call-update) | async-done | bytes 835600 | tf_op jit(solution)/shard_map/reduce_scatter | solution.py:499
  598.9 63.9 %reduce-scatter.16.cloned.1.call-done = bf16[272,1536]{1,0:T(8,128)(2,1)} async-done(((bf16[1088,1536]{1,0:T(8,128)(2,1)}), bf16[272,1536]{1,0:T(8,128)(2,1)}) %reduce-scatter.16.cloned.1.call-update) | async-done | bytes 835600 | tf_op jit(solution)/shard_map/reduce_scatter | solution.py:509
  662.8 3.7 fusion.15
  666.6 8.9 convolution_convert_fusion.1
  675.7 9.0 convolution_convert_fusion.2
  684.8 8.9 convolution_convert_fusion
  695.6 37.9 %all-gather.29.cloned.1.call-done.back = bf16[1088,1536]{1,0:T(8,128)(2,1)} async-done(((bf16[272,1536]{1,0:T(8,128)(2,1)}), bf16[1088,1536]{1,0:T(8,128)(2,1)}) %all-gather.29.cloned.1.call-update) | async-done | bytes 3342352 | tf_op jit(solution)/shard_map/all_gather | solution.py:507
  733.6 33.0 %shard_map.257 = (bf16[1088,1024]{1,0:T(8,128)(2,1)}, bf16[1088,1536]{1,0:T(8,128)(2,1)}, f32[8,512]{1,0:T(8,128)}, f32[4,128,256]{2,1,0:T(8,128)}, f32[1,1536]{1,0:T(1,128)}) custom-call(bf16[1088,1536]{1,0:T(8,128)(2,1)} %all-gather.29.cloned.1.call-done.back, bf16[1088,1536]{1,0:T(8,128)(2,1)} %all-gather.11.cloned.1.call-done.tokens.norm, ...), custom_call_target="tpu_custom_call" | custom-call | flops 8770289664 | bytes 31204192 | tf_op jit(solution)/shard_map/pallas_call | solution.py:387
  772.3 5.8 convolution_convert_fusion.4
  778.1 6.9 convolution_convert_fusion.3
  791.0 44.9 %reduce-scatter.28.cloned.1.call-done = bf16[192,1152]{1,0:T(8,128)(2,1)} async-done(((bf16[1536,1152]{1,0:T(8,128)(2,1)}), bf16[192,1152]{1,0:T(8,128)(2,1)}) %reduce-scatter.28.cloned.1.call-update) | async-done | bytes 442384 | tf_op jit(solution)/shard_map/reduce_scatter | solution.py:513
  837.9 49.9 %reduce-scatter.32.cloned.1.call-done = bf16[1152,192]{0,1:T(8,128)(2,1)} async-done(((bf16[1152,1536]{0,1:T(8,128)(2,1)}), bf16[1152,192]{0,1:T(8,128)(2,1)}) %reduce-scatter.32.cloned.1.call-update) | async-done | bytes 442384 | tf_op jit(solution)/shard_map/reduce_scatter | solution.py:513
  889.8 99.8 %reduce-scatter.34.cloned.1.call-done = f32[48,2]{1,0:T(8,128)} async-done(((f32[1536,2]{1,0:T(8,128)}), f32[48,2]{1,0:T(8,128)}) %reduce-scatter.34.cloned.1.call-update) | async-done | bytes 400
  991.0 55.1 %all-reduce.4.cloned.1.call-done = f32[8,16896]{1,0:T(8,128)} async-done(((f32[8,16896]{1,0:T(8,128)}), f32[8,16896]{1,0:T(8,128)}) %all-reduce.4.cloned.1.call-update) | async-done | bytes 540688
  1054.9 33.2 %reduce-scatter.26.cloned.1.call-done = bf16[512,192]{0,1:T(8,128)(2,1)} async-done(((bf16[512,1536]{0,1:T(8,128)(2,1)}), bf16[512,192]{0,1:T(8,128)(2,1)}) %reduce-scatter.26.cloned.1.call-update) | async-done | bytes 196624 | tf_op jit(solution)/shard_map/reduce_scatter | solution.py:513
  1089.9 39.9 %reduce-scatter.22.cloned.1.call-done = bf16[192,512]{1,0:T(8,128)(2,1)} async-done(((bf16[1536,512]{1,0:T(8,128)(2,1)}), bf16[192,512]{1,0:T(8,128)(2,1)}) %reduce-scatter.22.cloned.1.call-update) | async-done | bytes 196624 | tf_op jit(solution)/shard_map/reduce_scatter | solution.py:513
  1131.5 40.1 %reduce-scatter.24.cloned.1.call-done = bf16[192,512]{1,0:T(8,128)(2,1)} async-done(((bf16[1536,512]{1,0:T(8,128)(2,1)}), bf16[192,512]{1,0:T(8,128)(2,1)}) %reduce-scatter.24.cloned.1.call-update) | async-done | bytes 196624 | tf_op jit(solution)/shard_map/reduce_scatter | solution.py:513
  1173.3 63.9 %reduce-scatter.20.cloned.1.call-done = bf16[272,1536]{1,0:T(8,128)(2,1)} async-done(((bf16[1088,1536]{1,0:T(8,128)(2,1)}), bf16[272,1536]{1,0:T(8,128)(2,1)}) %reduce-scatter.20.cloned.1.call-update) | async-done | bytes 835600 | tf_op jit(solution)/shard_map/reduce_scatter | solution.py:553
  (160 shorter events, 60.6 us)
Async XLA Ops:
  7.2 5.1 copy-start
  7.2 31.7 %all-gather.17.cloned.1.call-start = ((), (), s32[]{:S(2)}) async-start(), calls=%async_computation.14 | async-start | bytes 1769472 | tf_op jit(solution)/shard_map/all_gather | solution.py:435
  7.9 58.6 %all-gather.13.cloned.1.call-start = ((), (), s32[]{:S(2)}) async-start(), calls=%async_computation.12 | async-start | bytes 1769472 | tf_op jit(solution)/shard_map/all_gather | solution.py:433
  8.7 85.5 %all-gather.15.cloned.1.call-start = ((), (), s32[]{:S(2)}) async-start(), calls=%async_computation.13 | async-start | bytes 1769472 | tf_op jit(solution)/shard_map/all_gather | solution.py:434
  9.4 153.5 %all-gather.11.cloned.1.call-start = ((), (), s32[]{:S(2)}) async-start(), calls=%async_computation.11 | async-start | bytes 4177920 | tf_op jit(solution)/shard_map/all_gather | solution.py:466
  10.2 3.3 copy-start.12
  11.6 3.8 copy-start.7
  12.2 3.4 copy-start.13
  12.3 3.4 copy-start.16
  13.4 13.8 %copy-start.17 = (s32[1,4]{1,0:T(1,128)S(1)}, s32[1,4]{1,0:T(1,128)}, u32[]{:S(2)}) copy-start(s32[1,4]{1,0:T(1,128)} %param.20) | copy-start | bytes 52
  13.5 238.8 %reduce-scatter.14.cloned.1.call-start = ((), (), s32[]{:S(2)}) async-start(), calls=%async_computation.15 | async-start | bytes 4177920 | tf_op jit(solution)/shard_map/reduce_scatter | solution.py:485
  29.3 12.2 copy-start.4
  190.2 98.1 %all-gather.27.cloned.1.call-start = ((), (), s32[]{:S(2)}) async-start(), calls=%async_computation.20 | async-start | bytes 3981312 | tf_op jit(solution)/shard_map/all_gather | solution.py:438
  190.8 166.5 %all-gather.21.cloned.1.call-start = ((), (), s32[]{:S(2)}) async-start(), calls=%async_computation.17 | async-start | bytes 4177920 | tf_op jit(solution)/shard_map/all_gather | solution.py:468
  192.4 199.5 %all-gather.23.cloned.1.call-start = ((), (), s32[]{:S(2)}) async-start(), calls=%async_computation.18 | async-start | bytes 3981312 | tf_op jit(solution)/shard_map/all_gather | solution.py:436
  193.2 234.8 %all-gather.25.cloned.1.call-start = ((), (), s32[]{:S(2)}) async-start(), calls=%async_computation.19 | async-start | bytes 3981312 | tf_op jit(solution)/shard_map/all_gather | solution.py:437
  193.9 302.9 %all-gather.19.cloned.1.call-start = ((), (), s32[]{:S(2)}) async-start(), calls=%async_computation.16 | async-start | bytes 4177920 | tf_op jit(solution)/shard_map/all_gather | solution.py:488
  255.1 342.0 %reduce-scatter.18.cloned.1.call-start = ((), (), s32[]{:S(2)}) async-start(), calls=%async_computation.22 | async-start | bytes 4177920 | tf_op jit(solution)/shard_map/reduce_scatter | solution.py:499
  535.1 127.8 %reduce-scatter.16.cloned.1.call-start = ((), (), s32[]{:S(2)}) async-start(), calls=%async_computation.21 | async-start | bytes 4177920 | tf_op jit(solution)/shard_map/reduce_scatter | solution.py:509
  535.6 197.9 %all-gather.29.cloned.1.call-start = ((), (), s32[]{:S(2)}) async-start(), calls=%async_computation.23 | async-start | bytes 4177920 | tf_op jit(solution)/shard_map/all_gather | solution.py:507
  666.5 122.5 %reduce-scatter.30.cloned.1.call-start = ((), (), s32[]{:S(2)}) async-start(), calls=%async_computation.29 | async-start | bytes 3981312 | tf_op jit(solution)/shard_map/reduce_scatter | solution.py:513
  675.5 160.5 %reduce-scatter.28.cloned.1.call-start = ((), (), s32[]{:S(2)}) async-start(), calls=%async_computation.28 | async-start | bytes 3981312 | tf_op jit(solution)/shard_map/reduce_scatter | solution.py:513
  684.8 203.0 %reduce-scatter.32.cloned.1.call-start = ((), (), s32[]{:S(2)}) async-start(), calls=%async_computation.30 | async-start | bytes 3981312 | tf_op jit(solution)/shard_map/reduce_scatter | solution.py:513
  693.8 295.9 %reduce-scatter.34.cloned.1.call-start = ((), (), s32[]{:S(2)}) async-start(), calls=%async_computation.31 | async-start | bytes 811008
  771.1 275.1 %all-reduce.4.cloned.1.call-start = ((), (), s32[]{:S(2)}) async-start(), calls=%async_computation.32 | async-start | bytes 1081344
  772.0 316.2 %reduce-scatter.26.cloned.1.call-start = ((), (), s32[]{:S(2)}) async-start(), calls=%async_computation.27 | async-start | bytes 1769472 | tf_op jit(solution)/shard_map/reduce_scatter | solution.py:513
  778.0 351.8 %reduce-scatter.22.cloned.1.call-start = ((), (), s32[]{:S(2)}) async-start(), calls=%async_computation.25 | async-start | bytes 1769472 | tf_op jit(solution)/shard_map/reduce_scatter | solution.py:513
  786.9 384.7 %reduce-scatter.24.cloned.1.call-start = ((), (), s32[]{:S(2)}) async-start(), calls=%async_computation.26 | async-start | bytes 1769472 | tf_op jit(solution)/shard_map/reduce_scatter | solution.py:513
  787.7 449.6 %reduce-scatter.20.cloned.1.call-start = ((), (), s32[]{:S(2)}) async-start(), calls=%async_computation.24 | async-start | bytes 4177920 | tf_op jit(solution)/shard_map/reduce_scatter | solution.py:553
  837.9 399.3 %copy-start.6 = (f32[1536]{0:T(1024)S(1)}, f32[1536]{0:T(1024)}, u32[]{:S(2)}) copy-start(f32[1536]{0:T(1024)} %copy-done.5) | copy-start | bytes 18436
  1054.9 183.9 %copy-start.10 = (f32[272]{0:T(512)S(1)}, f32[272]{0:T(512)}, u32[]{:S(2)}) copy-start(f32[272]{0:T(512)} %copy-done.9) | copy-start | bytes 3268
  1054.9 183.9 %copy-start.11 = (f32[272]{0:T(512)S(1)}, f32[272]{0:T(512)}, u32[]{:S(2)}) copy-start(f32[272]{0:T(512)} %get-tuple-element.58) | copy-start | bytes 3268
  (9 other events, 15.0 us)
Sparse Core Ops, SparseCore 0:
  9.9 28.9 all-gather.16
  40.8 25.6 all-gather.12
  68.4 25.6 all-gather.14
  96.1 66.7 all-gather.10
  190.3 61.9 reduce-scatter.13
  254.2 34.1 all-gather.26
  290.5 66.7 all-gather.20
  359.4 32.5 all-gather.22
  394.0 33.9 all-gather.24
  430.1 66.7 all-gather.18
  535.2 61.9 reduce-scatter.17
  599.3 63.4 reduce-scatter.15
  666.6 66.8 all-gather.28
  737.3 46.7 reduce-scatter.29
  787.8 48.0 reduce-scatter.27
  839.7 48.0 reduce-scatter.31
  894.1 95.4 reduce-scatter.33
  993.0 53.1 all-reduce.3
  1049.4 38.6 reduce-scatter.25
  1091.3 38.4 reduce-scatter.21
  1133.1 38.4 reduce-scatter.23
  1173.9 63.2 reduce-scatter.19
where the time goes:
time: 1250 us
  waiting for transfers between devices  1020 us (82%)
  Pallas kernels  98.4 us (8%)
  matrix products  39.5 us (3%)
  local copies, waits for them, and re-layouts  31.7 us (3%)
  other arithmetic  30.8 us (2%)
  between operations  15.1 us (1%)
    reduce_scatter x6, waiting for transfers between devices, reduced(): lax.psum_scatter(grad.astype(bf16), 'dp', scatter_dimension=dimension, ti...  208 us
    unnamed x24, waiting for transfers between devices  161 us
    pallas_call x3, Pallas kernels, local_call(): pl.pallas_call(body, out_shape=outs, in_specs=[whole] * len(args), out_sp...  98.4 us
    all_gather x1, waiting for transfers between devices, shards(): norm_mid_group = lax.all_gather(norm_mid, 'mp', axis=0, tiled=True)  68.9 us
    all_gather x1, waiting for transfers between devices, shards(): norm_group = lax.all_gather(norm_in, 'mp', axis=0, tiled=True)  68.8 us
    reduce_scatter x1, waiting for transfers between devices, shards(): lax.psum_scatter(d_norm_back, 'mp', scatter_dimension=0, tiled=True)  63.9 us
    reduce_scatter x1, waiting for transfers between devices, shards(): lax.psum_scatter(ffn_part, 'mp', scatter_dimension=0, tiled=True)  63.9 us
    all_gather x1, waiting for transfers between devices, shards(): cot_group = lax.all_gather(cot.astype(bf16), 'mp', axis=0, tiled=True)  63.2 us
  transfers between devices with their start and end apart: 22, of which 21 were waited for; matrix products, arithmetic and copies ran while one was open for 8% of the time, Pallas kernels for 3%

commit v1 on v0

--- a/solution.py
+++ b/solution.py
@@ -380,6 +380,260 @@
     dgain_ref[...] = dgain_ref[...] / gain[...]
 
 
+MESH = pl.DeviceIdType.MESH
+TILE = 16
+PIECES = 4
+
+
+def cut_rows(rows, parts):
+    tiles = rows // TILE
+    ends = [tiles * (k + 1) // parts for k in range(parts)]
+    return [(TILE * a, TILE * (b - a)) for a, b in zip([0] + ends[:-1], ends)]
+
+
+class Line:
+    def __init__(self, n, local, part, arrived, whole, sums, alls):
+        self.n, self.local, self.part, self.arrived, self.whole = n, local, part, arrived, whole
+        self.sums, self.alls = sums, alls
+        self.me = lax.axis_index("mp")
+        self.pieces = cut_rows(local, PIECES)
+        self.has = (self.me > 0, self.me < n - 1)
+
+    def greet(self):
+        barrier = pltpu.get_barrier_semaphore()
+        for has, other in zip(self.has, (self.me - 1, self.me + 1)):
+
+            @pl.when(has)
+            def _():
+                pl.semaphore_signal(barrier, inc=1, device_id={"mp": other}, device_id_type=MESH)
+
+        both = self.has[0] & self.has[1]
+
+        @pl.when(both)
+        def _():
+            pl.semaphore_wait(barrier, 2)
+
+        @pl.when(jnp.logical_not(both))
+        def _():
+            pl.semaphore_wait(barrier, 1)
+
+    def rows_at(self, owner, k):
+        first, rows = self.pieces[k]
+        return pl.ds(pl.multiple_of(owner * self.local + first, TILE), rows)
+
+    def copy(self, source, target, sems, way, owner, k):
+        return pltpu.make_async_remote_copy(
+            src_ref=source,
+            dst_ref=target,
+            send_sem=sems[0].at[way, owner, k],
+            recv_sem=sems[1].at[way, owner, k],
+            device_id={"mp": self.me + 1 - 2 * way},
+            device_id_type=MESH,
+        )
+
+    def sum_copy(self, way, owner, k, first=False):
+        at = self.rows_at(owner, k)
+        landed = self.arrived[way].at[at]
+        return self.copy(self.part.at[at] if first else landed, landed, self.sums, way, owner, k)
+
+    def all_copy(self, way, owner, k):
+        block = self.whole.at[self.rows_at(owner, k)]
+        return self.copy(block, block, self.alls, way, owner, k)
+
+    def relay(self, k):
+        for away in range(self.n - 1):
+            for way in range(2):
+                owner = away if way else self.n - 1 - away
+                beyond = self.me > owner if way else self.me < owner
+
+                @pl.when(beyond & jnp.logical_not(self.has[way]))
+                def _():
+                    self.sum_copy(way, owner, k, True).start()
+
+                @pl.when(beyond & self.has[way])
+                def _():
+                    self.sum_copy(way, owner, k).wait_recv()
+                    at = self.rows_at(owner, k)
+                    landed = self.arrived[way]
+                    landed[at, :] = (landed[at, :].astype(f32) + self.part[at, :].astype(f32)).astype(bf16)
+                    self.sum_copy(way, owner, k).start()
+
+    def total(self, k, into):
+        at = self.rows_at(self.me, k)
+        rows = pl.ds(0, self.pieces[k][1])
+        into[rows, :] = self.part[at, :].astype(f32)
+        for way in range(2):
+
+            @pl.when(self.has[way])
+            def _():
+                self.sum_copy(way, self.me, k).wait_recv()
+                into[rows, :] += self.arrived[way][at, :].astype(f32)
+
+    def spread(self, k):
+        for way in range(2):
+
+            @pl.when(self.has[1 - way])
+            def _():
+                self.all_copy(way, self.me, k).start()
+
+    def forward(self, k):
+        for away in range(self.n - 1):
+            for way in range(2):
+                owner = self.n - 1 - away if way else away
+                below = self.me < owner if way else self.me > owner
+
+                @pl.when(below)
+                def _():
+                    self.all_copy(way, owner, k).wait_recv()
+
+                @pl.when(below & self.has[1 - way])
+                def _():
+                    self.all_copy(way, owner, k).start()
+
+    def finish(self):
+        for k in range(PIECES):
+            for owner in range(self.n):
+                for way in range(2):
+                    if self.part is not None:
+
+                        @pl.when(self.me > owner if way else self.me < owner)
+                        def _():
+                            self.sum_copy(way, owner, k).wait_send()
+
+                    if self.whole is not None:
+                        reached = self.me <= owner if way else self.me >= owner
+
+                        @pl.when(reached & self.has[1 - way])
+                        def _():
+                            self.all_copy(way, owner, k).wait_send()
+
+    def run(self, point):
+        for k in range(PIECES + 2):
+            if k < PIECES and self.part is not None:
+                self.relay(k)
+            if 1 <= k <= PIECES:
+                point(k - 1)
+                if self.whole is not None:
+                    self.spread(k - 1)
+            if k >= 2 and self.whole is not None:
+                self.forward(k - 2)
+        self.finish()
+
+    def tiles(self, k, body):
+        first, rows = self.pieces[k]
+
+        def one(i, carry):
+            body(
+                pl.ds(pl.multiple_of(i * TILE, TILE), TILE),
+                pl.ds(pl.multiple_of(first + i * TILE, TILE), TILE),
+                pl.ds(pl.multiple_of(self.me * self.local + first + i * TILE, TILE), TILE),
+            )
+            return carry
+
+        lax.fori_loop(0, rows // TILE, one, 0)
+
+
+def gather_norm(n, x, gain, whole, send, recv):
+    line = Line(n, x.shape[0], None, None, whole, None, (send, recv))
+    line.greet()
+
+    def point(k):
+        def one(_, own, at):
+            v = x[own, :].astype(f32)
+            whole[at, :] = (v * rms_scale(v) * gain[...]).astype(bf16)
+
+        line.tiles(k, one)
+
+    line.run(point)
+
+
+def sum_norm_gather(n, x, gain, part, resid, whole, left, right, total, ss, sr, send, recv):
+    line = Line(n, x.shape[0], part, (left, right), whole, (ss, sr), (send, recv))
+    line.greet()
+
+    def point(k):
+        line.total(k, total)
+
+        def one(here, own, at):
+            v = x[own, :].astype(f32) + total[here, :]
+            resid[own, :] = v
+            whole[at, :] = (v * rms_scale(v) * gain[...]).astype(bf16)
+
+        line.tiles(k, one)
+
+    line.run(point)
+
+
+def norm_back(value, gain, grad):
+    scale = rms_scale(value)
+    e = gain * grad
+    slope = scale * scale * scale * jnp.mean(value * e, axis=-1, keepdims=True)
+    return scale * e - value * slope, grad * value * scale
+
+
+def sum_back_gather(
+    n, resid, cot, gain, part, d_resid, gain_grad, whole, left, right, total, ss, sr, send, recv
+):
+    line = Line(n, resid.shape[0], part, (left, right), whole, (ss, sr), (send, recv))
+    line.greet()
+    gain_grad[...] = jnp.zeros_like(gain_grad)
+
+    def point(k):
+        line.total(k, total)
+
+        def one(here, own, at):
+            back, terms = norm_back(resid[own, :], gain[...], total[here, :])
+            gain_grad[...] += jnp.sum(terms, axis=0, keepdims=True)
+            value = cot[own, :].astype(f32) + back
+            d_resid[own, :] = value
+            whole[at, :] = value.astype(bf16)
+
+        line.tiles(k, one)
+
+    line.run(point)
+
+
+def sum_back(n, x, d_resid, gain, part, grad_x, left, right, total, ss, sr):
+    line = Line(n, x.shape[0], part, (left, right), None, (ss, sr), None)
+    line.greet()
+
+    def point(k):
+        line.total(k, total)
+
+        def one(here, own, at):
+            back, _ = norm_back(x[own, :].astype(f32), gain[...], total[here, :])
+            grad_x[own, :] = (d_resid[own, :] + back).astype(bf16)
+
+        line.tiles(k, one)
+
+    line.run(point)
+
+
+def line_call(body, n, identity, outs, sums, alls, args):
+    whole = pl.BlockSpec(memory_space=pltpu.VMEM)
+    local, model = args[0].shape
+    sem = pltpu.SemaphoreType.DMA((2, n, PIECES))
+    scratch = []
+    if sums:
+        scratch += [pltpu.VMEM((n * local, model), bf16)] * 2
+        scratch += [pltpu.VMEM((max(rows for _, rows in cut_rows(local, PIECES)), model), f32)]
+        scratch += [sem, sem]
+    if alls:
+        scratch += [sem, sem]
+    moved = sum(a.size * a.dtype.itemsize for a in args)
+    return pl.pallas_call(
+        functools.partial(body, n),
+        out_shape=outs,
+        in_specs=[whole] * len(args),
+        out_specs=[whole] * len(outs),
+        scratch_shapes=scratch,
+        compiler_params=pltpu.CompilerParams(
+            vmem_limit_bytes=VMEM_MB << 20, collective_id=identity, has_side_effects=True
+        ),
+        cost_estimate=pl.CostEstimate(flops=0, bytes_accessed=100 * moved, transcendentals=0),
+    )(*args)
+
+
 def local_call(body, outs, scratch, flops, args):
     whole = pl.BlockSpec(memory_space=pltpu.VMEM)
     moved = sum(a.size * a.dtype.itemsize for a in args)
@@ -461,11 +715,12 @@
     ocol, orow = order_int.reshape(count, 1), order_int.reshape(1, count)
 
     gain_f = gains.astype(f32)
-    x_local = inputs.astype(f32)
-    norm_in = (x_local * rms_scale(x_local) * gain_f[0]).astype(bf16)
-    norm_group = lax.all_gather(norm_in, "mp", axis=0, tiled=True)
-    cot = cotangent.astype(f32) * token_mask.astype(f32)[:, None]
-    cot_group = lax.all_gather(cot.astype(bf16), "mp", axis=0, tiled=True)
+    n_mp = lax.axis_size("mp")
+    tok = shape_of(bf16, count, model)
+    own = shape_of(f32, local_rows, model)
+    (norm_group,) = line_call(gather_norm, n_mp, 0, [tok], False, True, (inputs, gain_f[0:1]))
+    cot = cotangent * token_mask.astype(bf16)[:, None]
+    cot_group = lax.all_gather(cot, "mp", axis=0, tiled=True)
 
     wide = pltpu.VMEM((count, width), f32)
     saved = [shape_of(f32, count, width)] * 6
@@ -482,13 +737,11 @@
         2 * count * (count * model + 3 * model * width),
         (norm_group, ocol, orow, pos_col, full_in, full_gate, full_out, chan, blocks_twice),
     )
-    resid = x_local + lax.psum_scatter(back_part, "mp", scatter_dimension=0, tiled=True).astype(f32)
-    rms_mid = rms_scale(resid)
-    norm_mid = (resid * rms_mid * gain_f[1]).astype(bf16)
-    norm_mid_group = lax.all_gather(norm_mid, "mp", axis=0, tiled=True)
+    resid, norm_mid_group = line_call(
+        sum_norm_gather, n_mp, 1, [own, tok], True, True, (inputs, gain_f[1:2], back_part)
+    )
 
     hid = shape_of(bf16, count, hidden_width)
-    tok = shape_of(bf16, count, model)
     ffn_part, d_norm_part, hidden, d_up, d_gate_ff = local_call(
         ffn,
         [tok, tok, hid, hid, hid],
@@ -496,15 +749,15 @@
         12 * count * model * hidden_width,
         (norm_mid_group, cot_group, full_up, full_gate_ff, full_down),
     )
-    d_norm_mid = lax.psum_scatter(d_norm_part, "mp", scatter_dimension=0, tiled=True).astype(f32)
-    scaled = gain_f[1] * d_norm_mid
-    gain_mid = jnp.sum(d_norm_mid * resid * rms_mid, axis=0)
-    d_resid = (
-        cot
-        + rms_mid * scaled
-        - resid * (rms_mid * rms_mid * rms_mid) * jnp.mean(resid * scaled, axis=-1, keepdims=True)
-    )
-    back_group = lax.all_gather(d_resid.astype(bf16), "mp", axis=0, tiled=True)
+    d_resid, gain_mid, back_group = line_call(
+        sum_back_gather,
+        n_mp,
+        2,
+        [own, shape_of(f32, 1, model), tok],
+        True,
+        True,
+        (resid, cot, gain_f[1:2], d_norm_part),
+    )
     output = (
         resid + lax.psum_scatter(ffn_part, "mp", scatter_dimension=0, tiled=True).astype(f32)
     ).astype(bf16)
@@ -550,7 +803,15 @@
             *kept,
         ),
     )
-    d_norm_in = lax.psum_scatter(d_norm_back, "mp", scatter_dimension=0, tiled=True).astype(f32)
+    (grad_inputs,) = line_call(
+        sum_back,
+        n_mp,
+        3,
+        [shape_of(bf16, local_rows, model)],
+        True,
+        False,
+        (inputs, d_resid, gain_f[0:1], d_norm_back),
+    )
     grad_out = reduced(dot_first(mixed, back_group), 1)
     grad_cat = dot_first(norm_group, d_cat)
     grad_in = reduced(grad_cat[:, :width], 0)
@@ -566,15 +827,8 @@
     rows = small_own[:split_at].reshape(8, heads, piece)
     grad_blocks = small_own[split_at:].reshape(2, heads, piece, LANE)
 
-    rms_in = rms_scale(x_local)
-    e_in = gain_f[0] * d_norm_in
-    grad_inputs = (
-        d_resid
-        + rms_in * e_in
-        - x_local * (rms_in * rms_in * rms_in) * jnp.mean(x_local * e_in, axis=-1, keepdims=True)
-    ).astype(bf16)
     grad_gains = lax.psum_scatter(
-        jnp.stack([gain_in[0], gain_mid]), ("dp", "mp"), scatter_dimension=1, tiled=True
+        jnp.concatenate([gain_in, gain_mid], axis=0), ("dp", "mp"), scatter_dimension=1, tiled=True
     )
     return (
         output,

time: 1250 us -> 1070 us (0.86)
  waiting for transfers between devices: 1020 us -> 364 us
  Pallas kernels: 98.4 us -> 576 us
    pallas_call x0 -> x4, Pallas kernels: none -> 478 us  [line_call(): pl.pallas_call(functools.partial(body, n), out_shape=outs, in_specs=[whol...]
    all_gather x4 -> x1, waiting for transfers between devices: 239 us -> 0.01 us  [shards(): cot_group = lax.all_gather(cot, 'mp', axis=0, tiled=True)]
    reduce_scatter x3 -> x0, waiting for transfers between devices: 184 us -> none  [the longest x1 63.9 us: shards(): lax.psum_scatter(d_norm_back, 'mp', scatter_dimension=0, tiled=True)]
    unnamed x24 -> x18, waiting for transfers between devices: 161 us -> 36.4 us
    reduce_scatter x6, waiting for transfers between devices: 208 us -> 264 us  [reduced(): lax.psum_scatter(grad.astype(bf16), 'dp', scatter_dimension=dimension, ti...]
    all_gather x1, waiting for transfers between devices: 36 us -> 0.01 us  [shards(): full_gate_ff = lax.all_gather(w_gate_ff, 'dp', axis=0, tiled=True)]
    all_gather x1, waiting for transfers between devices: 34.7 us -> 0.01 us  [shards(): full_up = lax.all_gather(w_up, 'dp', axis=0, tiled=True)]
    all_gather x1, waiting for transfers between devices: 33 us -> 0.02 us  [shards(): full_down = lax.all_gather(w_down, 'dp', axis=1, tiled=True)]
  transfers between devices with their start and end apart: 22 -> 16, of which waited for: 21 -> 8; matrix products, arithmetic and copies ran while one was open for 8% -> 8% of each run, Pallas kernels for 3% -> 33%
where the time goes in v1:
time: 1070 us; the launch traced here: 1060 us
  Pallas kernels  576 us (54%)
  waiting for transfers between devices  364 us (34%)
  matrix products  38.5 us (4%)
  local copies, waits for them, and re-layouts  38.2 us (4%)
  other arithmetic  20.8 us (2%)
  between operations  14.8 us (1%)
  blocking collectives  11.2 us (1%)
    pallas_call x4, Pallas kernels, line_call(): pl.pallas_call(functools.partial(body, n), out_shape=outs, in_specs=[whol...  478 us
    reduce_scatter x6, waiting for transfers between devices, reduced(): lax.psum_scatter(grad.astype(bf16), 'dp', scatter_dimension=dimension, ti...  264 us
    pallas_call x3, Pallas kernels, local_call(): pl.pallas_call(body, out_shape=outs, in_specs=[whole] * len(args), out_sp...  98.1 us
    reduce_scatter x1, waiting for transfers between devices, shards(): lax.psum_scatter(ffn_part, 'mp', scatter_dimension=0, tiled=True)  63.6 us
    dot_general x5, matrix products, dot_first(): lax.dot_general(left, right, (((0,), (0,)), ((), ())), preferred_element_...  38.5 us
    unnamed x18, waiting for transfers between devices  36.4 us
  transfers between devices with their start and end apart: 16, of which 8 were waited for; matrix products, arithmetic and copies ran while one was open for 8% of the time, Pallas kernels for 33%

profile of v1, /device:TPU:0, one launch (start us, length us, event | category | flops | bytes accessed | tf_op | source)
XLA Modules:
  0.0 1064.4 jit_solution(17083106466455732146)
XLA Ops:
  10.8 2.2 broadcast_multiply_fusion.cot
  18.3 11.2 %all_gather.27 = bf16[1056,128]{0,1:T(8,128)(2,1)S(1)} all-gather(bf16[1056,16]{0,1:T(8,128)(2,1)S(1)} %concatenate.23), channel_id=1, replica_groups=mesh['dp'=8,'mp'=4] {'dp'}, dimensions={1}, use_global_device_ids=true | all-gather | bytes 304128 | tf_op jit(solution)/shard_map/all_gather | solution.py:686
  31.2 75.7 %shard_map.255.tokens.norm = bf16[1088,1536]{1,0:T(8,128)(2,1)} custom-call(bf16[272,1536]{1,0:T(8,128)(2,1)} %x.7, f32[1,1536]{1,0:T(1,128)} %get-tuple-element.61.gain), custom_call_target="tpu_custom_call" | custom-call | bytes 84172800 | tf_op jit(solution)/shard_map/pallas_call | solution.py:624
  108.5 2.6 copy.101.w_out
  111.2 27.3 %shard_map.256 = (f32[1088,512]{1,0:T(8,128)}, f32[1088,512]{1,0:T(8,128)}, f32[1088,512]{1,0:T(8,128)}, f32[1088,512]{1,0:T(8,128)}, f32[1088,512]{1,0:T(8,128)...) custom-call(bf16[1088,1536]{1,0:T(8,128)(2,1)} %shard_map.255.tokens.norm, ...), custom_call_target="tpu_custom_call" | custom-call | flops 8770289664 | bytes 26456928 | tf_op jit(solution)/shard_map/pallas_call | solution.py:641
  138.5 187.0 %shard_map.257 = (f32[272,1536]{1,0:T(8,128)}, bf16[1088,1536]{1,0:T(8,128)(2,1)}) custom-call(bf16[272,1536]{1,0:T(8,128)(2,1)} %x.7, f32[1,1536]{1,0:T(1,128)} %get-tuple-element.62.gain, bf16[1088,1536]{1,0:T(8,128)(2,1)} %get-tuple-element.36.part), custom_call_target="tpu_custom_call" | custom-call | bytes 418406400 | tf_op jit(solution)/shard_map/pallas_call | solution.py:624
  325.5 5.8 copy.102.w_down
  331.3 38.1 %shard_map.258 = (bf16[1088,1536]{1,0:T(8,128)(2,1)}, bf16[1088,1536]{1,0:T(8,128)(2,1)}, bf16[1088,1152]{1,0:T(8,128)(2,1)}, bf16[1088,1152]{1,0:T(8,128)(2,1)}, bf16[1088,1152]{1,0:T(8,128)(2,1)}) custom-call(bf16[1088,1536]{1,0:T(8,128)(2,1)} %get-tuple-element.38.tokens, bf16[1088,1536]{1,0:T(8,128)(2,1)} %all-gather.14.cloned.1.call-done.cot, ...), custom_call_target="tpu_custom_call" | custom-call | flops 23102226432 | bytes 31506432 | tf_op jit(solution)/shard_map/pallas_call | solution.py:641
  369.3 149.3 %shard_map.259 = (f32[272,1536]{1,0:T(8,128)}, f32[1,1536]{1,0:T(1,128)}, bf16[1088,1536]{1,0:T(8,128)(2,1)}) custom-call(f32[272,1536]{1,0:T(8,128)} %get-tuple-element.37.resid, bf16[272,1536]{1,0:T(8,128)(2,1)} %broadcast_multiply_fusion.cot, f32[1,1536]{1,0:T(1,128)} %get-tuple-element.62.gain, bf16[1088,1536]{1,0:T(8,128)(2,1)} %get-tuple-element.40.part), custom_call_target="tpu_custom_call" | custom-call | bytes 585523200 | tf_op jit(solution)/shard_map/pallas_call | solution.py:624
  518.7 32.7 %shard_map.260 = (bf16[1088,1024]{1,0:T(8,128)(2,1)}, bf16[1088,1536]{1,0:T(8,128)(2,1)}, f32[8,512]{1,0:T(8,128)}, f32[4,128,256]{2,1,0:T(8,128)}, f32[1,1536]{1,0:T(1,128)}) custom-call(bf16[1088,1536]{1,0:T(8,128)(2,1)} %get-tuple-element.42.back, bf16[1088,1536]{1,0:T(8,128)(2,1)} %shard_map.255.tokens.norm, s32[1088,1]{1,0:T(8,128)} %reshape_reshape.8.ocol, ...), custom_call_target="tpu_custom_call" | custom-call | flops 8770289664 | bytes 31204192 | tf_op jit(solution)/shard_map/pallas_call | solution.py:641
  553.5 2.1 reshape.177
  555.6 2.1 copy.107
  561.4 7.3 convolution_convert_fusion.3
  568.8 3.8 fusion
  573.4 5.9 convolution_convert_fusion.4
  579.7 8.4 convolution_convert_fusion.2
  588.1 8.5 convolution_convert_fusion.1
  598.6 8.4 convolution_convert_fusion
  608.2 65.8 %shard_map.261 = bf16[272,1536]{1,0:T(8,128)(2,1)} custom-call(bf16[272,1536]{1,0:T(8,128)(2,1)} %x.7, f32[272,1536]{1,0:T(8,128)} %get-tuple-element.41.d_resid, f32[1,1536]{1,0:T(1,128)} %get-tuple-element.61.gain, bf16[1088,1536]{1,0:T(8,128)(2,1)} %get-tuple-element.49.part), custom_call_target="tpu_custom_call" | custom-call | bytes 585523200 | tf_op jit(solution)/shard_map/pallas_call | solution.py:624
  675.5 31.2 %all-reduce.4.cloned.1.call-done = f32[8,16896]{1,0:T(8,128)} async-done(((f32[8,16896]{1,0:T(8,128)}), f32[8,16896]{1,0:T(8,128)}) %all-reduce.4.cloned.1.call-update) | async-done | bytes 540688
  713.0 2.5 dynamic-slice.5
  715.6 33.4 %reduce-scatter.13.cloned.1.call-done = bf16[192,512]{1,0:T(8,128)(2,1)} async-done(((bf16[1536,512]{1,0:T(8,128)(2,1)}), bf16[192,512]{1,0:T(8,128)(2,1)}) %reduce-scatter.13.cloned.1.call-update) | async-done | bytes 196624 | tf_op jit(solution)/shard_map/reduce_scatter | solution.py:766
  750.7 40.4 %reduce-scatter.15.cloned.1.call-done = bf16[192,512]{1,0:T(8,128)(2,1)} async-done(((bf16[1536,512]{1,0:T(8,128)(2,1)}), bf16[192,512]{1,0:T(8,128)(2,1)}) %reduce-scatter.15.cloned.1.call-update) | async-done | bytes 196624 | tf_op jit(solution)/shard_map/reduce_scatter | solution.py:766
  792.8 40.3 %reduce-scatter.17.cloned.1.call-done = bf16[512,192]{0,1:T(8,128)(2,1)} async-done(((bf16[512,1536]{0,1:T(8,128)(2,1)}), bf16[512,192]{0,1:T(8,128)(2,1)}) %reduce-scatter.17.cloned.1.call-update) | async-done | bytes 196624 | tf_op jit(solution)/shard_map/reduce_scatter | solution.py:766
  834.7 50.3 %reduce-scatter.19.cloned.1.call-done = bf16[192,1152]{1,0:T(8,128)(2,1)} async-done(((bf16[1536,1152]{1,0:T(8,128)(2,1)}), bf16[192,1152]{1,0:T(8,128)(2,1)}) %reduce-scatter.19.cloned.1.call-update) | async-done | bytes 442384 | tf_op jit(solution)/shard_map/reduce_scatter | solution.py:766
  885.0 2.0 convert_element_type.57
  887.0 49.9 %reduce-scatter.21.cloned.1.call-done = bf16[192,1152]{1,0:T(8,128)(2,1)} async-done(((bf16[1536,1152]{1,0:T(8,128)(2,1)}), bf16[192,1152]{1,0:T(8,128)(2,1)}) %reduce-scatter.21.cloned.1.call-update) | async-done | bytes 442384 | tf_op jit(solution)/shard_map/reduce_scatter | solution.py:766
  936.9 2.0 convert_element_type.59
  938.8 49.9 %reduce-scatter.23.cloned.1.call-done = bf16[1152,192]{0,1:T(8,128)(2,1)} async-done(((bf16[1152,1536]{0,1:T(8,128)(2,1)}), bf16[1152,192]{0,1:T(8,128)(2,1)}) %reduce-scatter.23.cloned.1.call-update) | async-done | bytes 442384 | tf_op jit(solution)/shard_map/reduce_scatter | solution.py:766
  988.7 2.0 convert_element_type.61
  990.7 63.6 %reduce-scatter.11.cloned.1.call-done = bf16[272,1536]{1,0:T(8,128)(2,1)} async-done(((bf16[1088,1536]{1,0:T(8,128)(2,1)}), bf16[272,1536]{1,0:T(8,128)(2,1)}) %reduce-scatter.11.cloned.1.call-update) | async-done | bytes 835600 | tf_op jit(solution)/shard_map/reduce_scatter | solution.py:762
  1054.3 2.2 add_convert_fusion
  (127 shorter events, 35.9 us)
Async XLA Ops:
  7.2 7.2 copy-start.8
  7.2 9.1 copy-start.14
  7.2 10.7 %copy-start.9 = (bf16[4,4,16]{2,1,0:T(4,128)(2,1)S(1)}, bf16[4,4,16]{2,1,0:T(4,128)(2,1)}, u32[]{:S(2)}) copy-start(bf16[4,4,16]{2,1,0:T(4,128)(2,1)} %param.25) | copy-start | bytes 1540
  7.2 10.7 %copy-start.10 = (bf16[3,4,16]{2,1,0:T(4,128)(2,1)S(1)}, bf16[3,4,16]{2,1,0:T(4,128)(2,1)}, u32[]{:S(2)}) copy-start(bf16[3,4,16]{2,1,0:T(4,128)(2,1)} %param.26) | copy-start | bytes 1156
  7.2 10.8 %copy-start.11 = (bf16[4,16]{1,0:T(4,128)(2,1)S(1)}, bf16[4,16]{1,0:T(4,128)(2,1)}, u32[]{:S(2)}) copy-start(bf16[4,16]{1,0:T(4,128)(2,1)} %param.27) | copy-start | bytes 388
  7.2 10.9 %copy-start.4 = (bf16[2,4,16,128]{3,2,1,0:T(8,128)(2,1)S(1)}, bf16[2,4,16,128]{3,2,1,0:T(8,128)(2,1)}, u32[]{:S(2)}) copy-start(bf16[2,4,16,128]{3,2,1,0:T(8,128)(2,1)} %param.28) | copy-start | bytes 98308
  7.2 101.3 %all-gather.12.cloned.1.call-start = ((), (), s32[]{:S(2)}) async-start(), calls=%async_computation.10 | async-start | bytes 1769472 | tf_op jit(solution)/shard_map/all_gather | solution.py:689
  8.0 103.2 %all-gather.8.cloned.1.call-start = ((), (), s32[]{:S(2)}) async-start(), calls=%async_computation.8 | async-start | bytes 1769472 | tf_op jit(solution)/shard_map/all_gather | solution.py:687
  8.7 102.4 %all-gather.10.cloned.1.call-start = ((), (), s32[]{:S(2)}) async-start(), calls=%async_computation.9 | async-start | bytes 1769472 | tf_op jit(solution)/shard_map/all_gather | solution.py:688
  9.5 316.0 %all-gather.20.cloned.1.call-start = ((), (), s32[]{:S(2)}) async-start(), calls=%async_computation.14 | async-start | bytes 3981312 | tf_op jit(solution)/shard_map/all_gather | solution.py:692
  10.0 321.2 %all-gather.14.cloned.1.call-start = ((), (), s32[]{:S(2)}) async-start(), calls=%async_computation.11 | async-start | bytes 4177920 | tf_op jit(solution)/shard_map/all_gather | solution.py:723
  12.9 17.6 %copy-start.5 = (bf16[2,1536]{1,0:T(2,128)(2,1)S(1)}, bf16[2,1536]{1,0:T(2,128)(2,1)}, u32[]{:S(2)}) copy-start(bf16[2,1536]{1,0:T(2,128)(2,1)} %param.21) | copy-start | bytes 18436
  13.0 318.3 %all-gather.16.cloned.1.call-start = ((), (), s32[]{:S(2)}) async-start(), calls=%async_computation.12 | async-start | bytes 3981312 | tf_op jit(solution)/shard_map/all_gather | solution.py:690
  13.5 317.7 %all-gather.18.cloned.1.call-start = ((), (), s32[]{:S(2)}) async-start(), calls=%async_computation.13 | async-start | bytes 3981312 | tf_op jit(solution)/shard_map/all_gather | solution.py:691
  14.3 659.7 %reduce-scatter.25.cloned.1.call-start = ((), (), s32[]{:S(2)}) async-start(), calls=%async_computation.22 | async-start | bytes 811008
  30.5 80.7 %copy-start.3 = (bf16[4,128,256]{2,1,0:T(8,128)(2,1)}, bf16[4,128,256]{2,1,0:T(8,128)(2,1)S(1)}, u32[]{:S(2)}) copy-start(bf16[4,128,256]{2,1,0:T(8,128)(2,1)S(1)} %reshape.174.blocks) | copy-start | bytes 786436
  518.7 32.7 %copy-start.7 = (f32[1,1536]{1,0:T(1,128)S(1)}, f32[1,1536]{1,0:T(1,128)}, u32[]{:S(2)}) copy-start(f32[1,1536]{1,0:T(1,128)} %get-tuple-element.51) | copy-start | bytes 18436
  551.4 6.4 copy-start.6
  551.4 10.1 copy-start.1
  553.5 153.3 %all-reduce.4.cloned.1.call-start = ((), (), s32[]{:S(2)}) async-start(), calls=%async_computation.23 | async-start | bytes 1081344
  568.8 180.1 %reduce-scatter.13.cloned.1.call-start = ((), (), s32[]{:S(2)}) async-start(), calls=%async_computation.16 | async-start | bytes 1769472 | tf_op jit(solution)/shard_map/reduce_scatter | solution.py:766
  572.6 218.4 %reduce-scatter.15.cloned.1.call-start = ((), (), s32[]{:S(2)}) async-start(), calls=%async_computation.17 | async-start | bytes 1769472 | tf_op jit(solution)/shard_map/reduce_scatter | solution.py:766
  573.4 259.7 %reduce-scatter.17.cloned.1.call-start = ((), (), s32[]{:S(2)}) async-start(), calls=%async_computation.18 | async-start | bytes 1769472 | tf_op jit(solution)/shard_map/reduce_scatter | solution.py:766
  573.4 6.2 copy-start.13
  579.3 305.7 %reduce-scatter.19.cloned.1.call-start = ((), (), s32[]{:S(2)}) async-start(), calls=%async_computation.19 | async-start | bytes 3981312 | tf_op jit(solution)/shard_map/reduce_scatter | solution.py:766
  588.1 348.8 %reduce-scatter.21.cloned.1.call-start = ((), (), s32[]{:S(2)}) async-start(), calls=%async_computation.20 | async-start | bytes 3981312 | tf_op jit(solution)/shard_map/reduce_scatter | solution.py:766
  596.6 1.9 copy-start.12
  596.6 392.1 %reduce-scatter.23.cloned.1.call-start = ((), (), s32[]{:S(2)}) async-start(), calls=%async_computation.21 | async-start | bytes 3981312 | tf_op jit(solution)/shard_map/reduce_scatter | solution.py:766
  607.0 0.7 copy-start.15
  607.0 447.3 %reduce-scatter.11.cloned.1.call-start = ((), (), s32[]{:S(2)}) async-start(), calls=%async_computation.15 | async-start | bytes 4177920 | tf_op jit(solution)/shard_map/reduce_scatter | solution.py:762
  674.0 380.3 %copy-start = (f32[272,1536]{1,0:T(8,128)S(1)}, f32[272,1536]{1,0:T(8,128)}, u32[]{:S(2)}) copy-start(f32[272,1536]{1,0:T(8,128)} %get-tuple-element.37.resid) | copy-start | bytes 5013508
  887.0 169.6 %copy-start.2 = (bf16[272,1536]{1,0:T(8,128)(2,1)S(1)}, bf16[272,1536]{1,0:T(8,128)(2,1)}, u32[]{:S(2)}) copy-start(bf16[272,1536]{1,0:T(8,128)(2,1)} %shard_map.261) | copy-start | bytes 2506756
Sparse Core Ops, SparseCore 0:
  10.0 28.8 all-gather.11
  40.7 25.6 all-gather.7
  68.3 25.6 all-gather.9
  95.8 33.9 all-gather.19
  131.8 100.8 all-gather.13
  234.4 33.9 all-gather.15
  270.3 33.9 all-gather.17
  553.6 96.1 reduce-scatter.24
  653.5 53.2 all-reduce.3
  710.2 38.6 reduce-scatter.12
  752.6 38.4 reduce-scatter.14
  794.6 38.4 reduce-scatter.16
  836.9 48.0 reduce-scatter.18
  888.8 48.0 reduce-scatter.20
  940.6 48.0 reduce-scatter.22
  991.0 63.2 reduce-scatter.10

commit v2 on v1

--- a/solution.py
+++ b/solution.py
@@ -12,7 +12,7 @@
 SUB = 8
 TAIL = 24
 ROWS = 272
-VMEM_MB = 60
+VMEM_MB = 62
 f32 = jnp.float32
 bf16 = jnp.bfloat16
 GELU_C = 0.7978845608028654
@@ -129,7 +129,10 @@
                 earlier = before[pl.ds(TAIL - SUB * k, ROWS), lanes]
                 conv = conv + par[k : k + 1] * jnp.where(place >= k, earlier, 0.0)
             high, rest = split(conv)
-            pre = dot(jnp.concatenate([high, rest], axis=1), blocks[h])
+            pair = jnp.concatenate([blocks[h], blocks[heads + h]], axis=1)
+            pre = dot(
+                jnp.concatenate([high, rest], axis=1), jnp.concatenate([pair, pair], axis=0)
+            )
             gate_in = sigmoid(pre[:, :LANE] + par[5:6])
             gate_rec = sigmoid(pre[:, LANE:] + par[6:7])
             kept = jnp.exp(-8.0 * gate_rec * par[7:8])
@@ -175,7 +178,7 @@
         at = rows_of(b, ROWS)
         mixed = dot(put_rows(orow[...], b * ROWS, ROWS), low[...]).astype(bf16)
         mixed_ref[at, :] = mixed
-        out_ref[at, :] = dot(mixed, w_out[...]).astype(bf16)
+        out_ref[at, :] = dot_last(mixed, w_out[...]).astype(bf16)
         return carry
 
     lax.fori_loop(0, count // ROWS, leave, 0)
@@ -190,13 +193,13 @@
         value, slope = gelu_both(dot(tokens[at, :], w_gate[...]))
         hidden = (value * up).astype(bf16)
         hidden_ref[at, :] = hidden
-        d_hidden = dot_last(cot[at, :], w_down[...])
+        d_hidden = dot(cot[at, :], w_down[...])
         d_up = (d_hidden * value).astype(bf16)
         d_gate = (d_hidden * up * slope).astype(bf16)
         dup_ref[at, :] = d_up
         dgate_ref[at, :] = d_gate
         dnorm_ref[at, :] = (dot_last(d_up, w_up[...]) + dot_last(d_gate, w_gate[...])).astype(bf16)
-        part_ref[at, :] = dot(hidden, w_down[...]).astype(bf16)
+        part_ref[at, :] = dot_last(hidden, w_down[...]).astype(bf16)
         return carry
 
     lax.fori_loop(0, tokens.shape[0] // ROWS, block, 0)
@@ -241,7 +244,7 @@
 
     def enter(b, carry):
         at = rows_of(b, ROWS)
-        dmix_arr[at, :] = dot_last(back[at, :], w_out[...]).astype(bf16)
+        dmix_arr[at, :] = dot(back[at, :], w_out[...]).astype(bf16)
         return carry
 
     lax.fori_loop(0, blocks_of, enter, 0)
@@ -316,7 +319,8 @@
             d_rec = d_log * (-8.0 * par[7:8]) * gate_rec * (1.0 - gate_rec)
             both = jnp.concatenate([d_in, d_rec], axis=1)
             high, rest = split(both)
-            d_conv = scaled * root + dot_last(high, blocks[h]) + dot_last(rest, blocks[h])
+            pair = jnp.concatenate([blocks[h], blocks[heads + h]], axis=1)
+            d_conv = scaled * root + dot_last(high, pair) + dot_last(rest, pair)
             dblocks_ref[h] += dot_first(conv.astype(bf16), high)
             after[at, lanes] = d_conv
             small_ref[4:5, lanes] += jnp.sum(d_conv, axis=0, keepdims=True)
@@ -399,8 +403,15 @@
         self.pieces = cut_rows(local, PIECES)
         self.has = (self.me > 0, self.me < n - 1)
 
-    def greet(self):
+    def greet(self, plane=None):
         barrier = pltpu.get_barrier_semaphore()
+        more = 0
+        if plane is not None:
+            for bit in plane.bits:
+                more += 1
+                pl.semaphore_signal(
+                    barrier, inc=1, device_id={"dp": plane.other(bit)}, device_id_type=MESH
+                )
         for has, other in zip(self.has, (self.me - 1, self.me + 1)):
 
             @pl.when(has)
@@ -411,11 +422,11 @@
 
         @pl.when(both)
         def _():
-            pl.semaphore_wait(barrier, 2)
+            pl.semaphore_wait(barrier, more + 2)
 
         @pl.when(jnp.logical_not(both))
         def _():
-            pl.semaphore_wait(barrier, 1)
+            pl.semaphore_wait(barrier, more + 1)
 
     def rows_at(self, owner, k):
         first, rows = self.pieces[k]
@@ -440,23 +451,27 @@
         block = self.whole.at[self.rows_at(owner, k)]
         return self.copy(block, block, self.alls, way, owner, k)
 
-    def relay(self, k):
+    def first(self, k):
         for away in range(self.n - 1):
             for way in range(2):
                 owner = away if way else self.n - 1 - away
-                beyond = self.me > owner if way else self.me < owner
-
-                @pl.when(beyond & jnp.logical_not(self.has[way]))
+
+                @pl.when(jnp.logical_not(self.has[way]))
                 def _():
                     self.sum_copy(way, owner, k, True).start()
 
-                @pl.when(beyond & self.has[way])
-                def _():
-                    self.sum_copy(way, owner, k).wait_recv()
-                    at = self.rows_at(owner, k)
-                    landed = self.arrived[way]
-                    landed[at, :] = (landed[at, :].astype(f32) + self.part[at, :].astype(f32)).astype(bf16)
-                    self.sum_copy(way, owner, k).start()
+    def relay(self, k, stage):
+        for way in range(2):
+            late = stage - (self.n - 1 - self.me if way else self.me)
+            owner = late if way else self.n - 1 - late
+
+            @pl.when(self.has[way] & (late >= 0))
+            def _():
+                self.sum_copy(way, owner, k).wait_recv()
+                at = self.rows_at(owner, k)
+                landed = self.arrived[way]
+                landed[at, :] = (landed[at, :].astype(f32) + self.part[at, :].astype(f32)).astype(bf16)
+                self.sum_copy(way, owner, k).start()
 
     def total(self, k, into):
         at = self.rows_at(self.me, k)
@@ -476,19 +491,18 @@
             def _():
                 self.all_copy(way, self.me, k).start()
 
-    def forward(self, k):
-        for away in range(self.n - 1):
-            for way in range(2):
-                owner = self.n - 1 - away if way else away
-                below = self.me < owner if way else self.me > owner
-
-                @pl.when(below)
-                def _():
-                    self.all_copy(way, owner, k).wait_recv()
-
-                @pl.when(below & self.has[1 - way])
-                def _():
-                    self.all_copy(way, owner, k).start()
+    def forward(self, k, stage):
+        for way in range(2):
+            owner = self.me + stage if way else self.me - stage
+            there = owner < self.n if way else owner >= 0
+
+            @pl.when(there)
+            def _():
+                self.all_copy(way, owner, k).wait_recv()
+
+            @pl.when(there & self.has[1 - way])
+            def _():
+                self.all_copy(way, owner, k).start()
 
     def finish(self):
         for k in range(PIECES):
@@ -507,16 +521,31 @@
                         def _():
                             self.all_copy(way, owner, k).wait_send()
 
-    def run(self, point):
-        for k in range(PIECES + 2):
-            if k < PIECES and self.part is not None:
-                self.relay(k)
-            if 1 <= k <= PIECES:
-                point(k - 1)
-                if self.whole is not None:
-                    self.spread(k - 1)
-            if k >= 2 and self.whole is not None:
-                self.forward(k - 2)
+    def run(self, point, tasks=()):
+        tasks = iter(tasks)
+        sums, alls = self.part is not None, self.whole is not None
+        if sums:
+            self.first(0)
+        else:
+            for k in range(PIECES):
+                point(k)
+                self.spread(k)
+        for step in range(PIECES + (1 if alls and sums else 0)):
+            gathered = step - 1 if sums else step
+            if sums and alls and step > 0:
+                self.spread(gathered)
+            if sums and step + 1 < PIECES:
+                self.first(step + 1)
+            for stage in range(1, self.n):
+                next(tasks, idle)()
+                if alls and gathered >= 0:
+                    self.forward(gathered, stage)
+                if sums and step < PIECES and stage < self.n - 1:
+                    self.relay(step, stage)
+            if sums and step < PIECES:
+                point(step)
+        for task in tasks:
+            task()
         self.finish()
 
     def tiles(self, k, body):
@@ -533,6 +562,174 @@
         lax.fori_loop(0, rows // TILE, one, 0)
 
 
+def idle():
+    pass
+
+
+class Plane:
+    bits = (1, 2, 4)
+    orders = ((4, 2, 1), (2, 4, 1))
+
+    def __init__(self):
+        self.me = lax.axis_index("dp")
+
+    def bit(self, bit):
+        return lax.rem(self.me // bit, 2)
+
+    def other(self, *bits):
+        return self.me + sum(bit * (1 - 2 * self.bit(bit)) for bit in bits)
+
+    def gather_copies(self, item, view, halves, stage, sems):
+        copies = []
+        for half in halves:
+            order = self.orders[half]
+            for combo in range(1 << stage):
+                flipped = [bit for i, bit in enumerate(order[:stage]) if combo >> i & 1]
+                block = view(self.other(*flipped), half)
+                slot = (1 << stage) - 1 + combo
+                copies.append(
+                    pltpu.make_async_remote_copy(
+                        src_ref=block,
+                        dst_ref=block,
+                        send_sem=sems[0].at[item, half, slot],
+                        recv_sem=sems[1].at[item, half, slot],
+                        device_id={"dp": self.other(order[stage])},
+                        device_id_type=MESH,
+                    )
+                )
+        return copies
+
+
+class Reduce(Plane):
+    def __init__(self, index, left, right, lanes, mine, theirs, got, second, third, out, sems):
+        super().__init__()
+        self.index, self.left, self.right, self.lanes = index, left, right, lanes
+        self.mine, self.theirs, self.got = mine.at[index], theirs.at[index], got.at[index]
+        self.second, self.third, self.out = second.at[index], third.at[index], out
+        self.sems = sems
+        self.rows = out.shape[0]
+        self.half = self.rows // 2
+
+    def copy(self, source, target, slot, bit):
+        return pltpu.make_async_remote_copy(
+            src_ref=source,
+            dst_ref=target,
+            send_sem=self.sems[0].at[self.index, slot],
+            recv_sem=self.sems[1].at[self.index, slot],
+            device_id={"dp": self.other(bit)},
+            device_id_type=MESH,
+        )
+
+    def core_copy(self, t):
+        return self.copy(self.theirs.at[t], self.got.at[t], t, 1)
+
+    def second_copy(self, half, j):
+        x, y = self.bit(2), self.bit(4)
+        block = (1 - y) * 2 + j if half else j * 2 + 1 - x
+        rows = self.mine.at[block, pl.ds(half * self.half, self.half)]
+        return self.copy(rows, self.second.at[half, j], 4 + 2 * half + j, 4 if half else 2)
+
+    def third_block(self, half):
+        x, y = self.bit(2), self.bit(4)
+        return y * 2 + 1 - x if half else (1 - y) * 2 + x
+
+    def third_copy(self, half):
+        rows = self.mine.at[self.third_block(half), pl.ds(half * self.half, self.half)]
+        return self.copy(rows, self.third.at[half], 8 + half, 2 if half else 4)
+
+    def product(self, t):
+        def task():
+            core = self.bit(1)
+            pair = pl.ds(t * 2 * self.rows, 2 * self.rows)
+            both = dot_first(self.left[:, pair], self.right[:, self.lanes])
+            low, high = both[: self.rows], both[self.rows :]
+            self.mine[t] = jnp.where(core == 0, low, high).astype(bf16)
+            self.theirs[t] = jnp.where(core == 0, high, low).astype(bf16)
+            self.core_copy(t).start()
+
+        return task
+
+    def add_core(self):
+        for t in range(4):
+            self.core_copy(t).wait_recv()
+            self.mine[t] = (self.mine[t].astype(f32) + self.got[t].astype(f32)).astype(bf16)
+        for half in range(2):
+            for j in range(2):
+                self.second_copy(half, j).start()
+
+    def add_second(self):
+        for half in range(2):
+            for j in range(2):
+                self.second_copy(half, j).wait_recv()
+        for half in range(2):
+            block, at = self.third_block(half), pl.ds(half * self.half, self.half)
+            far = 1 - self.bit(2 if half else 4)
+            self.mine[block, at] = (
+                self.mine[block, at].astype(f32) + self.second[half, far].astype(f32)
+            ).astype(bf16)
+            self.third_copy(half).start()
+
+    def add_third(self):
+        own = self.bit(4) * 2 + self.bit(2)
+        for half in range(2):
+            self.third_copy(half).wait_recv()
+            at = pl.ds(half * self.half, self.half)
+            near = self.bit(2 if half else 4)
+            self.out[at, :] = (
+                self.mine[own, at].astype(f32)
+                + self.second[half, near].astype(f32)
+                + self.third[half].astype(f32)
+            )
+
+    def finish(self):
+        for t in range(4):
+            self.core_copy(t).wait_send()
+        for half in range(2):
+            for j in range(2):
+                self.second_copy(half, j).wait_send()
+            self.third_copy(half).wait_send()
+
+
+def reduce_tasks(parts):
+    tasks = [part.product(t) for part in parts for t in range(4)]
+
+    def also(at, extra):
+        while len(tasks) <= at:
+            tasks.append(idle)
+        before = tasks[at]
+
+        def both():
+            extra()
+            before()
+
+        tasks[at] = both
+
+    for i, part in enumerate(parts):
+        also(4 * i + 5, part.add_core)
+        also(4 * i + 8, part.add_second)
+        also(4 * i + 10, part.add_third)
+
+    def finish():
+        for part in parts:
+            part.finish()
+
+    return tasks + [finish]
+
+
+def reduce_scratch(arrays, rows, width):
+    block = pltpu.VMEM((arrays, 4, rows, width), bf16)
+    sem = pltpu.SemaphoreType.DMA((arrays, 10))
+    return [
+        block,
+        block,
+        block,
+        pltpu.VMEM((arrays, 2, 2, rows // 2, width), bf16),
+        pltpu.VMEM((arrays, 2, rows // 2, width), bf16),
+        sem,
+        sem,
+    ]
+
+
 def gather_norm(n, x, gain, whole, send, recv):
     line = Line(n, x.shape[0], None, None, whole, None, (send, recv))
     line.greet()
@@ -545,6 +742,110 @@
         line.tiles(k, one)
 
     line.run(point)
+
+
+def gather_weights(
+    n,
+    x,
+    gain,
+    w_in,
+    w_gate,
+    w_out,
+    blocks,
+    chan,
+    whole,
+    all_in,
+    all_gate,
+    all_out,
+    all_blocks,
+    all_chan,
+    send,
+    recv,
+    raw,
+    plane_send,
+    plane_recv,
+):
+    line = Line(n, x.shape[0], None, None, whole, None, (send, recv))
+    plane = Plane()
+    line.greet(plane)
+    sems = plane_send, plane_recv
+    rows, piece = w_in.shape[0], blocks.shape[1]
+    lines = chan.shape[0]
+
+    def view_of(array):
+        def view(owner, half):
+            first = owner * rows + half * (rows // 2)
+            return array.at[pl.ds(pl.multiple_of(first, TILE), rows // 2)]
+
+        return view
+
+    def blocks_view(owner, half):
+        return all_blocks.at[:, pl.ds(pl.multiple_of(owner * piece, TILE), piece)]
+
+    def chan_view(owner, half):
+        return raw.at[pl.ds(pl.multiple_of(owner * lines, TILE), lines)]
+
+    items = [(view_of(array), (0, 1)) for array in (all_in, all_gate, all_out)]
+    items += [(blocks_view, (0,)), (chan_view, (1,))]
+
+    def copies(stage):
+        return [
+            copy
+            for item, (view, halves) in enumerate(items)
+            for copy in plane.gather_copies(item, view, halves, stage, sems)
+        ]
+
+    def stage_task(stage):
+        def task():
+            if stage:
+                for copy in copies(stage - 1):
+                    copy.wait_recv()
+            for copy in copies(stage):
+                copy.start()
+
+        return task
+
+    def last():
+        for copy in copies(2):
+            copy.wait_recv()
+        lane = lax.broadcasted_iota(jnp.int32, (LANE, LANE), 1)
+        row = lax.broadcasted_iota(jnp.int32, (LANE, LANE), 0)
+        total = jnp.zeros((lines, LANE), f32)
+        for owner in range(LANE // piece):
+            moved = ((row < piece) & (row + owner * piece == lane)).astype(f32).astype(bf16)
+            total = total + dot(raw[pl.ds(owner * lines, lines), :], moved)
+        for h in range(lines // SUB):
+            par = total[h * SUB : (h + 1) * SUB]
+            lanes = pl.ds(h * LANE, LANE)
+            all_chan[0:SUB, lanes] = par
+            decay = par[SUB - 1 : SUB]
+            small = jnp.exp(-jnp.abs(decay))
+            one_more = 1.0 + small
+            rest = jnp.where(one_more == 1.0, 1.0, one_more - 1.0)
+            log_one_more = jnp.where(one_more == 1.0, small, jnp.log(one_more) * (small / rest))
+            all_chan[SUB - 1 : SUB, lanes] = jnp.maximum(decay, 0.0) + log_one_more
+            all_chan[SUB : 2 * SUB, lanes] = jnp.broadcast_to(sigmoid(decay), (SUB, LANE))
+        for stage in range(3):
+            for copy in copies(stage):
+                copy.wait_send()
+
+    own = pl.ds(pl.multiple_of(plane.me * rows, TILE), rows)
+    all_in[own, :] = w_in[...]
+    all_gate[own, :] = w_gate[...]
+    all_out[own, :] = w_out[...]
+    all_blocks[:, pl.ds(pl.multiple_of(plane.me * piece, TILE), piece), :] = blocks[...]
+    raw[pl.ds(pl.multiple_of(plane.me * lines, TILE), lines), :] = chan[...]
+
+    def point(k):
+        def one(_, own, at):
+            v = x[own, :].astype(f32)
+            whole[at, :] = (v * rms_scale(v) * gain[...]).astype(bf16)
+
+        line.tiles(k, one)
+
+    tasks = [idle, stage_task(1), idle, idle, stage_task(2), idle, idle, last]
+    stage_task(0)()
+    line.run(point, tasks)
 
 
 def sum_norm_gather(n, x, gain, part, resid, whole, left, right, total, ss, sr, send, recv):
@@ -571,11 +872,18 @@
     return scale * e - value * slope, grad * value * scale
 
 
-def sum_back_gather(
-    n, resid, cot, gain, part, d_resid, gain_grad, whole, left, right, total, ss, sr, send, recv
-):
+def sum_back_gather(n, resid, cot, gain, part, *rest):
+    if len(rest) > 10:
+        norm, cots, d_up, d_gate, hidden, *rest = rest
+        d_resid, gain_grad, whole, *outs = rest[:6]
+        left, right, total, ss, sr, send, recv, *reduce = rest[6:]
+        every = slice(None)
+        sides = ((norm, d_up, every), (norm, d_gate, every), (cots, hidden, every))
+    else:
+        d_resid, gain_grad, whole, left, right, total, ss, sr, send, recv = rest
+        sides = ()
     line = Line(n, resid.shape[0], part, (left, right), whole, (ss, sr), (send, recv))
-    line.greet()
+    line.greet(Plane() if sides else None)
     gain_grad[...] = jnp.zeros_like(gain_grad)
 
     def point(k):
@@ -590,12 +898,34 @@
 
         line.tiles(k, one)
 
-    line.run(point)
-
-
-def sum_back(n, x, d_resid, gain, part, grad_x, left, right, total, ss, sr):
+    if sides:
+        tasks = reduce_tasks(
+            [
+                Reduce(i, *side, *reduce[:5], out, reduce[5:])
+                for i, (side, out) in enumerate(zip(sides, outs))
+            ]
+        )
+        line.run(point, tasks)
+    else:
+        line.run(point)
+
+
+def sum_back(n, x, d_resid, gain, part, *rest):
+    if len(rest) > 6:
+        norm, back_all, cat, mixed, *rest = rest
+        grad_x, *outs = rest[:4]
+        left, right, total, ss, sr, *reduce = rest[4:]
+        width = mixed.shape[1]
+        sides = (
+            (norm, cat, slice(0, width)),
+            (norm, cat, slice(width, 2 * width)),
+            (back_all, mixed, slice(None)),
+        )
+    else:
+        grad_x, left, right, total, ss, sr = rest
+        sides = ()
     line = Line(n, x.shape[0], part, (left, right), None, (ss, sr), None)
-    line.greet()
+    line.greet(Plane() if sides else None)
 
     def point(k):
         line.total(k, total)
@@ -606,10 +936,19 @@
 
         line.tiles(k, one)
 
-    line.run(point)
-
-
-def line_call(body, n, identity, outs, sums, alls, args):
+    if sides:
+        tasks = reduce_tasks(
+            [
+                Reduce(i, *side, *reduce[:5], out, reduce[5:])
+                for i, (side, out) in enumerate(zip(sides, outs))
+            ]
+        )
+        line.run(point, tasks)
+    else:
+        line.run(point)
+
+
+def line_call(body, n, identity, outs, sums, alls, args, more=()):
     whole = pl.BlockSpec(memory_space=pltpu.VMEM)
     local, model = args[0].shape
     sem = pltpu.SemaphoreType.DMA((2, n, PIECES))
@@ -620,6 +959,7 @@
         scratch += [sem, sem]
     if alls:
         scratch += [sem, sem]
+    scratch += more
     moved = sum(a.size * a.dtype.itemsize for a in args)
     return pl.pallas_call(
         functools.partial(body, n),
@@ -678,28 +1018,14 @@
     width = heads * piece * n_dp
     hidden_width = w_up.shape[1]
 
-    flat = jnp.concatenate(
-        [conv_weight.reshape(-1, piece), chan_bias.reshape(-1, piece), decay]
-        + [gate_blocks.transpose(0, 1, 3, 2).reshape(-1, piece)],
-        axis=0,
-    )
-    small_all = lax.all_gather(flat, "dp", axis=1, tiled=True)
-    full_in = lax.all_gather(w_in, "dp", axis=0, tiled=True)
-    full_gate = lax.all_gather(w_gate, "dp", axis=0, tiled=True)
-    full_out = lax.all_gather(w_out, "dp", axis=1, tiled=True)
+    fused = n_dp == 8
+    rows = model // n_dp
+    out_rows, down_rows = w_out.T, w_down.T
     full_up = lax.all_gather(w_up, "dp", axis=0, tiled=True)
     full_gate_ff = lax.all_gather(w_gate_ff, "dp", axis=0, tiled=True)
-    full_down = lax.all_gather(w_down, "dp", axis=1, tiled=True)
-
-    params = small_all[: 8 * heads].astype(f32).reshape(8, width)
-    decay_row = params[7:8]
-    chan = jnp.concatenate(
-        [params[:7], jax.nn.softplus(decay_row), jax.nn.sigmoid(decay_row), jnp.zeros((7, width), f32)],
-        axis=0,
-    )
-    blocks = small_all[8 * heads :].reshape(2, heads, LANE, LANE)
-    blocks = blocks.transpose(1, 3, 0, 2).reshape(heads, LANE, 2 * LANE)
-    blocks_twice = jnp.concatenate([blocks, blocks], axis=1)
+    full_down = lax.all_gather(down_rows, "dp", axis=0, tiled=True)
+    lines = jnp.concatenate([conv_weight, chan_bias, decay[None]], axis=0).transpose(1, 0, 2)
+    lines = lines.reshape(SUB * heads, piece)
 
     steps = count // SUB
     ends = jnp.cumsum(lengths[0], dtype=jnp.int32)
@@ -718,7 +1044,38 @@
     n_mp = lax.axis_size("mp")
     tok = shape_of(bf16, count, model)
     own = shape_of(f32, local_rows, model)
-    (norm_group,) = line_call(gather_norm, n_mp, 0, [tok], False, True, (inputs, gain_f[0:1]))
+    if fused:
+        grown = shape_of(bf16, model, width)
+        norm_group, full_in, full_gate, full_out, blocks, chan = line_call(
+            gather_weights,
+            n_mp,
+            0,
+            [tok, grown, grown, grown, shape_of(bf16, 2 * heads, LANE, LANE), shape_of(f32, 16, width)],
+            False,
+            True,
+            (
+                inputs,
+                gain_f[0:1],
+                w_in,
+                w_gate,
+                out_rows,
+                gate_blocks.reshape(2 * heads, piece, LANE),
+                jnp.pad(lines, ((0, 0), (0, LANE - piece))),
+            ),
+            [pltpu.VMEM((n_dp * SUB * heads, LANE), bf16)] + [pltpu.SemaphoreType.DMA((5, 2, 7))] * 2,
+        )
+    else:
+        (norm_group,) = line_call(gather_norm, n_mp, 0, [tok], False, True, (inputs, gain_f[0:1]))
+        full_in = lax.all_gather(w_in, "dp", axis=0, tiled=True)
+        full_gate = lax.all_gather(w_gate, "dp", axis=0, tiled=True)
+        full_out = lax.all_gather(out_rows, "dp", axis=0, tiled=True)
+        blocks = lax.all_gather(gate_blocks, "dp", axis=2, tiled=True).reshape(2 * heads, LANE, LANE)
+        params = lax.all_gather(lines, "dp", axis=1, tiled=True).astype(f32)
+        params = params.reshape(heads, SUB, LANE).transpose(1, 0, 2).reshape(SUB, width)
+        decay_row = params[7:8]
+        chan = jnp.concatenate(
+            [params[:7], jax.nn.softplus(decay_row)] + [jax.nn.sigmoid(decay_row)] * SUB, axis=0
+        )
     cot = cotangent * token_mask.astype(bf16)[:, None]
     cot_group = lax.all_gather(cot, "mp", axis=0, tiled=True)
 
@@ -735,7 +1092,7 @@
             pltpu.VMEM((count, width), bf16),
         ],
         2 * count * (count * model + 3 * model * width),
-        (norm_group, ocol, orow, pos_col, full_in, full_gate, full_out, chan, blocks_twice),
+        (norm_group, ocol, orow, pos_col, full_in, full_gate, full_out, chan, blocks),
     )
     resid, norm_mid_group = line_call(
         sum_norm_gather, n_mp, 1, [own, tok], True, True, (inputs, gain_f[1:2], back_part)
@@ -749,25 +1106,31 @@
         12 * count * model * hidden_width,
         (norm_mid_group, cot_group, full_up, full_gate_ff, full_down),
     )
-    d_resid, gain_mid, back_group = line_call(
+    d_resid, gain_mid, back_group, *ffn_grads = line_call(
         sum_back_gather,
         n_mp,
         2,
-        [own, shape_of(f32, 1, model), tok],
+        [own, shape_of(f32, 1, model), tok] + [shape_of(f32, rows, hidden_width)] * (3 * fused),
         True,
         True,
-        (resid, cot, gain_f[1:2], d_norm_part),
+        (resid, cot, gain_f[1:2], d_norm_part)
+        + ((norm_mid_group, cot_group, d_up, d_gate_ff, hidden) if fused else ()),
+        reduce_scratch(3, rows, hidden_width) if fused else (),
     )
     output = (
         resid + lax.psum_scatter(ffn_part, "mp", scatter_dimension=0, tiled=True).astype(f32)
     ).astype(bf16)
 
-    def reduced(grad, dimension):
-        return lax.psum_scatter(grad.astype(bf16), "dp", scatter_dimension=dimension, tiled=True).astype(f32)
-
-    grad_down = reduced(dot_first(hidden, cot_group), 1)
-    grad_up = reduced(dot_first(norm_mid_group, d_up), 0)
-    grad_gate_ff = reduced(dot_first(norm_mid_group, d_gate_ff), 0)
+    def reduced(left, right):
+        grad = dot_first(left, right).astype(bf16)
+        return lax.psum_scatter(grad, "dp", scatter_dimension=0, tiled=True).astype(f32)
+
+    if not fused:
+        ffn_grads = [
+            reduced(norm_mid_group, d_up),
+            reduced(norm_mid_group, d_gate_ff),
+            reduced(cot_group, hidden),
+        ]
 
     d_cat, d_norm_back, small, d_blocks, gain_in = local_call(
         mixer_backward,
@@ -803,47 +1166,57 @@
             *kept,
         ),
     )
-    (grad_inputs,) = line_call(
+    grad_inputs, *mix_grads = line_call(
         sum_back,
         n_mp,
         3,
-        [shape_of(bf16, local_rows, model)],
+        [shape_of(bf16, local_rows, model)] + [shape_of(f32, rows, width)] * (3 * fused),
         True,
         False,
-        (inputs, d_resid, gain_f[0:1], d_norm_back),
+        (inputs, d_resid, gain_f[0:1], d_norm_back)
+        + ((norm_group, back_group, d_cat, mixed) if fused else ()),
+        reduce_scratch(3, rows, width) if fused else (),
     )
-    grad_out = reduced(dot_first(mixed, back_group), 1)
-    grad_cat = dot_first(norm_group, d_cat)
-    grad_in = reduced(grad_cat[:, :width], 0)
-    grad_gate = reduced(grad_cat[:, width:], 0)
+    if not fused:
+        mix_grads = [
+            reduced(norm_group, d_cat[:, :width]),
+            reduced(norm_group, d_cat[:, width:]),
+            reduced(back_group, mixed),
+        ]
 
     d_blocks_rows = d_blocks.reshape(heads, n_dp, piece, 2, LANE).transpose(1, 3, 0, 2, 4)
     small_rows = small.reshape(8 * heads, n_dp, piece).transpose(1, 0, 2)
     packed_small = jnp.concatenate(
         [small_rows.reshape(n_dp, -1), d_blocks_rows.reshape(n_dp, -1)], axis=1
     )
-    small_own = lax.psum_scatter(packed_small, "dp", scatter_dimension=0, tiled=True)[0]
+    pad = -packed_small.shape[1] % (SUB * LANE)
+    packed_small = jnp.pad(packed_small, ((0, 0), (0, pad))).reshape(-1, LANE)
+    small_own = lax.psum_scatter(packed_small, "dp", scatter_dimension=0, tiled=True).reshape(-1)
     split_at = 8 * heads * piece
-    rows = small_own[:split_at].reshape(8, heads, piece)
-    grad_blocks = small_own[split_at:].reshape(2, heads, piece, LANE)
-
-    grad_gains = lax.psum_scatter(
-        jnp.concatenate([gain_in, gain_mid], axis=0), ("dp", "mp"), scatter_dimension=1, tiled=True
-    )
+    lines_own = small_own[:split_at].reshape(8, heads, piece)
+    grad_blocks = small_own[split_at : split_at + gate_blocks.size].reshape(gate_blocks.shape)
+
+    owners = n_dp * n_mp
+    gain_parts = jnp.concatenate([gain_in, gain_mid], axis=0).reshape(2, owners, -1).transpose(1, 0, 2)
+    gain_parts = jnp.pad(
+        gain_parts.reshape(owners, -1), ((0, 0), (0, SUB * LANE - 2 * model // owners))
+    ).reshape(-1, LANE)
+    gain_own = lax.psum_scatter(gain_parts, ("dp", "mp"), scatter_dimension=0, tiled=True)
+    grad_gains = gain_own.reshape(-1)[: 2 * model // owners].reshape(2, -1)
     return (
         output,
         grad_inputs,
         grad_gains,
-        grad_in,
-        grad_gate,
-        grad_out,
-        rows[0:4],
-        rows[4:7],
-        rows[7],
+        mix_grads[0],
+        mix_grads[1],
+        mix_grads[2].T,
+        lines_own[0:4],
+        lines_own[4:7],
+        lines_own[7],
         grad_blocks,
-        grad_up,
-        grad_gate_ff,
-        grad_down,
+        ffn_grads[0],
+        ffn_grads[1],
+        ffn_grads[2].T,
     )
 
 

time: 1070 us -> 749 us (0.70)
  waiting for transfers between devices: 364 us -> 157 us
  matrix products: 38.5 us -> 0 us
  Pallas kernels: 576 us -> 543 us
  local copies, waits for them, and re-layouts: 38.2 us -> 20.6 us
  other arithmetic: 20.8 us -> 6.34 us
  blocking collectives: 11.2 us -> 0 us
    reduce_scatter x6 -> x0, waiting for transfers between devices: 264 us -> none  [reduced(): lax.psum_scatter(grad.astype(bf16), 'dp', scatter_dimension=dimension, ti...]
    unnamed x18 -> x9, waiting for transfers between devices: 36.4 us -> 96.1 us
    dot_general x5 -> x0, matrix products: 38.5 us -> none  [dot_first(): lax.dot_general(left, right, (((0,), (0,)), ((), ())), preferred_element_...]
    pallas_call x4, Pallas kernels: 478 us -> 446 us  [line_call(): pl.pallas_call(functools.partial(body, n), out_shape=outs, in_specs=[whol...]
    all_gather x1 -> x0, blocking collectives: 11.2 us -> none  [shards(): small_all = lax.all_gather(flat, 'dp', axis=1, tiled=True)]
    convert_element_type x7 -> x0, other arithmetic: 11.1 us -> none  [the longest x6 11.1 us: reduced(): lax.psum_scatter(grad.astype(bf16), 'dp', scatter_dimension=dimension, ti...]
  transfers between devices with their start and end apart: 16 -> 7, of which waited for: 8 -> 3; matrix products, arithmetic and copies ran while one was open for 8% -> 2% of each run, Pallas kernels for 33% -> 46%
where the time goes in v2:
time: 749 us; the launch traced here: 743 us
  Pallas kernels  543 us (72%)
  waiting for transfers between devices  157 us (21%)
  local copies, waits for them, and re-layouts  20.6 us (3%)
  between operations  15.3 us (2%)
    pallas_call x4, Pallas kernels, line_call(): pl.pallas_call(functools.partial(body, n), out_shape=outs, in_specs=[whol...  446 us
    pallas_call x3, Pallas kernels, local_call(): pl.pallas_call(body, out_shape=outs, in_specs=[whole] * len(args), out_sp...  97.6 us
    unnamed x9, waiting for transfers between devices  96.1 us
    reduce_scatter x1, waiting for transfers between devices, shards(): lax.psum_scatter(ffn_part, 'mp', scatter_dimension=0, tiled=True)  60.6 us
  transfers between devices with their start and end apart: 7, of which 3 were waited for; matrix products, arithmetic and copies ran while one was open for 2% of the time, Pallas kernels for 46%

profile of v2, /device:TPU:0, one launch (start us, length us, event | category | flops | bytes accessed | tf_op | source)
XLA Modules:
  0.0 742.5 jit_solution(15579603312886569423)
XLA Ops:
  7.2 0.7 convert_element_type.19
  7.9 2.2 broadcast_multiply_fusion.cot
  10.2 0.7 all-gather.7.cloned.1.call-update
  11.0 0.7 all-gather.9.cloned.1.call-update
  12.5 1.0 reshape_reshape.8.ocol
  13.5 0.7 reshape_reshape.7.orow
  14.8 1.0 reshape.103.pos
  17.1 120.7 %shard_map.255 = (bf16[1088,1536]{1,0:T(8,128)(2,1)}, bf16[1536,512]{1,0:T(8,128)(2,1)}, bf16[1536,512]{1,0:T(8,128)(2,1)}, bf16[1536,512]{1,0:T(8,128)(2,1)}, b...) custom-call(bf16[272,1536]{1,0:T(8,128)(2,1)} %x.13, f32[1,1536]{1,0:T(1,128)} %get-tuple-element.85.gain, ...), custom_call_target="tpu_custom_call" | custom-call | bytes 147251200 | tf_op jit(solution)/shard_map/pallas_call | solution.py:964
  137.8 27.2 %shard_map.256 = (f32[1088,512]{1,0:T(8,128)}, f32[1088,512]{1,0:T(8,128)}, f32[1088,512]{1,0:T(8,128)}, f32[1088,512]{1,0:T(8,128)}, f32[1088,512]{1,0:T(8,128)...) custom-call(bf16[1088,1536]{1,0:T(8,128)(2,1)} %get-tuple-element.49.tokens.norm.rest_0_, ...), custom_call_target="tpu_custom_call" | custom-call | flops 8770289664 | bytes 26194784 | tf_op jit(solution)/shard_map/pallas_call | solution.py:981
  165.0 114.8 %shard_map.257 = (f32[272,1536]{1,0:T(8,128)}, bf16[1088,1536]{1,0:T(8,128)(2,1)}) custom-call(bf16[272,1536]{1,0:T(8,128)(2,1)} %x.13, f32[1,1536]{1,0:T(1,128)} %get-tuple-element.86.gain, bf16[1088,1536]{1,0:T(8,128)(2,1)} %get-tuple-element.55.part), custom_call_target="tpu_custom_call" | custom-call | bytes 418406400 | tf_op jit(solution)/shard_map/pallas_call | solution.py:964
  279.8 37.9 %shard_map.258 = (bf16[1088,1536]{1,0:T(8,128)(2,1)}, bf16[1088,1536]{1,0:T(8,128)(2,1)}, bf16[1088,1152]{1,0:T(8,128)(2,1)}, bf16[1088,1152]{1,0:T(8,128)(2,1)}, bf16[1088,1152]{1,0:T(8,128)(2,1)}) custom-call(bf16[1088,1536]{1,0:T(8,128)(2,1)} %get-tuple-element.57.tokens.rest_0_, bf16[1088,1536]{1,0:T(8,128)(2,1)} %all-gather.5.cloned.1.call-done.cot.rest_1_, ...), custom_call_target="tpu_custom_call" | custom-call | flops 23102226432 | bytes 31506432 | tf_op jit(solution)/shard_map/pallas_call | solution.py:981
  317.8 131.4 %shard_map.259 = (f32[272,1536]{1,0:T(8,128)}, f32[1,1536]{1,0:T(1,128)}, bf16[1088,1536]{1,0:T(8,128)(2,1)}, f32[192,1152]{1,0:T(8,128)}, f32[192,1152]{1,0:T(8,128)}, /*index=5*/f32[192,1152]{1,0:T(8,128)}) custom-call(f32[272,1536]{1,0:T(8,128)} %get-tuple-element.56.resid, bf16[272,1536]{1,0:T(8,128)(2,1)} %broadcast_multiply_fusion.cot, ...), custom_call_target="tpu_custom_call" | custom-call | bytes 2006016000 | tf_op jit(solution)/shard_map/pallas_call | solution.py:964
  449.2 32.5 %shard_map.260 = (bf16[1088,1024]{1,0:T(8,128)(2,1)}, bf16[1088,1536]{1,0:T(8,128)(2,1)}, f32[8,512]{1,0:T(8,128)}, f32[4,128,256]{2,1,0:T(8,128)}, f32[1,1536]{1,0:T(1,128)}) custom-call(bf16[1088,1536]{1,0:T(8,128)(2,1)} %get-tuple-element.64.back.rest_1_, bf16[1088,1536]{1,0:T(8,128)(2,1)} %get-tuple-element.49.tokens.norm.rest_0_, ...), custom_call_target="tpu_custom_call" | custom-call | flops 8770289664 | bytes 31204192 | tf_op jit(solution)/shard_map/pallas_call | solution.py:981
  481.7 0.7 pad_maximum_fusion
  482.6 0.7 reshape.92
  483.4 1.3 reshape.97
  485.4 0.9 reshape.99
  486.4 0.7 reduce-scatter.2.cloned.1.call-update
  488.3 78.8 %shard_map.261 = (bf16[272,1536]{1,0:T(8,128)(2,1)}, f32[192,512]{1,0:T(8,128)}, f32[192,512]{1,0:T(8,128)}, f32[192,512]{1,0:T(8,128)}) custom-call(bf16[272,1536]{1,0:T(8,128)(2,1)} %x.13, f32[272,1536]{1,0:T(8,128)} %get-tuple-element.63.d_resid, f32[1,1536]{1,0:T(1,128)} %get-tuple-element.85.gain, bf16[1088,1536]{1,0:T(8,128)(2,1)} %get-tuple-element.71.part, ...), custom_call_target="tpu_custom_call" | custom-call | bytes 1588224000 | tf_op jit(solution)/shard_map/pallas_call | solution.py:964
  567.1 37.6 %all-reduce.9.cloned.1.call-done = f32[256,128]{1,0:T(8,128)} async-done(((f32[256,128]{1,0:T(8,128)}), f32[256,128]{1,0:T(8,128)}) %all-reduce.9.cloned.1.call-update) | async-done | bytes 131088
  606.0 55.9 %all-reduce.11.cloned.1.call-done = f32[1088,128]{1,0:T(8,128)} async-done(((f32[1088,128]{1,0:T(8,128)}), f32[1088,128]{1,0:T(8,128)}) %all-reduce.11.cloned.1.call-update) | async-done | bytes 557072
  662.6 0.7 slice.41
  664.6 1.5 constant_dynamic-slice_fusion.2
  666.7 60.6 %reduce-scatter.2.cloned.1.call-done = bf16[272,1536]{1,0:T(8,128)(2,1)} async-done(((bf16[1088,1536]{1,0:T(8,128)(2,1)}), bf16[272,1536]{1,0:T(8,128)(2,1)}) %reduce-scatter.2.cloned.1.call-update) | async-done | bytes 835600 | tf_op jit(solution)/shard_map/reduce_scatter | solution.py:1121
  727.3 2.3 add_convert_fusion
  729.6 0.9 copy.77
  730.5 0.7 copy.78
  731.3 0.7 copy.79
  732.0 0.7 copy.80
  732.8 0.9 copy.81
  733.7 0.9 copy.82
  734.6 0.9 copy.83
  (83 shorter events, 8.3 us)
Async XLA Ops:
  7.2 5.1 copy-start.11
  7.2 272.6 %all-gather.5.cloned.1.call-start = ((), (), s32[]{:S(2)}) async-start(), calls=%async_computation.1 | async-start | bytes 4177920 | tf_op jit(solution)/shard_map/all_gather | solution.py:1080
  7.9 6.3 copy-start.12
  7.9 6.3 copy-start.13
  7.9 6.3 copy-start.14
  7.9 6.3 copy-start.15
  10.2 6.3 copy-start.8
  10.2 269.6 %all-gather.7.cloned.1.call-start = ((), (), s32[]{:S(2)}) async-start(), calls=%async_computation.2 | async-start | bytes 3981312 | tf_op jit(solution)/shard_map/all_gather | solution.py:1024
  10.9 268.9 %all-gather.9.cloned.1.call-start = ((), (), s32[]{:S(2)}) async-start(), calls=%async_computation.3 | async-start | bytes 3981312 | tf_op jit(solution)/shard_map/all_gather | solution.py:1025
  11.7 268.2 %all-gather.11.cloned.1.call-start = ((), (), s32[]{:S(2)}) async-start(), calls=%async_computation.4 | async-start | bytes 3981312 | tf_op jit(solution)/shard_map/all_gather | solution.py:1026
  12.2 592.4 %all-reduce.9.cloned.1.call-start = ((), (), s32[]{:S(2)}) async-start(), calls=%async_computation.6 | async-start | bytes 262144
  449.2 32.5 %copy-start.10 = (f32[1,1536]{1,0:T(1,128)S(1)}, f32[1,1536]{1,0:T(1,128)}, u32[]{:S(2)}) copy-start(f32[1,1536]{1,0:T(1,128)} %get-tuple-element.76) | copy-start | bytes 18436
  481.7 3.4 copy-start.9
  483.4 178.5 %all-reduce.11.cloned.1.call-start = ((), (), s32[]{:S(2)}) async-start(), calls=%async_computation.7 | async-start | bytes 1114112
  486.3 0.8 copy-start.16
  486.3 241.0 %reduce-scatter.2.cloned.1.call-start = ((), (), s32[]{:S(2)}) async-start(), calls=%async_computation.5 | async-start | bytes 4177920 | tf_op jit(solution)/shard_map/reduce_scatter | solution.py:1121
  488.3 239.0 %copy-start = (f32[272,1536]{1,0:T(8,128)S(1)}, f32[272,1536]{1,0:T(8,128)}, u32[]{:S(2)}) copy-start(f32[272,1536]{1,0:T(8,128)} %get-tuple-element.56.resid) | copy-start | bytes 5013508
  567.1 162.5 %copy-start.4 = (bf16[272,1536]{1,0:T(8,128)(2,1)S(1)}, bf16[272,1536]{1,0:T(8,128)(2,1)}, u32[]{:S(2)}) copy-start(bf16[272,1536]{1,0:T(8,128)(2,1)} %get-tuple-element.101) | copy-start | bytes 2506756
  666.7 64.5 %copy-start.6 = (f32[192,512]{1,0:T(8,128)S(1)}, f32[192,512]{1,0:T(8,128)}, u32[]{:S(2)}) copy-start(f32[192,512]{1,0:T(8,128)} %get-tuple-element.104) | copy-start | bytes 1179652
  727.3 3.2 copy-start.7
  729.6 2.4 copy-start.5
  729.6 3.2 copy-start.3
  730.5 3.2 copy-start.2
  732.0 2.6 copy-start.1
Sparse Core Ops, SparseCore 0:
  10.3 94.7 all-gather.4
  107.0 31.8 all-gather.6
  140.8 33.9 all-gather.8
  176.6 33.9 all-gather.10
  483.5 121.1 all-reduce.8
  608.2 53.5 all-reduce.10
  664.3 62.9 reduce-scatter.1

commit v3 on v2

--- a/solution.py
+++ b/solution.py
@@ -225,8 +225,7 @@
     state_ref,
     dcat_ref,
     dnorm_ref,
-    small_ref,
-    dblocks_ref,
+    little_ref,
     dgain_ref,
     dmix_arr,
     dmix,
@@ -235,6 +234,8 @@
     after,
     before,
     low,
+    small_ref,
+    dblocks_ref,
 ):
     count, _ = back.shape
     width = w_in.shape[1]
@@ -369,6 +370,11 @@
         return carry
 
     lax.fori_loop(0, blocks_of, unmix, 0)
+    lines = [small_ref[0:SUB, h * LANE : (h + 1) * LANE] for h in range(heads)]
+    lines.append(jnp.zeros((LANE - SUB * heads, LANE), f32))
+    little_ref[:, pl.ds(2 * width, LANE)] = jnp.concatenate(lines, axis=0).T
+    for h in range(heads):
+        little_ref[:, pl.ds(2 * h * LANE, 2 * LANE)] = dblocks_ref[h]
     dgain_ref[...] = jnp.zeros_like(dgain_ref)
 
     def leave(b, carry):
@@ -649,10 +655,13 @@
 
         return task
 
+    def keep(self, t):
+        return self.mine[t]
+
     def add_core(self):
         for t in range(4):
             self.core_copy(t).wait_recv()
-            self.mine[t] = (self.mine[t].astype(f32) + self.got[t].astype(f32)).astype(bf16)
+            self.mine[t] = (self.keep(t).astype(f32) + self.got[t].astype(f32)).astype(self.mine.dtype)
         for half in range(2):
             for j in range(2):
                 self.second_copy(half, j).start()
@@ -666,7 +675,7 @@
             far = 1 - self.bit(2 if half else 4)
             self.mine[block, at] = (
                 self.mine[block, at].astype(f32) + self.second[half, far].astype(f32)
-            ).astype(bf16)
+            ).astype(self.mine.dtype)
             self.third_copy(half).start()
 
     def add_third(self):
@@ -690,7 +699,26 @@
             self.third_copy(half).wait_send()
 
 
-def reduce_tasks(parts):
+class Given(Reduce):
+    def __init__(self, given, mine, got, second, third, out, sems):
+        super().__init__(0, None, None, None, mine, mine, got, second, third, out, sems)
+        self.given = given
+
+    def rows_of(self, t, core):
+        return pl.ds(pl.multiple_of((2 * t + core) * self.rows, self.rows), self.rows)
+
+    def core_copy(self, t):
+        return self.copy(self.given.at[self.rows_of(t, 1 - self.bit(1))], self.got.at[t], t, 1)
+
+    def start(self):
+        for t in range(4):
+            self.core_copy(t).start()
+
+    def keep(self, t):
+        return self.given[self.rows_of(t, self.bit(1)), :]
+
+
+def reduce_tasks(parts, given=None):
     tasks = [part.product(t) for part in parts for t in range(4)]
 
     def also(at, extra):
@@ -709,11 +737,29 @@
         also(4 * i + 8, part.add_second)
         also(4 * i + 10, part.add_third)
 
+    if given is not None:
+        also(0, given.start)
+        also(2, given.add_core)
+        also(4, given.add_second)
+        also(6, given.add_third)
+
     def finish():
-        for part in parts:
+        for part in parts + ([] if given is None else [given]):
             part.finish()
 
     return tasks + [finish]
+
+
+def given_scratch(rows, width):
+    sem = pltpu.SemaphoreType.DMA((1, 10))
+    return [
+        pltpu.VMEM((1, 4, rows, width), f32),
+        pltpu.VMEM((1, 4, rows, width), f32),
+        pltpu.VMEM((1, 2, 2, rows // 2, width), f32),
+        pltpu.VMEM((1, 2, rows // 2, width), f32),
+        sem,
+        sem,
+    ]
 
 
 def reduce_scratch(arrays, rows, width):
@@ -912,9 +958,10 @@
 
 def sum_back(n, x, d_resid, gain, part, *rest):
     if len(rest) > 6:
-        norm, back_all, cat, mixed, *rest = rest
-        grad_x, *outs = rest[:4]
-        left, right, total, ss, sr, *reduce = rest[4:]
+        norm, back_all, cat, mixed, little, *rest = rest
+        grad_x, *outs, little_out = rest[:5]
+        left, right, total, ss, sr, *reduce = rest[5:]
+        given = Given(little, *reduce[7:11], little_out, reduce[11:])
         width = mixed.shape[1]
         sides = (
             (norm, cat, slice(0, width)),
@@ -939,9 +986,10 @@
     if sides:
         tasks = reduce_tasks(
             [
-                Reduce(i, *side, *reduce[:5], out, reduce[5:])
+                Reduce(i, *side, *reduce[:5], out, reduce[5:7])
                 for i, (side, out) in enumerate(zip(sides, outs))
-            ]
+            ],
+            given,
         )
         line.run(point, tasks)
     else:
@@ -1077,7 +1125,8 @@
             [params[:7], jax.nn.softplus(decay_row)] + [jax.nn.sigmoid(decay_row)] * SUB, axis=0
         )
     cot = cotangent * token_mask.astype(bf16)[:, None]
-    cot_group = lax.all_gather(cot, "mp", axis=0, tiled=True)
+    cot_late, norm_group = lax.optimization_barrier((cot, norm_group))
+    cot_group = lax.all_gather(cot_late, "mp", axis=0, tiled=True)
 
     wide = pltpu.VMEM((count, width), f32)
     saved = [shape_of(f32, count, width)] * 6
@@ -1117,10 +1166,6 @@
         + ((norm_mid_group, cot_group, d_up, d_gate_ff, hidden) if fused else ()),
         reduce_scratch(3, rows, hidden_width) if fused else (),
     )
-    output = (
-        resid + lax.psum_scatter(ffn_part, "mp", scatter_dimension=0, tiled=True).astype(f32)
-    ).astype(bf16)
-
     def reduced(left, right):
         grad = dot_first(left, right).astype(bf16)
         return lax.psum_scatter(grad, "dp", scatter_dimension=0, tiled=True).astype(f32)
@@ -1132,13 +1177,12 @@
             reduced(cot_group, hidden),
         ]
 
-    d_cat, d_norm_back, small, d_blocks, gain_in = local_call(
+    d_cat, d_norm_back, little, gain_in = local_call(
         mixer_backward,
         [
             shape_of(bf16, count, 2 * width),
             tok,
-            shape_of(f32, 8, width),
-            shape_of(f32, heads, LANE, 2 * LANE),
+            shape_of(f32, LANE, 2 * width + LANE),
             shape_of(f32, 1, model),
         ],
         [
@@ -1149,6 +1193,8 @@
             pltpu.VMEM((count + TAIL, width), f32),
             pltpu.VMEM((ROWS + TAIL, width), f32),
             pltpu.VMEM((count, 2 * width), bf16),
+            pltpu.VMEM((SUB, width), f32),
+            pltpu.VMEM((heads, LANE, 2 * LANE), f32),
         ],
         2 * count * (3 * count * width + 3 * model * width),
         (
@@ -1166,35 +1212,33 @@
             *kept,
         ),
     )
+    ffn_sum = lax.psum_scatter(ffn_part, "mp", scatter_dimension=0, tiled=True)
+    ffn_sum, d_norm_back = lax.optimization_barrier((ffn_sum, d_norm_back))
+    output = (resid + ffn_sum.astype(f32)).astype(bf16)
     grad_inputs, *mix_grads = line_call(
         sum_back,
         n_mp,
         3,
-        [shape_of(bf16, local_rows, model)] + [shape_of(f32, rows, width)] * (3 * fused),
+        [shape_of(bf16, local_rows, model)]
+        + ([shape_of(f32, rows, width)] * 3 + [shape_of(f32, piece, little.shape[1])]) * fused,
         True,
         False,
         (inputs, d_resid, gain_f[0:1], d_norm_back)
-        + ((norm_group, back_group, d_cat, mixed) if fused else ()),
-        reduce_scratch(3, rows, width) if fused else (),
+        + ((norm_group, back_group, d_cat, mixed, little) if fused else ()),
+        reduce_scratch(3, rows, width) + given_scratch(piece, little.shape[1]) if fused else (),
     )
-    if not fused:
+    if fused:
+        *mix_grads, little_own = mix_grads
+    else:
         mix_grads = [
             reduced(norm_group, d_cat[:, :width]),
             reduced(norm_group, d_cat[:, width:]),
             reduced(back_group, mixed),
         ]
-
-    d_blocks_rows = d_blocks.reshape(heads, n_dp, piece, 2, LANE).transpose(1, 3, 0, 2, 4)
-    small_rows = small.reshape(8 * heads, n_dp, piece).transpose(1, 0, 2)
-    packed_small = jnp.concatenate(
-        [small_rows.reshape(n_dp, -1), d_blocks_rows.reshape(n_dp, -1)], axis=1
-    )
-    pad = -packed_small.shape[1] % (SUB * LANE)
-    packed_small = jnp.pad(packed_small, ((0, 0), (0, pad))).reshape(-1, LANE)
-    small_own = lax.psum_scatter(packed_small, "dp", scatter_dimension=0, tiled=True).reshape(-1)
-    split_at = 8 * heads * piece
-    lines_own = small_own[:split_at].reshape(8, heads, piece)
-    grad_blocks = small_own[split_at : split_at + gate_blocks.size].reshape(gate_blocks.shape)
+        little_own = lax.psum_scatter(little, "dp", scatter_dimension=0, tiled=True)
+    lines_own = little_own[:, 2 * width : 2 * width + SUB * heads].reshape(piece, heads, SUB)
+    lines_own = lines_own.transpose(2, 1, 0)
+    grad_blocks = little_own[:, : 2 * width].reshape(piece, heads, 2, LANE).transpose(2, 1, 0, 3)
 
     owners = n_dp * n_mp
     gain_parts = jnp.concatenate([gain_in, gain_mid], axis=0).reshape(2, owners, -1).transpose(1, 0, 2)

time: 749 us -> 778 us (1.039)
  waiting for transfers between devices: 157 us -> 216 us
  Pallas kernels: 543 us -> 515 us
    unnamed x9 -> x7, waiting for transfers between devices: 96.1 us -> 126 us
    pallas_call x4, Pallas kernels: 446 us -> 417 us  [line_call(): pl.pallas_call(functools.partial(body, n), out_shape=outs, in_specs=[whol...]
    all_gather x1, waiting for transfers between devices: 0.02 us -> 26.7 us  [shards(): full_down = lax.all_gather(down_rows, 'dp', axis=0, tiled=True)]
  transfers between devices with their start and end apart: 7 -> 6, of which waited for: 3 -> 3; matrix products, arithmetic and copies ran while one was open for 2% -> 1% of each run, Pallas kernels for 46% -> 22%
where the time goes in v3:
time: 778 us; the launch traced here: 772 us
  Pallas kernels  515 us (66%)
  waiting for transfers between devices  216 us (28%)
  local copies, waits for them, and re-layouts  19.6 us (3%)
  between operations  14.5 us (2%)
    pallas_call x4, Pallas kernels, line_call(): pl.pallas_call(functools.partial(body, n), out_shape=outs, in_specs=[whol...  417 us
    unnamed x7, waiting for transfers between devices  126 us
    pallas_call x3, Pallas kernels, local_call(): pl.pallas_call(body, out_shape=outs, in_specs=[whole] * len(args), out_sp...  98.4 us
    reduce_scatter x1, waiting for transfers between devices, shards(): ffn_sum = lax.psum_scatter(ffn_part, 'mp', scatter_dimension=0, tiled=True)  63.2 us
    all_gather x1, waiting for transfers between devices, shards(): full_down = lax.all_gather(down_rows, 'dp', axis=0, tiled=True)  26.7 us
  transfers between devices with their start and end apart: 6, of which 3 were waited for; matrix products, arithmetic and copies ran while one was open for 1% of the time, Pallas kernels for 22%

profile of v3, /device:TPU:0, one launch (start us, length us, event | category | flops | bytes accessed | tf_op | source)
XLA Modules:
  0.0 772.1 jit_solution(1662587722201274618)
XLA Ops:
  7.2 1.4 fusion
  8.6 0.7 convert_element_type.17
  9.3 0.7 maximum_bitcast_fusion
  10.0 2.2 broadcast_multiply_fusion.cot
  12.8 67.1 %shard_map.255 = (bf16[1088,1536]{1,0:T(8,128)(2,1)}, bf16[1536,512]{1,0:T(8,128)(2,1)}, bf16[1536,512]{1,0:T(8,128)(2,1)}, bf16[1536,512]{1,0:T(8,128)(2,1)}, b...) custom-call(bf16[272,1536]{1,0:T(8,128)(2,1)} %x.11, f32[1,1536]{1,0:T(1,128)} %get-tuple-element.132.gain, ...), custom_call_target="tpu_custom_call" | custom-call | bytes 147251200 | tf_op jit(solution)/shard_map/pallas_call | solution.py:1012
  80.0 0.7 all-gather.7.cloned.1.call-update
  80.8 0.7 all-gather.9.cloned.1.call-update
  82.3 1.0 reshape_reshape.8.ocol
  83.3 0.7 reshape_reshape.7.orow
  84.6 1.0 reshape.76.pos
  85.6 27.8 %shard_map.256 = (f32[1088,512]{1,0:T(8,128)}, f32[1088,512]{1,0:T(8,128)}, f32[1088,512]{1,0:T(8,128)}, f32[1088,512]{1,0:T(8,128)}, f32[1088,512]{1,0:T(8,128)...) custom-call(bf16[1088,1536]{1,0:T(8,128)(2,1)} %get-tuple-element.54.tokens.norm.rest_0_, ...), custom_call_target="tpu_custom_call" | custom-call | flops 8770289664 | bytes 26194784 | tf_op jit(solution)/shard_map/pallas_call | solution.py:1029
  113.4 141.1 %shard_map.257 = (f32[272,1536]{1,0:T(8,128)}, bf16[1088,1536]{1,0:T(8,128)(2,1)}) custom-call(bf16[272,1536]{1,0:T(8,128)(2,1)} %x.11, f32[1,1536]{1,0:T(1,128)} %get-tuple-element.133.gain, bf16[1088,1536]{1,0:T(8,128)(2,1)} %get-tuple-element.60.part), custom_call_target="tpu_custom_call" | custom-call | bytes 418406400 | tf_op jit(solution)/shard_map/pallas_call | solution.py:1012
  254.5 26.7 %all-gather.11.cloned.1.call-done.w_down = bf16[1536,1152]{1,0:T(8,128)(2,1)} async-done(((bf16[192,1152]{1,0:T(8,128)(2,1)}), bf16[1536,1152]{1,0:T(8,128)(2,1)}) %all-gather.11.cloned.1.call-update) | async-done | bytes 3538960 | tf_op jit(solution)/shard_map/all_gather | solution.py:1074
  281.2 37.9 %shard_map.258 = (bf16[1088,1536]{1,0:T(8,128)(2,1)}, bf16[1088,1536]{1,0:T(8,128)(2,1)}, bf16[1088,1152]{1,0:T(8,128)(2,1)}, bf16[1088,1152]{1,0:T(8,128)(2,1)}, bf16[1088,1152]{1,0:T(8,128)(2,1)}) custom-call(bf16[1088,1536]{1,0:T(8,128)(2,1)} %get-tuple-element.62.tokens.rest_0_, bf16[1088,1536]{1,0:T(8,128)(2,1)} %all-gather.5.cloned.1.call-done.cot.rest_1_, ...), custom_call_target="tpu_custom_call" | custom-call | flops 23102226432 | bytes 31506432 | tf_op jit(solution)/shard_map/pallas_call | solution.py:1029
  319.1 129.6 %shard_map.259 = (f32[272,1536]{1,0:T(8,128)}, f32[1,1536]{1,0:T(1,128)}, bf16[1088,1536]{1,0:T(8,128)(2,1)}, f32[192,1152]{1,0:T(8,128)}, f32[192,1152]{1,0:T(8,128)}, /*index=5*/f32[192,1152]{1,0:T(8,128)}) custom-call(f32[272,1536]{1,0:T(8,128)} %get-tuple-element.61.resid, bf16[272,1536]{1,0:T(8,128)(2,1)} %broadcast_multiply_fusion.cot, ...), custom_call_target="tpu_custom_call" | custom-call | bytes 2006016000 | tf_op jit(solution)/shard_map/pallas_call | solution.py:1012
  448.7 32.8 %shard_map.260 = (bf16[1088,1024]{1,0:T(8,128)(2,1)}, bf16[1088,1536]{1,0:T(8,128)(2,1)}, f32[128,1152]{1,0:T(8,128)}, f32[1,1536]{1,0:T(1,128)}) custom-call(bf16[1088,1536]{1,0:T(8,128)(2,1)} %get-tuple-element.69.back.rest_1_, bf16[1088,1536]{1,0:T(8,128)(2,1)} %get-tuple-element.54.tokens.norm.rest_0_, s32[1088,1]{1,0:T(8,128)} %reshape_reshape.8.ocol, ...), custom_call_target="tpu_custom_call" | custom-call | flops 8770289664 | bytes 31253344 | tf_op jit(solution)/shard_map/pallas_call | solution.py:1029
  481.5 0.7 pad_maximum_fusion
  482.5 0.7 reshape.71
  483.8 123.2 %all-reduce.6.cloned.1.call-done = f32[256,128]{1,0:T(8,128)} async-done(((f32[256,128]{1,0:T(8,128)}), f32[256,128]{1,0:T(8,128)}) %all-reduce.6.cloned.1.call-update) | async-done | bytes 131088
  606.9 0.7 dynamic-slice_bitcast_fusion
  608.2 63.2 %reduce-scatter.2.cloned.1.call-done = bf16[272,1536]{1,0:T(8,128)(2,1)} async-done(((bf16[1088,1536]{1,0:T(8,128)(2,1)}), bf16[272,1536]{1,0:T(8,128)(2,1)}) %reduce-scatter.2.cloned.1.call-update) | async-done | bytes 835600 | tf_op jit(solution)/shard_map/reduce_scatter | solution.py:1215
  671.5 79.0 %shard_map.261 = (bf16[272,1536]{1,0:T(8,128)(2,1)}, f32[192,512]{1,0:T(8,128)}, f32[192,512]{1,0:T(8,128)}, f32[192,512]{1,0:T(8,128)}, f32[16,1152]{1,0:T(8,128)}) custom-call(bf16[272,1536]{1,0:T(8,128)(2,1)} %x.11, f32[272,1536]{1,0:T(8,128)} %get-tuple-element.78.d_resid, f32[1,1536]{1,0:T(1,128)} %get-tuple-element.132.gain, ...), custom_call_target="tpu_custom_call" | custom-call | bytes 1647206400 | tf_op jit(solution)/shard_map/pallas_call | solution.py:1012
  750.5 0.7 slice.34
  751.9 0.8 slice.38
  752.7 2.2 add_convert_fusion
  756.9 2.1 copy.83
  759.0 1.8 copy.84
  760.8 0.7 copy.85
  761.6 0.7 copy.86
  762.3 0.9 copy.87
  763.2 0.9 copy.88
  764.1 0.9 copy.89
  (58 shorter events, 6.2 us)
Async XLA Ops:
  7.2 247.3 %all-gather.5.cloned.1.call-start = ((), (), s32[]{:S(2)}) async-start(), calls=%async_computation.1 | async-start | bytes 4177920 | tf_op jit(solution)/shard_map/all_gather | solution.py:1129
  12.2 69.9 %copy-start.7 = (s32[1,1088]{1,0:T(1,128)S(1)}, s32[1,1088]{1,0:T(1,128)}, u32[]{:S(2)}) copy-start(s32[1,1088]{1,0:T(1,128)} %param.19) | copy-start | bytes 13060
  12.8 71.2 %copy-start.8 = (s32[1,4]{1,0:T(1,128)S(1)}, s32[1,4]{1,0:T(1,128)}, u32[]{:S(2)}) copy-start(s32[1,4]{1,0:T(1,128)} %param.20) | copy-start | bytes 52
  80.0 174.5 %all-gather.7.cloned.1.call-start = ((), (), s32[]{:S(2)}) async-start(), calls=%async_computation.2 | async-start | bytes 3981312 | tf_op jit(solution)/shard_map/all_gather | solution.py:1072
  80.7 173.8 %all-gather.9.cloned.1.call-start = ((), (), s32[]{:S(2)}) async-start(), calls=%async_computation.3 | async-start | bytes 3981312 | tf_op jit(solution)/shard_map/all_gather | solution.py:1073
  81.5 199.8 %all-gather.11.cloned.1.call-start = ((), (), s32[]{:S(2)}) async-start(), calls=%async_computation.4 | async-start | bytes 3981312 | tf_op jit(solution)/shard_map/all_gather | solution.py:1074
  82.0 524.9 %all-reduce.6.cloned.1.call-start = ((), (), s32[]{:S(2)}) async-start(), calls=%async_computation.6 | async-start | bytes 262144
  448.7 32.8 %copy-start.6 = (f32[1,1536]{1,0:T(1,128)S(1)}, f32[1,1536]{1,0:T(1,128)}, u32[]{:S(2)}) copy-start(f32[1,1536]{1,0:T(1,128)} %get-tuple-element.85) | copy-start | bytes 18436
  483.2 188.3 %reduce-scatter.2.cloned.1.call-start = ((), (), s32[]{:S(2)}) async-start(), calls=%async_computation.5 | async-start | bytes 4177920 | tf_op jit(solution)/shard_map/reduce_scatter | solution.py:1215
  671.5 81.2 %copy-start = (f32[272,1536]{1,0:T(8,128)S(1)}, f32[272,1536]{1,0:T(8,128)}, u32[]{:S(2)}) copy-start(f32[272,1536]{1,0:T(8,128)} %get-tuple-element.61.resid) | copy-start | bytes 5013508
  755.0 5.9 copy-start.5
  755.0 6.6 copy-start.4
  755.0 7.4 copy-start.3
  759.0 4.3 copy-start.2
  761.6 2.6 copy-start.1
Sparse Core Ops, SparseCore 0:
  80.1 88.2 all-gather.4
  170.3 39.2 all-gather.6
  211.5 33.9 all-gather.8
  247.2 33.9 all-gather.10
  483.3 123.5 all-reduce.5
  609.1 62.3 reduce-scatter.1

commit v4 on v3

--- a/solution.py
+++ b/solution.py
@@ -418,21 +418,15 @@
                 pl.semaphore_signal(
                     barrier, inc=1, device_id={"dp": plane.other(bit)}, device_id_type=MESH
                 )
-        for has, other in zip(self.has, (self.me - 1, self.me + 1)):
-
-            @pl.when(has)
-            def _():
-                pl.semaphore_signal(barrier, inc=1, device_id={"mp": other}, device_id_type=MESH)
-
-        both = self.has[0] & self.has[1]
-
-        @pl.when(both)
-        def _():
-            pl.semaphore_wait(barrier, more + 2)
-
-        @pl.when(jnp.logical_not(both))
-        def _():
-            pl.semaphore_wait(barrier, more + 1)
+        for away in range(1, self.n):
+            more += 1
+            pl.semaphore_signal(
+                barrier,
+                inc=1,
+                device_id={"mp": lax.rem(self.me + away, self.n)},
+                device_id_type=MESH,
+            )
+        pl.semaphore_wait(barrier, more)
 
     def rows_at(self, owner, k):
         first, rows = self.pieces[k]
@@ -572,6 +566,11 @@
     pass
 
 
+def all_of(tasks):
+    for task in tasks:
+        task()
+
+
 class Plane:
     bits = (1, 2, 4)
     orders = ((4, 2, 1), (2, 4, 1))
@@ -718,7 +717,7 @@
         return self.given[self.rows_of(t, self.bit(1)), :]
 
 
-def reduce_tasks(parts, given=None):
+def reduce_tasks(parts, given=()):
     tasks = [part.product(t) for part in parts for t in range(4)]
 
     def also(at, extra):
@@ -737,14 +736,14 @@
         also(4 * i + 8, part.add_second)
         also(4 * i + 10, part.add_third)
 
-    if given is not None:
-        also(0, given.start)
-        also(2, given.add_core)
-        also(4, given.add_second)
-        also(6, given.add_third)
+    for part in given:
+        also(0, part.start)
+        also(2, part.add_core)
+        also(4, part.add_second)
+        also(6, part.add_third)
 
     def finish():
-        for part in parts + ([] if given is None else [given]):
+        for part in [*parts, *given]:
             part.finish()
 
     return tasks + [finish]
@@ -894,9 +893,18 @@
     line.run(point, tasks)
 
 
-def sum_norm_gather(n, x, gain, part, resid, whole, left, right, total, ss, sr, send, recv):
+def sum_norm_gather(
+    n, x, cot, gain, part, resid, whole, cots, left, right, total, ss, sr, send, recv, cot_send, cot_recv
+):
     line = Line(n, x.shape[0], part, (left, right), whole, (ss, sr), (send, recv))
+    other = Line(n, x.shape[0], None, None, cots, None, (cot_send, cot_recv))
     line.greet()
+
+    def keep(_, own, at):
+        cots[at, :] = cot[own, :]
+
+    for k in range(PIECES):
+        other.tiles(k, keep)
 
     def point(k):
         line.total(k, total)
@@ -908,7 +916,15 @@
 
         line.tiles(k, one)
 
-    line.run(point)
+    tasks = []
+    for k in range(PIECES):
+        for stage in range(n):
+            at = k * (n - 1) + stage
+            task = functools.partial(other.forward, k, stage) if stage else functools.partial(other.spread, k)
+            tasks += [[] for _ in range(at + 1 - len(tasks))]
+            tasks[at].append(task)
+    line.run(point, [functools.partial(all_of, group) for group in tasks])
+    other.finish()
 
 
 def norm_back(value, gain, grad):
@@ -958,10 +974,14 @@
 
 def sum_back(n, x, d_resid, gain, part, *rest):
     if len(rest) > 6:
-        norm, back_all, cat, mixed, little, *rest = rest
-        grad_x, *outs, little_out = rest[:5]
-        left, right, total, ss, sr, *reduce = rest[5:]
-        given = Given(little, *reduce[7:11], little_out, reduce[11:])
+        norm, back_all, cat, mixed, little, gains, *rest = rest
+        grad_x, *outs, little_out, gains_out = rest[:6]
+        left, right, total, ss, sr, *reduce = rest[6:]
+        given = [
+            Given(little, *reduce[7:11], little_out, reduce[11:13]),
+            Given(gains, *reduce[13:17], gains_out, reduce[17:19]),
+        ]
+        met, met_send, met_recv = reduce[19:]
         width = mixed.shape[1]
         sides = (
             (norm, cat, slice(0, width)),
@@ -991,6 +1011,29 @@
             ],
             given,
         )
+        me = lax.axis_index("mp")
+
+        def meet(away):
+            return pltpu.make_async_remote_copy(
+                src_ref=gains_out,
+                dst_ref=met.at[away - 1],
+                send_sem=met_send.at[away - 1],
+                recv_sem=met_recv.at[away - 1],
+                device_id={"mp": lax.rem(me + away, n)},
+                device_id_type=MESH,
+            )
+
+        def send_gains():
+            for away in range(1, n):
+                meet(away).start()
+
+        def add_gains():
+            for away in range(1, n):
+                meet(away).wait()
+            gains_out[...] += sum(met[away] for away in range(n - 1))
+
+        tasks[7:7] = [send_gains]
+        tasks.append(add_gains)
         line.run(point, tasks)
     else:
         line.run(point)
@@ -1125,8 +1168,6 @@
             [params[:7], jax.nn.softplus(decay_row)] + [jax.nn.sigmoid(decay_row)] * SUB, axis=0
         )
     cot = cotangent * token_mask.astype(bf16)[:, None]
-    cot_late, norm_group = lax.optimization_barrier((cot, norm_group))
-    cot_group = lax.all_gather(cot_late, "mp", axis=0, tiled=True)
 
     wide = pltpu.VMEM((count, width), f32)
     saved = [shape_of(f32, count, width)] * 6
@@ -1143,8 +1184,15 @@
         2 * count * (count * model + 3 * model * width),
         (norm_group, ocol, orow, pos_col, full_in, full_gate, full_out, chan, blocks),
     )
-    resid, norm_mid_group = line_call(
-        sum_norm_gather, n_mp, 1, [own, tok], True, True, (inputs, gain_f[1:2], back_part)
+    resid, norm_mid_group, cot_group = line_call(
+        sum_norm_gather,
+        n_mp,
+        1,
+        [own, tok, tok],
+        True,
+        True,
+        (inputs, cot, gain_f[1:2], back_part),
+        [pltpu.SemaphoreType.DMA((2, n_mp, PIECES))] * 2,
     )
 
     hid = shape_of(bf16, count, hidden_width)
@@ -1212,6 +1260,11 @@
             *kept,
         ),
     )
+    share = model // (n_dp * n_mp)
+    gain_parts = jnp.concatenate([gain_in, gain_mid], axis=0).reshape(2, n_dp, n_mp, share)
+    gain_parts = gain_parts.transpose(1, 2, 0, 3).reshape(n_dp, 2 * n_mp, share)
+    gain_parts = jnp.pad(gain_parts, ((0, 0), (0, 2 * SUB - 2 * n_mp), (0, LANE - share)))
+    gain_parts = gain_parts.reshape(2 * SUB * n_dp, LANE)
     ffn_sum = lax.psum_scatter(ffn_part, "mp", scatter_dimension=0, tiled=True)
     ffn_sum, d_norm_back = lax.optimization_barrier((ffn_sum, d_norm_back))
     output = (resid + ffn_sum.astype(f32)).astype(bf16)
@@ -1220,15 +1273,25 @@
         n_mp,
         3,
         [shape_of(bf16, local_rows, model)]
-        + ([shape_of(f32, rows, width)] * 3 + [shape_of(f32, piece, little.shape[1])]) * fused,
+        + (
+            [shape_of(f32, rows, width)] * 3
+            + [shape_of(f32, piece, little.shape[1]), shape_of(f32, 2 * SUB, LANE)]
+        )
+        * fused,
         True,
         False,
         (inputs, d_resid, gain_f[0:1], d_norm_back)
-        + ((norm_group, back_group, d_cat, mixed, little) if fused else ()),
-        reduce_scratch(3, rows, width) + given_scratch(piece, little.shape[1]) if fused else (),
+        + ((norm_group, back_group, d_cat, mixed, little, gain_parts) if fused else ()),
+        reduce_scratch(3, rows, width)
+        + given_scratch(piece, little.shape[1])
+        + given_scratch(2 * SUB, LANE)
+        + [pltpu.VMEM((n_mp - 1, 2 * SUB, LANE), f32)]
+        + [pltpu.SemaphoreType.DMA((n_mp - 1,))] * 2
+        if fused
+        else (),
     )
     if fused:
-        *mix_grads, little_own = mix_grads
+        *mix_grads, little_own, gain_own = mix_grads
     else:
         mix_grads = [
             reduced(norm_group, d_cat[:, :width]),
@@ -1236,17 +1299,12 @@
             reduced(back_group, mixed),
         ]
         little_own = lax.psum_scatter(little, "dp", scatter_dimension=0, tiled=True)
+        gain_own = lax.psum(lax.psum_scatter(gain_parts, "dp", scatter_dimension=0, tiled=True), "mp")
+    grad_gains = lax.dynamic_slice_in_dim(gain_own, 2 * lax.axis_index("mp"), 2, axis=0)[:, :share]
     lines_own = little_own[:, 2 * width : 2 * width + SUB * heads].reshape(piece, heads, SUB)
     lines_own = lines_own.transpose(2, 1, 0)
     grad_blocks = little_own[:, : 2 * width].reshape(piece, heads, 2, LANE).transpose(2, 1, 0, 3)
 
-    owners = n_dp * n_mp
-    gain_parts = jnp.concatenate([gain_in, gain_mid], axis=0).reshape(2, owners, -1).transpose(1, 0, 2)
-    gain_parts = jnp.pad(
-        gain_parts.reshape(owners, -1), ((0, 0), (0, SUB * LANE - 2 * model // owners))
-    ).reshape(-1, LANE)
-    gain_own = lax.psum_scatter(gain_parts, ("dp", "mp"), scatter_dimension=0, tiled=True)
-    grad_gains = gain_own.reshape(-1)[: 2 * model // owners].reshape(2, -1)
     return (
         output,
         grad_inputs,

time: 778 us -> 638 us (0.82)
  waiting for transfers between devices: 216 us -> 2.13 us
  Pallas kernels: 515 us -> 589 us
    unnamed x7 -> x4, waiting for transfers between devices: 126 us -> 2.08 us
    pallas_call x4, Pallas kernels: 417 us -> 491 us  [line_call(): pl.pallas_call(functools.partial(body, n), out_shape=outs, in_specs=[whol...]
    reduce_scatter x1, waiting for transfers between devices: 63.2 us -> 0.01 us  [shards(): ffn_sum = lax.psum_scatter(ffn_part, 'mp', scatter_dimension=0, tiled=True)]
    all_gather x1, waiting for transfers between devices: 26.7 us -> 0.02 us  [shards(): full_down = lax.all_gather(down_rows, 'dp', axis=0, tiled=True)]
  transfers between devices with their start and end apart: 6 -> 4, of which waited for: 3 -> 0; matrix products, arithmetic and copies ran while one was open for 1% -> 2% of each run, Pallas kernels for 22% -> 74%
where the time goes in v4:
time: 638 us; the launch traced here: 632 us
  Pallas kernels  589 us (92%)
  local copies, waits for them, and re-layouts  18.6 us (3%)
  between operations  14.1 us (2%)
  other arithmetic  7.76 us (1%)
    pallas_call x4, Pallas kernels, line_call(): pl.pallas_call(functools.partial(body, n), out_shape=outs, in_specs=[whol...  491 us
    pallas_call x3, Pallas kernels, local_call(): pl.pallas_call(body, out_shape=outs, in_specs=[whole] * len(args), out_sp...  97.8 us
  transfers between devices with their start and end apart: 4, of which 0 were waited for; matrix products, arithmetic and copies ran while one was open for 2% of the time, Pallas kernels for 74%

profile of v4, /device:TPU:0, one launch (start us, length us, event | category | flops | bytes accessed | tf_op | source)
XLA Modules:
  0.0 631.9 jit_solution(16838713562754118311)
XLA Ops:
  7.2 0.7 all-gather.4.cloned.1.call-update
  8.0 0.7 all-gather.6.cloned.1.call-update
  8.7 0.7 all-gather.8.cloned.1.call-update
  9.5 0.7 reduce
  10.4 1.0 reshape_reshape.8.ocol
  11.4 0.7 reshape_reshape.7.orow
  12.1 0.7 convert_element_type.16
  12.7 0.7 maximum_bitcast_fusion
  13.5 0.8 reduce-window_clone.1
  14.3 0.7 subtract_bitcast_fusion.1
  15.4 1.0 reshape.68.pos
  17.6 72.8 %shard_map.255 = (bf16[1088,1536]{1,0:T(8,128)(2,1)}, bf16[1536,512]{1,0:T(8,128)(2,1)}, bf16[1536,512]{1,0:T(8,128)(2,1)}, bf16[1536,512]{1,0:T(8,128)(2,1)}, b...) custom-call(bf16[272,1536]{1,0:T(8,128)(2,1)} %x.11, f32[1,1536]{1,0:T(1,128)} %get-tuple-element.119.gain, ...), custom_call_target="tpu_custom_call" | custom-call | bytes 147251200 | tf_op jit(solution)/shard_map/pallas_call | solution.py:1055
  90.4 1.0 broadcast_multiply_fusion.cot
  91.4 27.2 %shard_map.256 = (f32[1088,512]{1,0:T(8,128)}, f32[1088,512]{1,0:T(8,128)}, f32[1088,512]{1,0:T(8,128)}, f32[1088,512]{1,0:T(8,128)}, f32[1088,512]{1,0:T(8,128)...) custom-call(bf16[1088,1536]{1,0:T(8,128)(2,1)} %get-tuple-element.53.tokens.norm.rest_0_, ...), custom_call_target="tpu_custom_call" | custom-call | flops 8770289664 | bytes 26194784 | tf_op jit(solution)/shard_map/pallas_call | solution.py:1072
  118.5 159.7 %shard_map.257 = (f32[272,1536]{1,0:T(8,128)}, bf16[1088,1536]{1,0:T(8,128)(2,1)}, bf16[1088,1536]{1,0:T(8,128)(2,1)}) custom-call(bf16[272,1536]{1,0:T(8,128)(2,1)} %x.11, bf16[272,1536]{1,0:T(8,128)(2,1)} %broadcast_multiply_fusion.cot, f32[1,1536]{1,0:T(1,128)} %get-tuple-element.120.gain, bf16[1088,1536]{1,0:T(8,128)(2,1)} %get-tuple-element.59.part), custom_call_target="tpu_custom_call" | custom-call | bytes 501964800 | tf_op jit(solution)/shard_map/pallas_call | solution.py:1055
  278.3 37.9 %shard_map.258 = (bf16[1088,1536]{1,0:T(8,128)(2,1)}, bf16[1088,1536]{1,0:T(8,128)(2,1)}, bf16[1088,1152]{1,0:T(8,128)(2,1)}, bf16[1088,1152]{1,0:T(8,128)(2,1)}, bf16[1088,1152]{1,0:T(8,128)(2,1)}) custom-call(bf16[1088,1536]{1,0:T(8,128)(2,1)} %get-tuple-element.61.tokens.rest_0_, bf16[1088,1536]{1,0:T(8,128)(2,1)} %get-tuple-element.62.cot.rest_1_, ...), custom_call_target="tpu_custom_call" | custom-call | flops 23102226432 | bytes 31506432 | tf_op jit(solution)/shard_map/pallas_call | solution.py:1072
  316.2 176.4 %shard_map.259 = (f32[272,1536]{1,0:T(8,128)}, f32[1,1536]{1,0:T(1,128)}, bf16[1088,1536]{1,0:T(8,128)(2,1)}, f32[192,1152]{1,0:T(8,128)}, f32[192,1152]{1,0:T(8,128)}, /*index=5*/f32[192,1152]{1,0:T(8,128)}) custom-call(f32[272,1536]{1,0:T(8,128)} %get-tuple-element.60.resid, bf16[272,1536]{1,0:T(8,128)(2,1)} %broadcast_multiply_fusion.cot, ...), custom_call_target="tpu_custom_call" | custom-call | bytes 2006016000 | tf_op jit(solution)/shard_map/pallas_call | solution.py:1055
  492.6 32.8 %shard_map.260 = (bf16[1088,1024]{1,0:T(8,128)(2,1)}, bf16[1088,1536]{1,0:T(8,128)(2,1)}, f32[128,1152]{1,0:T(8,128)}, f32[1,1536]{1,0:T(1,128)}) custom-call(bf16[1088,1536]{1,0:T(8,128)(2,1)} %get-tuple-element.68.back.rest_1_, bf16[1088,1536]{1,0:T(8,128)(2,1)} %get-tuple-element.53.tokens.norm.rest_0_, s32[1088,1]{1,0:T(8,128)} %reshape_reshape.8.ocol, ...), custom_call_target="tpu_custom_call" | custom-call | flops 8770289664 | bytes 31253344 | tf_op jit(solution)/shard_map/pallas_call | solution.py:1072
  525.4 0.7 pad_maximum_fusion
  526.9 82.5 %shard_map.261 = (bf16[272,1536]{1,0:T(8,128)(2,1)}, f32[192,512]{1,0:T(8,128)}, f32[192,512]{1,0:T(8,128)}, f32[192,512]{1,0:T(8,128)}, f32[16,1152]{1,0:T(8,128)}, /*index=5*/f32[16,128]{1,0:T(8,128)}) custom-call(bf16[272,1536]{1,0:T(8,128)(2,1)} %x.11, f32[272,1536]{1,0:T(8,128)} %get-tuple-element.77.d_resid, f32[1,1536]{1,0:T(1,128)} %get-tuple-element.119.gain, ...), custom_call_target="tpu_custom_call" | custom-call | bytes 1653760000 | tf_op jit(solution)/shard_map/pallas_call | solution.py:1055
  609.4 0.7 slice.34
  610.8 0.8 slice.38
  611.6 2.2 add_convert_fusion
  615.1 0.6 copy.60
  615.8 1.2 constant_dynamic-slice_fusion
  617.0 2.1 copy.69
  619.1 1.8 copy.70
  621.0 0.7 copy.71
  621.7 0.7 copy.72
  622.5 0.9 copy.73
  623.4 0.9 copy.74
  624.3 0.9 copy.75
  (48 shorter events, 4.7 us)
Async XLA Ops:
  7.2 9.8 %copy-start.7 = (bf16[2,1536]{1,0:T(2,128)(2,1)S(1)}, bf16[2,1536]{1,0:T(2,128)(2,1)}, u32[]{:S(2)}) copy-start(bf16[2,1536]{1,0:T(2,128)(2,1)} %param.21) | copy-start | bytes 18436
  7.2 83.2 %copy-start.4 = (bf16[272,1536]{1,0:T(8,128)(2,1)S(1)}, bf16[272,1536]{1,0:T(8,128)(2,1)}, u32[]{:S(2)}) copy-start(bf16[272,1536]{1,0:T(8,128)(2,1)} %param.17) | copy-start | bytes 2506756
  7.2 271.1 %all-gather.4.cloned.1.call-start = ((), (), s32[]{:S(2)}) async-start(), calls=%async_computation.1 | async-start | bytes 3981312 | tf_op jit(solution)/shard_map/all_gather | solution.py:1115
  7.9 270.4 %all-gather.6.cloned.1.call-start = ((), (), s32[]{:S(2)}) async-start(), calls=%async_computation.2 | async-start | bytes 3981312 | tf_op jit(solution)/shard_map/all_gather | solution.py:1116
  8.7 269.6 %all-gather.8.cloned.1.call-start = ((), (), s32[]{:S(2)}) async-start(), calls=%async_computation.3 | async-start | bytes 3981312 | tf_op jit(solution)/shard_map/all_gather | solution.py:1117
  9.4 517.5 %reduce-scatter.2.cloned.1.call-start = ((), (), s32[]{:S(2)}) async-start(), calls=%async_computation.4 | async-start | bytes 4177920 | tf_op jit(solution)/shard_map/reduce_scatter | solution.py:1268
  492.6 32.8 %copy-start.8 = (f32[1,1536]{1,0:T(1,128)S(1)}, f32[1,1536]{1,0:T(1,128)}, u32[]{:S(2)}) copy-start(f32[1,1536]{1,0:T(1,128)} %get-tuple-element.83) | copy-start | bytes 18436
  526.9 84.7 %copy-start = (f32[272,1536]{1,0:T(8,128)S(1)}, f32[272,1536]{1,0:T(8,128)}, u32[]{:S(2)}) copy-start(f32[272,1536]{1,0:T(8,128)} %get-tuple-element.60.resid) | copy-start | bytes 5013508
  613.9 7.1 %copy-start.6 = (f32[192,512]{1,0:T(8,128)S(1)}, f32[192,512]{1,0:T(8,128)}, u32[]{:S(2)}) copy-start(f32[192,512]{1,0:T(8,128)} %get-tuple-element.138) | copy-start | bytes 1179652
  613.9 7.8 %copy-start.5 = (f32[192,512]{1,0:T(8,128)S(1)}, f32[192,512]{1,0:T(8,128)}, u32[]{:S(2)}) copy-start(f32[192,512]{1,0:T(8,128)} %get-tuple-element.88) | copy-start | bytes 1179652
  613.9 8.6 %copy-start.3 = (f32[192,1152]{1,0:T(8,128)S(1)}, f32[192,1152]{1,0:T(8,128)}, u32[]{:S(2)}) copy-start(f32[192,1152]{1,0:T(8,128)} %get-tuple-element.144) | copy-start | bytes 2654212
  619.1 4.3 copy-start.2
  621.7 2.6 copy-start.1
Sparse Core Ops, SparseCore 0:
  9.9 50.5 all-gather.3
  62.4 34.0 all-gather.5
  98.4 33.9 all-gather.7
  316.4 111.3 reduce-scatter.1

commit v5 on v4

--- a/solution.py
+++ b/solution.py
@@ -185,7 +185,7 @@
 
 
 def ffn(
-    tokens, cot, w_up, w_gate, w_down, part_ref, dnorm_ref, hidden_ref, dup_ref, dgate_ref
+    tokens, cot, w_up, w_gate, w_down, dnorm_ref, hidden_ref, dup_ref, dgate_ref
 ):
     def block(b, carry):
         at = rows_of(b, ROWS)
@@ -199,7 +199,6 @@
         dup_ref[at, :] = d_up
         dgate_ref[at, :] = d_gate
         dnorm_ref[at, :] = (dot_last(d_up, w_up[...]) + dot_last(d_gate, w_gate[...])).astype(bf16)
-        part_ref[at, :] = dot_last(hidden, w_down[...]).astype(bf16)
         return carry
 
     lax.fori_loop(0, tokens.shape[0] // ROWS, block, 0)
@@ -392,7 +391,9 @@
 
 MESH = pl.DeviceIdType.MESH
 TILE = 16
-PIECES = 4
+PIECES = 8
+HOP = 1
+AFTER = 1
 
 
 def cut_rows(rows, parts):
@@ -522,28 +523,26 @@
                             self.all_copy(way, owner, k).wait_send()
 
     def run(self, point, tasks=()):
+        sums, alls = self.part is not None, self.whole is not None
+        slots = [[] for _ in range(PIECES + (HOP + AFTER) * (self.n - 1) + 1)]
+        for k in range(PIECES):
+            done = k + HOP * (self.n - 1) if sums else 0
+            if sums:
+                slots[k].append((0, functools.partial(self.first, k)))
+                for stage in range(1, self.n - 1):
+                    slots[k + HOP * stage].append((2, functools.partial(self.relay, k, stage)))
+            slots[done].append((3, functools.partial(point, k)))
+            if alls:
+                slots[done].append((4, functools.partial(self.spread, k)))
+                for stage in range(1, self.n):
+                    at = (done if sums else k) + AFTER * stage
+                    slots[at].append((1, functools.partial(self.forward, k, stage)))
         tasks = iter(tasks)
-        sums, alls = self.part is not None, self.whole is not None
-        if sums:
-            self.first(0)
-        else:
-            for k in range(PIECES):
-                point(k)
-                self.spread(k)
-        for step in range(PIECES + (1 if alls and sums else 0)):
-            gathered = step - 1 if sums else step
-            if sums and alls and step > 0:
-                self.spread(gathered)
-            if sums and step + 1 < PIECES:
-                self.first(step + 1)
-            for stage in range(1, self.n):
-                next(tasks, idle)()
-                if alls and gathered >= 0:
-                    self.forward(gathered, stage)
-                if sums and step < PIECES and stage < self.n - 1:
-                    self.relay(step, stage)
-            if sums and step < PIECES:
-                point(step)
+        for slot in slots:
+            for step, (_, work) in enumerate(sorted(slot, key=lambda entry: entry[0])):
+                if step in (0, 3):
+                    next(tasks, idle)()
+                work()
         for task in tasks:
             task()
         self.finish()
@@ -566,9 +565,21 @@
     pass
 
 
-def all_of(tasks):
-    for task in tasks:
-        task()
+class Late:
+    def __init__(self, source, ref, sem):
+        self.ref = ref
+        self.copy = pltpu.make_async_copy(source, ref, sem)
+        self.pending = True
+        self.copy.start()
+
+    def ready(self):
+        if self.pending:
+            self.copy.wait()
+        self.pending = False
+
+
+def late_all(sources, refs, sems):
+    return [Late(source, ref, sems.at[i]) for i, (source, ref) in enumerate(zip(sources, refs))]
 
 
 class Plane:
@@ -606,10 +617,11 @@
 
 
 class Reduce(Plane):
-    def __init__(self, index, left, right, lanes, mine, theirs, got, second, third, out, sems):
+    def __init__(self, index, left, right, lanes, sent, mine, theirs, got, second, third, out, sems):
         super().__init__()
+        self.sent, self.theirs = sent, theirs
         self.index, self.left, self.right, self.lanes = index, left, right, lanes
-        self.mine, self.theirs, self.got = mine.at[index], theirs.at[index], got.at[index]
+        self.mine, self.got = mine.at[index], got.at[index]
         self.second, self.third, self.out = second.at[index], third.at[index], out
         self.sems = sems
         self.rows = out.shape[0]
@@ -626,7 +638,7 @@
         )
 
     def core_copy(self, t):
-        return self.copy(self.theirs.at[t], self.got.at[t], t, 1)
+        return self.copy(self.theirs.at[(4 * self.index + t) % 2], self.got.at[t], t, 1)
 
     def second_copy(self, half, j):
         x, y = self.bit(2), self.bit(4)
@@ -646,11 +658,17 @@
         def task():
             core = self.bit(1)
             pair = pl.ds(t * 2 * self.rows, 2 * self.rows)
-            both = dot_first(self.left[:, pair], self.right[:, self.lanes])
+            if t == 0:
+                self.left.ready()
+                self.right.ready()
+            if len(self.sent) > 1:
+                self.sent[-2].wait_send()
+            both = dot_first(self.left.ref[:, pair], self.right.ref[:, self.lanes])
             low, high = both[: self.rows], both[self.rows :]
             self.mine[t] = jnp.where(core == 0, low, high).astype(bf16)
-            self.theirs[t] = jnp.where(core == 0, high, low).astype(bf16)
-            self.core_copy(t).start()
+            self.theirs[(4 * self.index + t) % 2] = jnp.where(core == 0, high, low).astype(bf16)
+            self.sent.append(self.core_copy(t))
+            self.sent[-1].start()
 
         return task
 
@@ -690,8 +708,6 @@
             )
 
     def finish(self):
-        for t in range(4):
-            self.core_copy(t).wait_send()
         for half in range(2):
             for j in range(2):
                 self.second_copy(half, j).wait_send()
@@ -700,7 +716,7 @@
 
 class Given(Reduce):
     def __init__(self, given, mine, got, second, third, out, sems):
-        super().__init__(0, None, None, None, mine, mine, got, second, third, out, sems)
+        super().__init__(0, None, None, None, None, mine, None, got, second, third, out, sems)
         self.given = given
 
     def rows_of(self, t, core):
@@ -712,6 +728,11 @@
     def start(self):
         for t in range(4):
             self.core_copy(t).start()
+
+    def finish(self):
+        for t in range(4):
+            self.core_copy(t).wait_send()
+        super().finish()
 
     def keep(self, t):
         return self.given[self.rows_of(t, self.bit(1)), :]
@@ -743,10 +764,12 @@
         also(6, part.add_third)
 
     def finish():
+        for copy in parts[0].sent[-2:]:
+            copy.wait_send()
         for part in [*parts, *given]:
             part.finish()
 
-    return tasks + [finish]
+    return tasks, finish
 
 
 def given_scratch(rows, width):
@@ -766,7 +789,7 @@
     sem = pltpu.SemaphoreType.DMA((arrays, 10))
     return [
         block,
-        block,
+        pltpu.VMEM((2, rows, width), bf16),
         block,
         pltpu.VMEM((arrays, 2, 2, rows // 2, width), bf16),
         pltpu.VMEM((arrays, 2, rows // 2, width), bf16),
@@ -787,6 +810,42 @@
         line.tiles(k, one)
 
     line.run(point)
+
+
+def row_view(array, rows):
+    def view(owner, half):
+        first = owner * rows + half * (rows // 2)
+        return array.at[pl.ds(pl.multiple_of(first, TILE), rows // 2)]
+
+    return view
+
+
+def gather_tasks(plane, items, sems):
+    def copies(stage):
+        return [
+            copy
+            for item, (view, halves) in enumerate(items)
+            for copy in plane.gather_copies(item, view, halves, stage, sems)
+        ]
+
+    def stage_task(stage):
+        def task():
+            if stage:
+                for copy in copies(stage - 1):
+                    copy.wait_recv()
+            for copy in copies(stage):
+                copy.start()
+
+        return task
+
+    def last():
+        for copy in copies(2):
+            copy.wait_recv()
+        for stage in range(3):
+            for copy in copies(stage):
+                copy.wait_send()
+
+    return stage_task(0), stage_task(1), stage_task(2), last
 
 
 def gather_weights(
@@ -817,42 +876,19 @@
     rows, piece = w_in.shape[0], blocks.shape[1]
     lines = chan.shape[0]
 
-    def view_of(array):
-        def view(owner, half):
-            first = owner * rows + half * (rows // 2)
-            return array.at[pl.ds(pl.multiple_of(first, TILE), rows // 2)]
-
-        return view
-
     def blocks_view(owner, half):
         return all_blocks.at[:, pl.ds(pl.multiple_of(owner * piece, TILE), piece)]
 
     def chan_view(owner, half):
         return raw.at[pl.ds(pl.multiple_of(owner * lines, TILE), lines)]
 
-    items = [(view_of(array), (0, 1)) for array in (all_in, all_gate, all_out)]
+    items = [(row_view(array, rows), (0, 1)) for array in (all_in, all_gate, all_out)]
     items += [(blocks_view, (0,)), (chan_view, (1,))]
 
-    def copies(stage):
-        return [
-            copy
-            for item, (view, halves) in enumerate(items)
-            for copy in plane.gather_copies(item, view, halves, stage, sems)
-        ]
-
-    def stage_task(stage):
-        def task():
-            if stage:
-                for copy in copies(stage - 1):
-                    copy.wait_recv()
-            for copy in copies(stage):
-                copy.start()
-
-        return task
+    first, second, third, finish = gather_tasks(plane, items, sems)
 
     def last():
-        for copy in copies(2):
-            copy.wait_recv()
+        finish()
         lane = lax.broadcasted_iota(jnp.int32, (LANE, LANE), 1)
         row = lax.broadcasted_iota(jnp.int32, (LANE, LANE), 0)
         total = jnp.zeros((lines, LANE), f32)
@@ -870,9 +906,6 @@
             log_one_more = jnp.where(one_more == 1.0, small, jnp.log(one_more) * (small / rest))
             all_chan[SUB - 1 : SUB, lanes] = jnp.maximum(decay, 0.0) + log_one_more
             all_chan[SUB : 2 * SUB, lanes] = jnp.broadcast_to(sigmoid(decay), (SUB, LANE))
-        for stage in range(3):
-            for copy in copies(stage):
-                copy.wait_send()
 
     own = pl.ds(pl.multiple_of(plane.me * rows, TILE), rows)
     all_in[own, :] = w_in[...]
@@ -888,23 +921,30 @@
 
         line.tiles(k, one)
 
-    tasks = [idle, stage_task(1), idle, idle, stage_task(2), idle, idle, last]
-    stage_task(0)()
-    line.run(point, tasks)
-
-
-def sum_norm_gather(
-    n, x, cot, gain, part, resid, whole, cots, left, right, total, ss, sr, send, recv, cot_send, cot_recv
-):
+    first()
+    line.run(point, [idle] * 4 + [second] + [idle] * 3 + [third] + [idle] * 3 + [last])
+
+
+def sum_norm_gather(n, x, gain, part, *rest):
+    if len(rest) > 9:
+        shares, rest = rest[:3], rest[3:]
+        resid, whole, *alls = rest[:5]
+        left, right, total, ss, sr, send, recv, plane_send, plane_recv = rest[5:]
+        plane = Plane()
+    else:
+        resid, whole, left, right, total, ss, sr, send, recv = rest
+        plane = None
     line = Line(n, x.shape[0], part, (left, right), whole, (ss, sr), (send, recv))
-    other = Line(n, x.shape[0], None, None, cots, None, (cot_send, cot_recv))
-    line.greet()
-
-    def keep(_, own, at):
-        cots[at, :] = cot[own, :]
-
-    for k in range(PIECES):
-        other.tiles(k, keep)
+    line.greet(plane)
+    tasks = []
+    if plane is not None:
+        rows = shares[0].shape[0]
+        own = pl.ds(pl.multiple_of(plane.me * rows, TILE), rows)
+        for share, array in zip(shares, alls):
+            array[own, :] = share[...]
+        items = [(row_view(array, rows), (0, 1)) for array in alls]
+        first, second, third, last = gather_tasks(plane, items, (plane_send, plane_recv))
+        tasks = [first] + [idle] * 5 + [second] + [idle] * 9 + [third] + [idle] * 6 + [last]
 
     def point(k):
         line.total(k, total)
@@ -916,15 +956,7 @@
 
         line.tiles(k, one)
 
-    tasks = []
-    for k in range(PIECES):
-        for stage in range(n):
-            at = k * (n - 1) + stage
-            task = functools.partial(other.forward, k, stage) if stage else functools.partial(other.spread, k)
-            tasks += [[] for _ in range(at + 1 - len(tasks))]
-            tasks[at].append(task)
-    line.run(point, [functools.partial(all_of, group) for group in tasks])
-    other.finish()
+    line.run(point, tasks)
 
 
 def norm_back(value, gain, grad):
@@ -936,16 +968,15 @@
 
 def sum_back_gather(n, resid, cot, gain, part, *rest):
     if len(rest) > 10:
-        norm, cots, d_up, d_gate, hidden, *rest = rest
-        d_resid, gain_grad, whole, *outs = rest[:6]
-        left, right, total, ss, sr, send, recv, *reduce = rest[6:]
-        every = slice(None)
-        sides = ((norm, d_up, every), (norm, d_gate, every), (cots, hidden, every))
+        sources, rest = rest[:6], rest[6:]
+        d_resid, gain_grad, whole, ffn_part, *outs = rest[:7]
+        left, right, total, ss, sr, send, recv, *reduce = rest[7:]
+        reduce, refs, late_sems = reduce[:7], reduce[7:13], reduce[13]
     else:
         d_resid, gain_grad, whole, left, right, total, ss, sr, send, recv = rest
-        sides = ()
+        sources = ()
     line = Line(n, resid.shape[0], part, (left, right), whole, (ss, sr), (send, recv))
-    line.greet(Plane() if sides else None)
+    line.greet(Plane() if sources else None)
     gain_grad[...] = jnp.zeros_like(gain_grad)
 
     def point(k):
@@ -960,39 +991,48 @@
 
         line.tiles(k, one)
 
-    if sides:
-        tasks = reduce_tasks(
-            [
-                Reduce(i, *side, *reduce[:5], out, reduce[5:])
-                for i, (side, out) in enumerate(zip(sides, outs))
-            ]
-        )
-        line.run(point, tasks)
-    else:
+    if not sources:
         line.run(point)
+        return
+    norm, cots, d_up, d_gate, hidden, w_down = late_all(sources, refs, late_sems)
+    sent = []
+    tasks, finish = reduce_tasks(
+        [
+            Reduce(i, *side, slice(None), sent, *reduce[:5], out, reduce[5:])
+            for i, (side, out) in enumerate(
+                zip(((norm, d_up), (norm, d_gate), (cots, hidden)), outs)
+            )
+        ]
+    )
+
+    def project(b):
+        w_down.ready()
+        at = pl.ds(b * ROWS, ROWS)
+        ffn_part[at, :] = dot_last(hidden.ref[at, :], w_down.ref[...]).astype(bf16)
+
+    for b in range(part.shape[0] // ROWS):
+        tasks.insert(12 + b, functools.partial(project, b))
+    line.run(point, tasks)
+    finish()
 
 
 def sum_back(n, x, d_resid, gain, part, *rest):
     if len(rest) > 6:
-        norm, back_all, cat, mixed, little, gains, *rest = rest
+        little, gains, *rest = rest
+        sources, rest = rest[:4], rest[4:]
         grad_x, *outs, little_out, gains_out = rest[:6]
         left, right, total, ss, sr, *reduce = rest[6:]
+        refs, late_sems = reduce[22:26], reduce[26]
         given = [
             Given(little, *reduce[7:11], little_out, reduce[11:13]),
             Given(gains, *reduce[13:17], gains_out, reduce[17:19]),
         ]
-        met, met_send, met_recv = reduce[19:]
-        width = mixed.shape[1]
-        sides = (
-            (norm, cat, slice(0, width)),
-            (norm, cat, slice(width, 2 * width)),
-            (back_all, mixed, slice(None)),
-        )
+        met, met_send, met_recv = reduce[19:22]
     else:
         grad_x, left, right, total, ss, sr = rest
-        sides = ()
+        sources = ()
     line = Line(n, x.shape[0], part, (left, right), None, (ss, sr), None)
-    line.greet(Plane() if sides else None)
+    line.greet(Plane() if sources else None)
 
     def point(k):
         line.total(k, total)
@@ -1003,43 +1043,52 @@
 
         line.tiles(k, one)
 
-    if sides:
-        tasks = reduce_tasks(
-            [
-                Reduce(i, *side, *reduce[:5], out, reduce[5:7])
-                for i, (side, out) in enumerate(zip(sides, outs))
-            ],
-            given,
+    if not sources:
+        line.run(point)
+        return
+    norm, back_all, cat, mixed = late_all(sources, refs, late_sems)
+    width = mixed.ref.shape[1]
+    sent = []
+    sides = (
+        (norm, cat, slice(0, width)),
+        (norm, cat, slice(width, 2 * width)),
+        (back_all, mixed, slice(None)),
+    )
+    tasks, finish = reduce_tasks(
+        [
+            Reduce(i, *side, sent, *reduce[:5], out, reduce[5:7])
+            for i, (side, out) in enumerate(zip(sides, outs))
+        ],
+        given,
+    )
+    me = lax.axis_index("mp")
+
+    def meet(away):
+        return pltpu.make_async_remote_copy(
+            src_ref=gains_out,
+            dst_ref=met.at[away - 1],
+            send_sem=met_send.at[away - 1],
+            recv_sem=met_recv.at[away - 1],
+            device_id={"mp": lax.rem(me + away, n)},
+            device_id_type=MESH,
         )
-        me = lax.axis_index("mp")
-
-        def meet(away):
-            return pltpu.make_async_remote_copy(
-                src_ref=gains_out,
-                dst_ref=met.at[away - 1],
-                send_sem=met_send.at[away - 1],
-                recv_sem=met_recv.at[away - 1],
-                device_id={"mp": lax.rem(me + away, n)},
-                device_id_type=MESH,
-            )
-
-        def send_gains():
-            for away in range(1, n):
-                meet(away).start()
-
-        def add_gains():
-            for away in range(1, n):
-                meet(away).wait()
-            gains_out[...] += sum(met[away] for away in range(n - 1))
-
-        tasks[7:7] = [send_gains]
-        tasks.append(add_gains)
-        line.run(point, tasks)
-    else:
-        line.run(point)
-
-
-def line_call(body, n, identity, outs, sums, alls, args, more=()):
+
+    def send_gains():
+        for away in range(1, n):
+            meet(away).start()
+
+    def add_gains():
+        for away in range(1, n):
+            meet(away).wait()
+        gains_out[...] += sum(met[away] for away in range(n - 1))
+
+    tasks[7:7] = [send_gains]
+    line.run(point, tasks)
+    finish()
+    add_gains()
+
+
+def line_call(body, n, identity, outs, sums, alls, args, more=(), late=0):
     whole = pl.BlockSpec(memory_space=pltpu.VMEM)
     local, model = args[0].shape
     sem = pltpu.SemaphoreType.DMA((2, n, PIECES))
@@ -1051,11 +1100,14 @@
     if alls:
         scratch += [sem, sem]
     scratch += more
+    if late:
+        scratch += [pltpu.VMEM(a.shape, a.dtype) for a in args[-late:]]
+        scratch += [pltpu.SemaphoreType.DMA((late,))]
     moved = sum(a.size * a.dtype.itemsize for a in args)
     return pl.pallas_call(
         functools.partial(body, n),
         out_shape=outs,
-        in_specs=[whole] * len(args),
+        in_specs=[whole] * (len(args) - late) + [pl.BlockSpec(memory_space=pl.ANY)] * late,
         out_specs=[whole] * len(outs),
         scratch_shapes=scratch,
         compiler_params=pltpu.CompilerParams(
@@ -1112,9 +1164,6 @@
     fused = n_dp == 8
     rows = model // n_dp
     out_rows, down_rows = w_out.T, w_down.T
-    full_up = lax.all_gather(w_up, "dp", axis=0, tiled=True)
-    full_gate_ff = lax.all_gather(w_gate_ff, "dp", axis=0, tiled=True)
-    full_down = lax.all_gather(down_rows, "dp", axis=0, tiled=True)
     lines = jnp.concatenate([conv_weight, chan_bias, decay[None]], axis=0).transpose(1, 0, 2)
     lines = lines.reshape(SUB * heads, piece)
 
@@ -1169,6 +1218,9 @@
         )
     cot = cotangent * token_mask.astype(bf16)[:, None]
 
+    cot_late, norm_group = lax.optimization_barrier((cot, norm_group))
+    cot_group = lax.all_gather(cot_late, "mp", axis=0, tiled=True)
+
     wide = pltpu.VMEM((count, width), f32)
     saved = [shape_of(f32, count, width)] * 6
     *kept, mixed, back_part = local_call(
@@ -1184,41 +1236,50 @@
         2 * count * (count * model + 3 * model * width),
         (norm_group, ocol, orow, pos_col, full_in, full_gate, full_out, chan, blocks),
     )
-    resid, norm_mid_group, cot_group = line_call(
+    shares = (w_up, w_gate_ff, down_rows)
+    resid, norm_mid_group, *ffn_weights = line_call(
         sum_norm_gather,
         n_mp,
         1,
-        [own, tok, tok],
+        [own, tok] + [shape_of(bf16, model, hidden_width)] * (3 * fused),
         True,
         True,
-        (inputs, cot, gain_f[1:2], back_part),
-        [pltpu.SemaphoreType.DMA((2, n_mp, PIECES))] * 2,
+        (inputs, gain_f[1:2], back_part) + (shares if fused else ()),
+        [pltpu.SemaphoreType.DMA((3, 2, 7))] * (2 * fused),
     )
+    if not fused:
+        ffn_weights = [lax.all_gather(share, "dp", axis=0, tiled=True) for share in shares]
+    full_up, full_gate_ff, full_down = ffn_weights
 
     hid = shape_of(bf16, count, hidden_width)
-    ffn_part, d_norm_part, hidden, d_up, d_gate_ff = local_call(
+    d_norm_part, hidden, d_up, d_gate_ff = local_call(
         ffn,
-        [tok, tok, hid, hid, hid],
+        [tok, hid, hid, hid],
         [],
-        12 * count * model * hidden_width,
+        10 * count * model * hidden_width,
         (norm_mid_group, cot_group, full_up, full_gate_ff, full_down),
     )
     d_resid, gain_mid, back_group, *ffn_grads = line_call(
         sum_back_gather,
         n_mp,
         2,
-        [own, shape_of(f32, 1, model), tok] + [shape_of(f32, rows, hidden_width)] * (3 * fused),
+        [own, shape_of(f32, 1, model), tok]
+        + ([tok] + [shape_of(f32, rows, hidden_width)] * 3) * fused,
         True,
         True,
         (resid, cot, gain_f[1:2], d_norm_part)
-        + ((norm_mid_group, cot_group, d_up, d_gate_ff, hidden) if fused else ()),
+        + ((norm_mid_group, cot_group, d_up, d_gate_ff, hidden, full_down) if fused else ()),
         reduce_scratch(3, rows, hidden_width) if fused else (),
+        6 * fused,
     )
     def reduced(left, right):
         grad = dot_first(left, right).astype(bf16)
         return lax.psum_scatter(grad, "dp", scatter_dimension=0, tiled=True).astype(f32)
 
-    if not fused:
+    if fused:
+        ffn_part, *ffn_grads = ffn_grads
+    else:
+        ffn_part = dot_last(hidden, full_down).astype(bf16)
         ffn_grads = [
             reduced(norm_mid_group, d_up),
             reduced(norm_mid_group, d_gate_ff),
@@ -1281,7 +1342,7 @@
         True,
         False,
         (inputs, d_resid, gain_f[0:1], d_norm_back)
-        + ((norm_group, back_group, d_cat, mixed, little, gain_parts) if fused else ()),
+        + ((little, gain_parts, norm_group, back_group, d_cat, mixed) if fused else ()),
         reduce_scratch(3, rows, width)
         + given_scratch(piece, little.shape[1])
         + given_scratch(2 * SUB, LANE)
@@ -1289,6 +1350,7 @@
         + [pltpu.SemaphoreType.DMA((n_mp - 1,))] * 2
         if fused
         else (),
+        4 * fused,
     )
     if fused:
         *mix_grads, little_own, gain_own = mix_grads

time: 638 us -> 575 us (0.901)
  Pallas kernels: 589 us -> 502 us
  waiting for transfers between devices: 2.13 us -> 26.8 us
    pallas_call x4, Pallas kernels: 491 us -> 406 us  [line_call(): pl.pallas_call(functools.partial(body, n), out_shape=outs, in_specs=[whol...]
    reduce_scatter x1, waiting for transfers between devices: 0.01 us -> 26.7 us  [shards(): ffn_sum = lax.psum_scatter(ffn_part, 'mp', scatter_dimension=0, tiled=True)]
  transfers between devices with their start and end apart: 4 -> 2, of which waited for: 0 -> 1; matrix products, arithmetic and copies ran while one was open for 2% -> 1% of each run, Pallas kernels for 74% -> 36%
where the time goes in v5:
time: 575 us; the launch traced here: 568 us
  Pallas kernels  502 us (87%)
  waiting for transfers between devices  26.8 us (5%)
  local copies, waits for them, and re-layouts  17.3 us (3%)
  between operations  14.7 us (3%)
  other arithmetic  7 us (1%)
    pallas_call x4, Pallas kernels, line_call(): pl.pallas_call(functools.partial(body, n), out_shape=outs, in_specs=[whol...  406 us
    pallas_call x3, Pallas kernels, local_call(): pl.pallas_call(body, out_shape=outs, in_specs=[whole] * len(args), out_sp...  96.1 us
    reduce_scatter x1, waiting for transfers between devices, shards(): ffn_sum = lax.psum_scatter(ffn_part, 'mp', scatter_dimension=0, tiled=True)  26.7 us
  transfers between devices with their start and end apart: 2, of which 1 were waited for; matrix products, arithmetic and copies ran while one was open for 1% of the time, Pallas kernels for 36%

profile of v5, /device:TPU:0, one launch (start us, length us, event | category | flops | bytes accessed | tf_op | source)
XLA Modules:
  0.0 568.0 jit_solution(8094259640334538246)
XLA Ops:
  7.2 1.4 fusion
  8.6 0.7 maximum_bitcast_fusion
  9.4 0.7 convert_element_type.17
  10.0 0.6 pad.9.chan
  10.6 2.2 broadcast_multiply_fusion.cot
  12.8 69.5 %shard_map.255 = (bf16[1088,1536]{1,0:T(8,128)(2,1)}, bf16[1536,512]{1,0:T(8,128)(2,1)}, bf16[1536,512]{1,0:T(8,128)(2,1)}, bf16[1536,512]{1,0:T(8,128)(2,1)}, b...) custom-call(bf16[272,1536]{1,0:T(8,128)(2,1)} %x.11, f32[1,1536]{1,0:T(1,128)} %get-tuple-element.127.gain, ...), custom_call_target="tpu_custom_call" | custom-call | bytes 147251200 | tf_op jit(solution)/shard_map/pallas_call | solution.py:1107
  82.7 1.0 reshape_reshape.8.ocol
  83.7 0.7 reshape_reshape.7.orow
  85.0 1.0 reshape.68.pos
  86.0 27.4 %shard_map.256 = (f32[1088,512]{1,0:T(8,128)}, f32[1088,512]{1,0:T(8,128)}, f32[1088,512]{1,0:T(8,128)}, f32[1088,512]{1,0:T(8,128)}, f32[1088,512]{1,0:T(8,128)...) custom-call(bf16[1088,1536]{1,0:T(8,128)(2,1)} %get-tuple-element.58.tokens.norm.rest_2_, ...), custom_call_target="tpu_custom_call" | custom-call | flops 8770289664 | bytes 26194784 | tf_op jit(solution)/shard_map/pallas_call | solution.py:1124
  113.3 142.1 %shard_map.257 = (f32[272,1536]{1,0:T(8,128)}, bf16[1088,1536]{1,0:T(8,128)(2,1)}, bf16[1536,1152]{1,0:T(8,128)(2,1)}, bf16[1536,1152]{1,0:T(8,128)(2,1)}, bf16[1536,1152]{1,0:T(8,128)(2,1)}) custom-call(bf16[272,1536]{1,0:T(8,128)(2,1)} %x.11, f32[1,1536]{1,0:T(1,128)} %get-tuple-element.128.gain, bf16[1088,1536]{1,0:T(8,128)(2,1)} %get-tuple-element.64.part, ...), custom_call_target="tpu_custom_call" | custom-call | bytes 551116800 | tf_op jit(solution)/shard_map/pallas_call | solution.py:1107
  255.4 35.3 %shard_map.258 = (bf16[1088,1536]{1,0:T(8,128)(2,1)}, bf16[1088,1152]{1,0:T(8,128)(2,1)}, bf16[1088,1152]{1,0:T(8,128)(2,1)}, bf16[1088,1152]{1,0:T(8,128)(2,1)}) custom-call(bf16[1088,1536]{1,0:T(8,128)(2,1)} %get-tuple-element.66.tokens.rest_0_, bf16[1088,1536]{1,0:T(8,128)(2,1)} %all-gather.2.cloned.1.call-done.cot.rest_1_, ...), custom_call_target="tpu_custom_call" | custom-call | flops 19251855360 | bytes 28164096 | tf_op jit(solution)/shard_map/pallas_call | solution.py:1124
  290.7 117.9 %shard_map.259 = (f32[272,1536]{1,0:T(8,128)}, f32[1,1536]{1,0:T(1,128)}, bf16[1088,1536]{1,0:T(8,128)(2,1)}, bf16[1088,1536]{1,0:T(8,128)(2,1)}, f32[192,1152]{...) custom-call(f32[272,1536]{1,0:T(8,128)} %get-tuple-element.65.resid, ...), custom_call_target="tpu_custom_call" | custom-call | bytes 2359910400 | tf_op jit(solution)/shard_map/pallas_call | solution.py:1107
  408.7 33.4 %shard_map.260 = (bf16[1088,1024]{1,0:T(8,128)(2,1)}, bf16[1088,1536]{1,0:T(8,128)(2,1)}, f32[128,1152]{1,0:T(8,128)}, f32[1,1536]{1,0:T(1,128)}) custom-call(bf16[1088,1536]{1,0:T(8,128)(2,1)} %get-tuple-element.76.back.rest_3_, bf16[1088,1536]{1,0:T(8,128)(2,1)} %get-tuple-element.58.tokens.norm.rest_2_, s32[1088,1]{1,0:T(8,128)} %reshape_reshape.8.ocol, ...), custom_call_target="tpu_custom_call" | custom-call | flops 8770289664 | bytes 31253344 | tf_op jit(solution)/shard_map/pallas_call | solution.py:1124
  442.1 0.7 pad_maximum_fusion
  443.0 0.6 pad.10
  443.6 26.7 %reduce-scatter.2.cloned.1.call-done = bf16[272,1536]{1,0:T(8,128)(2,1)} async-done(((bf16[1088,1536]{1,0:T(8,128)(2,1)}), bf16[272,1536]{1,0:T(8,128)(2,1)}) %reduce-scatter.2.cloned.1.call-update) | async-done | bytes 835600 | tf_op jit(solution)/shard_map/reduce_scatter | solution.py:1329
  470.4 76.6 %shard_map.261 = (bf16[272,1536]{1,0:T(8,128)(2,1)}, f32[192,512]{1,0:T(8,128)}, f32[192,512]{1,0:T(8,128)}, f32[192,512]{1,0:T(8,128)}, f32[16,1152]{1,0:T(8,128)}, /*index=5*/f32[16,128]{1,0:T(8,128)}) custom-call(bf16[272,1536]{1,0:T(8,128)(2,1)} %x.11, f32[272,1536]{1,0:T(8,128)} %get-tuple-element.85.d_resid, f32[1,1536]{1,0:T(1,128)} %get-tuple-element.127.gain, ...), custom_call_target="tpu_custom_call" | custom-call | bytes 1653760000 | tf_op jit(solution)/shard_map/pallas_call | solution.py:1107
  547.0 0.9 slice.38
  547.9 0.7 slice.34
  549.3 0.6 copy.60
  550.0 0.6 copy.56
  550.6 0.6 copy.57
  551.2 2.3 add_convert_fusion
  553.5 1.3 constant_dynamic-slice_fusion
  554.8 0.9 copy.69
  555.7 0.7 copy.70
  556.5 0.7 copy.71
  557.2 0.7 copy.72
  558.0 0.9 copy.73
  558.9 0.9 copy.74
  559.8 0.9 copy.75
  (46 shorter events, 1.8 us)
Async XLA Ops:
  7.2 75.3 %copy-start.9 = (s32[1,1088]{1,0:T(1,128)S(1)}, s32[1,1088]{1,0:T(1,128)}, u32[]{:S(2)}) copy-start(s32[1,1088]{1,0:T(1,128)} %param.19) | copy-start | bytes 13060
  7.2 248.3 %all-gather.2.cloned.1.call-start = ((), (), s32[]{:S(2)}) async-start(), calls=%async_computation.1 | async-start | bytes 4177920 | tf_op jit(solution)/shard_map/all_gather | solution.py:1222
  10.6 73.7 %copy-start.10 = (s32[1,4]{1,0:T(1,128)S(1)}, s32[1,4]{1,0:T(1,128)}, u32[]{:S(2)}) copy-start(s32[1,4]{1,0:T(1,128)} %param.20) | copy-start | bytes 52
  82.4 388.0 %reduce-scatter.2.cloned.1.call-start = ((), (), s32[]{:S(2)}) async-start(), calls=%async_computation.2 | async-start | bytes 4177920 | tf_op jit(solution)/shard_map/reduce_scatter | solution.py:1329
  408.7 33.4 %copy-start.8 = (f32[1,1536]{1,0:T(1,128)S(1)}, f32[1,1536]{1,0:T(1,128)}, u32[]{:S(2)}) copy-start(f32[1,1536]{1,0:T(1,128)} %get-tuple-element.89) | copy-start | bytes 18436
  470.4 80.8 %copy-start = (f32[272,1536]{1,0:T(8,128)S(1)}, f32[272,1536]{1,0:T(8,128)}, u32[]{:S(2)}) copy-start(f32[272,1536]{1,0:T(8,128)} %get-tuple-element.65.resid) | copy-start | bytes 5013508
  547.0 7.9 %copy-start.4 = (bf16[272,1536]{1,0:T(8,128)(2,1)S(1)}, bf16[272,1536]{1,0:T(8,128)(2,1)}, u32[]{:S(2)}) copy-start(bf16[272,1536]{1,0:T(8,128)(2,1)} %get-tuple-element.143) | copy-start | bytes 2506756
  551.2 4.6 copy-start.7
  551.2 5.3 copy-start.6
  553.5 3.8 copy-start.5
  553.5 4.5 copy-start.3
  555.7 3.2 copy-start.2
  557.2 2.6 copy-start.1
Sparse Core Ops, SparseCore 0:
  82.5 90.0 all-gather.1
  408.8 61.4 reduce-scatter.1

commit v6 on v5

--- a/solution.py
+++ b/solution.py
@@ -70,30 +70,15 @@
     return (places == order_row).astype(f32).astype(bf16)
 
 
-def mixer_forward(
-    tokens,
-    ocol,
-    orow,
-    pos,
-    w_in,
-    w_gate,
-    w_out,
-    chan,
-    blocks,
-    gate_ref,
-    branch_ref,
-    conv_ref,
-    gin_ref,
-    grec_ref,
-    state_ref,
-    mixed_ref,
-    out_ref,
-    packed,
-    rate,
-    prod,
-    before,
-    low,
-):
+def mixer_forward(tokens, ocol, orow, pos, w_in, w_gate, chan, blocks, w_out_far, *rest):
+    far, rest = rest[:8], rest[8:]
+    packed, rate, prod, before, low, w_out, *near, late_sem, held_sem = rest
+    gate_ref, branch_ref, conv_ref, gin_ref, grec_ref, state_ref, mixed_ref, out_ref = near
+    (late_out,) = late_all([w_out_far], [w_out], late_sem)
+    leaving = [
+        pltpu.make_async_copy(source, target, held_sem.at[i, 0])
+        for i, (source, target) in enumerate(zip(near, far))
+    ]
     count, _ = tokens.shape
     width = w_in.shape[1]
     steps = count // SUB
@@ -107,6 +92,8 @@
         return carry
 
     lax.fori_loop(0, count // ROWS, project, 0)
+    leaving[0].start()
+    leaving[1].start()
 
     for k in range(TAIL // SUB):
         last = branch_ref[pl.ds(count - TAIL + k * SUB, SUB), :]
@@ -145,6 +132,8 @@
         return carry
 
     lax.fori_loop(0, count // ROWS, gates, 0)
+    for copy in leaving[2:5]:
+        copy.start()
 
     def scan(i, carry):
         held, passed = carry
@@ -173,6 +162,8 @@
         return carry
 
     lax.fori_loop(0, steps // 2, finish, 0, unroll=2)
+    leaving[5].start()
+    late_out.ready()
 
     def leave(b, carry):
         at = rows_of(b, ROWS)
@@ -182,60 +173,58 @@
         return carry
 
     lax.fori_loop(0, count // ROWS, leave, 0)
-
-
-def ffn(
-    tokens, cot, w_up, w_gate, w_down, dnorm_ref, hidden_ref, dup_ref, dgate_ref
-):
+    for copy in leaving[6:]:
+        copy.start()
+    for copy in leaving:
+        copy.wait()
+
+
+def ffn(tokens, w_up, w_gate_far, cot_far, w_down_far, *rest):
+    far, rest = rest[:4], rest[4:]
+    w_gate, cot, w_down, *near, late_sem, held_sem = rest
+    dnorm_ref, hidden_ref, dup_ref, dgate_ref = near
+    late = late_all([w_gate_far, cot_far, w_down_far], [w_gate, cot, w_down], late_sem)
+    blocks_of = tokens.shape[0] // ROWS
+
+    def leaving(b):
+        at = rows_of(b, ROWS)
+        return [
+            pltpu.make_async_copy(source.at[at], target.at[at], held_sem.at[i, b])
+            for i, (source, target) in enumerate(zip(near, far))
+        ]
+
     def block(b, carry):
         at = rows_of(b, ROWS)
         up = dot(tokens[at, :], w_up[...])
+
+        @pl.when(b == 0)
+        def _():
+            for array in late:
+                array.copy.wait()
+
         value, slope = gelu_both(dot(tokens[at, :], w_gate[...]))
-        hidden = (value * up).astype(bf16)
-        hidden_ref[at, :] = hidden
+        hidden_ref[at, :] = (value * up).astype(bf16)
         d_hidden = dot(cot[at, :], w_down[...])
         d_up = (d_hidden * value).astype(bf16)
         d_gate = (d_hidden * up * slope).astype(bf16)
         dup_ref[at, :] = d_up
         dgate_ref[at, :] = d_gate
         dnorm_ref[at, :] = (dot_last(d_up, w_up[...]) + dot_last(d_gate, w_gate[...])).astype(bf16)
+        for copy in leaving(b):
+            copy.start()
         return carry
 
-    lax.fori_loop(0, tokens.shape[0] // ROWS, block, 0)
-
-
-def mixer_backward(
-    back,
-    norm,
-    ocol,
-    orow,
-    pos,
-    gain,
-    w_in,
-    w_gate,
-    w_out,
-    chan,
-    blocks,
-    gate_ref,
-    branch_ref,
-    conv_ref,
-    gin_ref,
-    grec_ref,
-    state_ref,
-    dcat_ref,
-    dnorm_ref,
-    little_ref,
-    dgain_ref,
-    dmix_arr,
-    dmix,
-    adj,
-    prod,
-    after,
-    before,
-    low,
-    small_ref,
-    dblocks_ref,
-):
+    lax.fori_loop(0, blocks_of, block, 0)
+    for b in range(blocks_of):
+        for copy in leaving(b):
+            copy.wait()
+
+
+def mixer_backward(back, w_out, ocol, orow, pos, gain, chan, blocks, *rest):
+    far, (dcat_ref, dnorm_ref, little_ref, dgain_ref), rest = rest[:9], rest[9:13], rest[13:]
+    dmix_arr, dmix, adj, prod, after, before, low, small_ref, dblocks_ref, *rest = rest
+    gate_ref, grec_ref, state_ref, conv_ref, gin_ref, branch_ref, norm, w_in, w_gate, late_sem = rest
+    late = late_all(far, rest[:9], late_sem)
     count, _ = back.shape
     width = w_in.shape[1]
     steps = count // SUB
@@ -248,6 +237,8 @@
         return carry
 
     lax.fori_loop(0, blocks_of, enter, 0)
+    for array in late[:3]:
+        array.ready()
 
     def pack(b, carry):
         at = rows_of(b, ROWS)
@@ -260,6 +251,8 @@
         return carry
 
     lax.fori_loop(0, blocks_of, pack, 0)
+    for array in late:
+        array.ready()
 
     def scan(i, carry):
         held, passed, following = carry
@@ -969,8 +962,8 @@
 def sum_back_gather(n, resid, cot, gain, part, *rest):
     if len(rest) > 10:
         sources, rest = rest[:6], rest[6:]
-        d_resid, gain_grad, whole, ffn_part, *outs = rest[:7]
-        left, right, total, ss, sr, send, recv, *reduce = rest[7:]
+        d_resid, gain_grad, whole, low_part, high_part, *outs = rest[:8]
+        left, right, total, ss, sr, send, recv, *reduce = rest[8:]
         reduce, refs, late_sems = reduce[:7], reduce[7:13], reduce[13]
     else:
         d_resid, gain_grad, whole, left, right, total, ss, sr, send, recv = rest
@@ -1008,7 +1001,9 @@
     def project(b):
         w_down.ready()
         at = pl.ds(b * ROWS, ROWS)
-        ffn_part[at, :] = dot_last(hidden.ref[at, :], w_down.ref[...]).astype(bf16)
+        value = dot_last(hidden.ref[at, :], w_down.ref[...]).astype(bf16)
+        low_part[at, :] = value[:, : value.shape[1] // 2]
+        high_part[at, :] = value[:, value.shape[1] // 2 :]
 
     for b in range(part.shape[0] // ROWS):
         tasks.insert(12 + b, functools.partial(project, b))
@@ -1117,15 +1112,61 @@
     )(*args)
 
 
-def local_call(body, outs, scratch, flops, args):
-    whole = pl.BlockSpec(memory_space=pltpu.VMEM)
+def finish(heads, piece, share, resid, low, high, gains, little, *rest):
+    count = (len(rest) - 6) // 2
+    sources, rest = rest[:count], rest[count:]
+    output, grad_gains, grad_conv, grad_bias, grad_decay, grad_blocks, *rest = rest
+    targets, sems = rest[:count], rest[count:]
+    copies = [
+        pltpu.make_async_copy(source, target, sems[0].at[i])
+        for i, (source, target) in enumerate(zip(sources, targets))
+    ]
+    for copy in copies:
+        copy.start()
+    half = low.shape[1]
+    output[:, :half] = (resid[:, :half] + low[...].astype(f32)).astype(bf16)
+    output[:, half:] = (resid[:, half:] + high[...].astype(f32)).astype(bf16)
+    for position in range(gains.shape[0] // 2):
+
+        @pl.when(lax.axis_index("mp") == position)
+        def _():
+            grad_gains[...] = gains[2 * position : 2 * position + 2, :share]
+
+    for h in range(heads):
+        for gate in range(2):
+            first = (2 * h + gate) * LANE
+            grad_blocks[gate, h] = little[:, first : first + LANE]
+    first = 2 * heads * LANE
+    lines = little[:, first : first + LANE]
+    lines = jnp.concatenate([lines, jnp.zeros((LANE - piece, LANE), f32)], axis=0).T
+    for h in range(heads):
+        for k in range(SUB):
+            row = lines[h * SUB + k : h * SUB + k + 1, :piece]
+            if k < 4:
+                grad_conv[k, h : h + 1, :] = row
+            elif k < SUB - 1:
+                grad_bias[k - 4, h : h + 1, :] = row
+            else:
+                grad_decay[h : h + 1, :] = row
+    for copy in copies:
+        copy.wait()
+
+
+def local_call(body, outs, scratch, flops, args, late=0, held=0, far=0):
+    whole, away = pl.BlockSpec(memory_space=pltpu.VMEM), pl.BlockSpec(memory_space=pl.ANY)
+    twins = list(args[len(args) - late :]) + list(outs[len(outs) - held :])
+    scratch = scratch + [pltpu.VMEM(a.shape, a.dtype) for a in twins]
+    if late:
+        scratch.append(pltpu.SemaphoreType.DMA((late,)))
+    if held:
+        scratch.append(pltpu.SemaphoreType.DMA((held, 4)))
     moved = sum(a.size * a.dtype.itemsize for a in args)
     moved += sum(o.size * o.dtype.itemsize for o in outs)
     return pl.pallas_call(
         body,
         out_shape=outs,
-        in_specs=[whole] * len(args),
-        out_specs=[whole] * len(outs),
+        in_specs=[whole] * (len(args) - late - far) + [away] * (late + far),
+        out_specs=[whole] * (len(outs) - held - far) + [away] * (held + far),
         scratch_shapes=scratch,
         compiler_params=pltpu.CompilerParams(vmem_limit_bytes=VMEM_MB << 20),
         cost_estimate=pl.CostEstimate(flops=flops, bytes_accessed=moved, transcendentals=0),
@@ -1223,7 +1264,7 @@
 
     wide = pltpu.VMEM((count, width), f32)
     saved = [shape_of(f32, count, width)] * 6
-    *kept, mixed, back_part = local_call(
+    gate_pre, branch, conv, gate_in, gate_rec, state, mixed, back_part = local_call(
         mixer_forward,
         saved + [shape_of(bf16, count, width), shape_of(bf16, count, model)],
         [
@@ -1234,7 +1275,9 @@
             pltpu.VMEM((count, width), bf16),
         ],
         2 * count * (count * model + 3 * model * width),
-        (norm_group, ocol, orow, pos_col, full_in, full_gate, full_out, chan, blocks),
+        (norm_group, ocol, orow, pos_col, full_in, full_gate, chan, blocks, full_out),
+        1,
+        8,
     )
     shares = (w_up, w_gate_ff, down_rows)
     resid, norm_mid_group, *ffn_weights = line_call(
@@ -1257,14 +1300,16 @@
         [tok, hid, hid, hid],
         [],
         10 * count * model * hidden_width,
-        (norm_mid_group, cot_group, full_up, full_gate_ff, full_down),
+        (norm_mid_group, full_up, full_gate_ff, cot_group, full_down),
+        3,
+        4,
     )
     d_resid, gain_mid, back_group, *ffn_grads = line_call(
         sum_back_gather,
         n_mp,
         2,
         [own, shape_of(f32, 1, model), tok]
-        + ([tok] + [shape_of(f32, rows, hidden_width)] * 3) * fused,
+        + ([shape_of(bf16, count, model // 2)] * 2 + [shape_of(f32, rows, hidden_width)] * 3) * fused,
         True,
         True,
         (resid, cot, gain_f[1:2], d_norm_part)
@@ -1277,14 +1322,12 @@
         return lax.psum_scatter(grad, "dp", scatter_dimension=0, tiled=True).astype(f32)
 
     if fused:
-        ffn_part, *ffn_grads = ffn_grads
+        *ffn_parts, up_grad, gate_ff_grad, down_grad = ffn_grads
     else:
-        ffn_part = dot_last(hidden, full_down).astype(bf16)
-        ffn_grads = [
-            reduced(norm_mid_group, d_up),
-            reduced(norm_mid_group, d_gate_ff),
-            reduced(cot_group, hidden),
-        ]
+        ffn_parts = jnp.split(dot_last(hidden, full_down).astype(bf16), 2, axis=1)
+        up_grad = reduced(norm_mid_group, d_up)
+        gate_ff_grad = reduced(norm_mid_group, d_gate_ff)
+        down_grad = reduced(cot_group, hidden)
 
     d_cat, d_norm_back, little, gain_in = local_call(
         mixer_backward,
@@ -1308,27 +1351,34 @@
         2 * count * (3 * count * width + 3 * model * width),
         (
             back_group,
-            norm_group,
+            full_out,
             ocol,
             orow,
             pos_col,
             gain_f[0:1],
+            chan,
+            blocks,
+            gate_pre,
+            gate_rec,
+            state,
+            conv,
+            gate_in,
+            branch,
+            norm_group,
             full_in,
             full_gate,
-            full_out,
-            chan,
-            blocks,
-            *kept,
         ),
+        9,
     )
     share = model // (n_dp * n_mp)
     gain_parts = jnp.concatenate([gain_in, gain_mid], axis=0).reshape(2, n_dp, n_mp, share)
     gain_parts = gain_parts.transpose(1, 2, 0, 3).reshape(n_dp, 2 * n_mp, share)
     gain_parts = jnp.pad(gain_parts, ((0, 0), (0, 2 * SUB - 2 * n_mp), (0, LANE - share)))
     gain_parts = gain_parts.reshape(2 * SUB * n_dp, LANE)
-    ffn_sum = lax.psum_scatter(ffn_part, "mp", scatter_dimension=0, tiled=True)
-    ffn_sum, d_norm_back = lax.optimization_barrier((ffn_sum, d_norm_back))
-    output = (resid + ffn_sum.astype(f32)).astype(bf16)
+    ffn_low, ffn_high = (
+        lax.psum_scatter(part, "mp", scatter_dimension=0, tiled=True) for part in ffn_parts
+    )
+    ffn_low, d_norm_back = lax.optimization_barrier((ffn_low, d_norm_back))
     grad_inputs, *mix_grads = line_call(
         sum_back,
         n_mp,
@@ -1362,25 +1412,41 @@
         ]
         little_own = lax.psum_scatter(little, "dp", scatter_dimension=0, tiled=True)
         gain_own = lax.psum(lax.psum_scatter(gain_parts, "dp", scatter_dimension=0, tiled=True), "mp")
-    grad_gains = lax.dynamic_slice_in_dim(gain_own, 2 * lax.axis_index("mp"), 2, axis=0)[:, :share]
-    lines_own = little_own[:, 2 * width : 2 * width + SUB * heads].reshape(piece, heads, SUB)
-    lines_own = lines_own.transpose(2, 1, 0)
-    grad_blocks = little_own[:, : 2 * width].reshape(piece, heads, 2, LANE).transpose(2, 1, 0, 3)
-
+    outs = [
+        shape_of(bf16, local_rows, model),
+        shape_of(f32, 2, share),
+        shape_of(f32, 4, heads, piece),
+        shape_of(f32, 3, heads, piece),
+        shape_of(f32, heads, piece),
+        shape_of(f32, 2, heads, piece, LANE),
+    ]
+    copied = [grad_inputs, mix_grads[0], mix_grads[1], up_grad, gate_ff_grad] if fused else []
+    output, grad_gains, grad_conv, grad_bias, grad_decay, grad_blocks, *copied = local_call(
+        functools.partial(finish, heads, piece, share),
+        outs + [shape_of(a.dtype, *a.shape) for a in copied],
+        [pltpu.SemaphoreType.DMA((5,))] if fused else [],
+        0,
+        (resid, ffn_low, ffn_high, gain_own, little_own, *copied),
+        far=len(copied),
+    )
+    if fused:
+        grad_inputs, grad_in, grad_gate, up_grad, gate_ff_grad = copied
+    else:
+        grad_in, grad_gate, _ = mix_grads
     return (
         output,
         grad_inputs,
         grad_gains,
-        mix_grads[0],
-        mix_grads[1],
+        grad_in,
+        grad_gate,
         mix_grads[2].T,
-        lines_own[0:4],
-        lines_own[4:7],
-        lines_own[7],
+        grad_conv,
+        grad_bias,
+        grad_decay,
         grad_blocks,
-        ffn_grads[0],
-        ffn_grads[1],
-        ffn_grads[2].T,
+        up_grad,
+        gate_ff_grad,
+        down_grad.T,
     )
 
 

time: 575 us -> 669 us (1.16)
  Pallas kernels: 502 us -> 629 us
  waiting for transfers between devices: 26.8 us -> 5.77 us
  local copies, waits for them, and re-layouts: 17.3 us -> 7.49 us
    pallas_call x3 -> x4, Pallas kernels: 96.1 us -> 194 us  [local_call(): pl.pallas_call(body, out_shape=outs, in_specs=[whole] * (len(args) - late...]
    pallas_call x4, Pallas kernels: 406 us -> 435 us  [line_call(): pl.pallas_call(functools.partial(body, n), out_shape=outs, in_specs=[whol...]
    reduce_scatter x1 -> x2, waiting for transfers between devices: 26.7 us -> 5.04 us  [shards(): lax.psum_scatter(part, 'mp', scatter_dimension=0, tiled=True)]
  transfers between devices with their start and end apart: 2 -> 3, of which waited for: 1 -> 1; matrix products, arithmetic and copies ran while one was open for 1% -> 1% of each run, Pallas kernels for 36% -> 45%
where the time goes in v6:
time: 669 us; the launch traced here: 662 us
  Pallas kernels  629 us (94%)
  between operations  14.4 us (2%)
  local copies, waits for them, and re-layouts  7.49 us (1%)
    pallas_call x4, Pallas kernels, line_call(): pl.pallas_call(functools.partial(body, n), out_shape=outs, in_specs=[whol...  435 us
    pallas_call x4, Pallas kernels, local_call(): pl.pallas_call(body, out_shape=outs, in_specs=[whole] * (len(args) - late...  194 us
  transfers between devices with their start and end apart: 3, of which 1 were waited for; matrix products, arithmetic and copies ran while one was open for 1% of the time, Pallas kernels for 45%

profile of v6, /device:TPU:0, one launch (start us, length us, event | category | flops | bytes accessed | tf_op | source)
XLA Modules:
  0.0 661.8 jit_solution(3635566982499563469)
XLA Ops:
  7.2 0.7 convert_element_type.11
  7.9 0.7 maximum_bitcast_fusion
  8.7 1.4 fusion
  10.0 0.6 pad.9.chan
  10.6 2.2 broadcast_multiply_fusion.cot
  12.8 69.4 %shard_map.255 = (bf16[1088,1536]{1,0:T(8,128)(2,1)}, bf16[1536,512]{1,0:T(8,128)(2,1)}, bf16[1536,512]{1,0:T(8,128)(2,1)}, bf16[1536,512]{1,0:T(8,128)(2,1)}, b...) custom-call(bf16[272,1536]{1,0:T(8,128)(2,1)} %x.11, f32[1,1536]{1,0:T(1,128)} %get-tuple-element.125.gain, ...), custom_call_target="tpu_custom_call" | custom-call | bytes 147251200 | tf_op jit(solution)/shard_map/pallas_call | solution.py:1102
  82.3 0.0 reduce-scatter.3.cloned.1.call-start
  82.4 0.1 reshape_squeeze.3
  82.5 0.1 copy.41
  82.6 0.7 reshape_reshape.7.orow
  83.3 1.0 reshape_reshape.8.ocol
  84.3 0.2 reduce-window_clone.1
  84.5 0.1 select_reduce_fusion
  84.5 0.1 reduce_max.12
  84.7 0.1 select_add_fusion
  84.7 0.1 copy.42
  84.8 1.0 reshape.60.pos
  85.9 23.7 %shard_map.256 = (f32[1088,512]{1,0:T(8,128)}, f32[1088,512]{1,0:T(8,128)}, f32[1088,512]{1,0:T(8,128)}, f32[1088,512]{1,0:T(8,128)}, f32[1088,512]{1,0:T(8,128)...) custom-call(bf16[1088,1536]{1,0:T(8,128)(2,1)} %get-tuple-element.70.tokens.rest_6_.rest_2_, ...), custom_call_target="tpu_custom_call" | custom-call | flops 8770289664 | bytes 26194784 | tf_op jit(solution)/shard_map/pallas_call | solution.py:1165
  109.6 145.7 %shard_map.257 = (f32[272,1536]{1,0:T(8,128)}, bf16[1088,1536]{1,0:T(8,128)(2,1)}, bf16[1536,1152]{1,0:T(8,128)(2,1)}, bf16[1536,1152]{1,0:T(8,128)(2,1)}, bf16[1536,1152]{1,0:T(8,128)(2,1)}) custom-call(bf16[272,1536]{1,0:T(8,128)(2,1)} %x.11, f32[1,1536]{1,0:T(1,128)} %get-tuple-element.126.gain, bf16[1088,1536]{1,0:T(8,128)(2,1)} %get-tuple-element.76.part, ...), custom_call_target="tpu_custom_call" | custom-call | bytes 551116800 | tf_op jit(solution)/shard_map/pallas_call | solution.py:1102
  255.3 35.9 %shard_map.258 = (bf16[1088,1536]{1,0:T(8,128)(2,1)}, bf16[1088,1152]{1,0:T(8,128)(2,1)}, bf16[1088,1152]{1,0:T(8,128)(2,1)}, bf16[1088,1152]{1,0:T(8,128)(2,1)}) custom-call(bf16[1088,1536]{1,0:T(8,128)(2,1)} %get-tuple-element.78.tokens.rest_0_, bf16[1536,1152]{1,0:T(8,128)(2,1)} %get-tuple-element.79.w_up, ...), custom_call_target="tpu_custom_call" | custom-call | flops 19251855360 | bytes 28164096 | tf_op jit(solution)/shard_map/pallas_call | solution.py:1165
  291.2 117.7 %shard_map.259 = (f32[272,1536]{1,0:T(8,128)}, f32[1,1536]{1,0:T(1,128)}, bf16[1088,1536]{1,0:T(8,128)(2,1)}, bf16[1088,768]{1,0:T(8,128)(2,1)}, bf16[1088,768]{...) custom-call(f32[272,1536]{1,0:T(8,128)} %get-tuple-element.77.resid, ...), custom_call_target="tpu_custom_call" | custom-call | bytes 2359910400 | tf_op jit(solution)/shard_map/pallas_call | solution.py:1102
  408.9 0.0 reduce-scatter.5.cloned.1.call-start
  409.0 0.7 reduce-scatter.5.cloned.1.call-update
  409.7 28.0 %shard_map.260 = (bf16[1088,1024]{1,0:T(8,128)(2,1)}, bf16[1088,1536]{1,0:T(8,128)(2,1)}, f32[128,1152]{1,0:T(8,128)}, f32[1,1536]{1,0:T(1,128)}) custom-call(bf16[1088,1536]{1,0:T(8,128)(2,1)} %get-tuple-element.88.back.rest_3_, bf16[1536,512]{1,0:T(8,128)(2,1)} %get-tuple-element.75.w_out_far.w_out, s32[1088,1]{1,0:T(8,128)} %reshape_reshape.8.ocol, ...), custom_call_target="tpu_custom_call" | custom-call | flops 8770289664 | bytes 31253344 | tf_op jit(solution)/shard_map/pallas_call | solution.py:1165
  437.7 0.7 pad_maximum_fusion
  438.4 0.1 reshape.57
  438.6 0.6 pad.10
  439.2 5.0 reduce-scatter.3.cloned.1.call-done.low
  444.2 102.3 %shard_map.261 = (bf16[272,1536]{1,0:T(8,128)(2,1)}, f32[192,512]{1,0:T(8,128)}, f32[192,512]{1,0:T(8,128)}, f32[192,512]{1,0:T(8,128)}, f32[16,1152]{1,0:T(8,128)}, /*index=5*/f32[16,128]{1,0:T(8,128)}) custom-call(bf16[272,1536]{1,0:T(8,128)(2,1)} %x.11, f32[272,1536]{1,0:T(8,128)} %get-tuple-element.98.d_resid, f32[1,1536]{1,0:T(1,128)} %get-tuple-element.125.gain, ...), custom_call_target="tpu_custom_call" | custom-call | bytes 1653760000 | tf_op jit(solution)/shard_map/pallas_call | solution.py:1102
  546.6 106.6 %shard_map.262 = (bf16[272,1536]{1,0:T(8,128)(2,1)}, f32[2,48]{1,0:T(2,128)}, f32[4,4,16]{2,1,0:T(4,128)}, f32[3,4,16]{2,1,0:T(4,128)}, f32[4,16]{1,0:T(4,128)},...) custom-call(f32[272,1536]{1,0:T(8,128)} %get-tuple-element.77.resid,, ...), custom_call_target="tpu_custom_call" | custom-call | bytes 10275200 | tf_op jit(solution)/shard_map/pallas_call | solution.py:1165
  653.2 0.7 copy.52
  653.9 0.9 copy.53
  (21 shorter events, 0.2 us)
Async XLA Ops:
  7.2 75.2 %copy-start.3 = (s32[1,1088]{1,0:T(1,128)S(1)}, s32[1,1088]{1,0:T(1,128)}, u32[]{:S(2)}) copy-start(s32[1,1088]{1,0:T(1,128)} %param.19) | copy-start | bytes 13060
  7.2 248.1 %all-gather.2.cloned.1.call-start = ((), (), s32[]{:S(2)}) async-start(), calls=%async_computation.2 | async-start | bytes 4177920 | tf_op jit(solution)/shard_map/all_gather | solution.py:1263
  10.6 73.6 %copy-start.4 = (s32[1,4]{1,0:T(1,128)S(1)}, s32[1,4]{1,0:T(1,128)}, u32[]{:S(2)}) copy-start(s32[1,4]{1,0:T(1,128)} %param.20) | copy-start | bytes 52
  82.3 361.9 %reduce-scatter.3.cloned.1.call-start = ((), (), s32[]{:S(2)}) async-start(), calls=%async_computation.3 | async-start | bytes 2088960 | tf_op jit(solution)/shard_map/reduce_scatter | solution.py:1379
  408.9 137.6 %reduce-scatter.5.cloned.1.call-start = ((), (), s32[]{:S(2)}) async-start(), calls=%async_computation.4 | async-start | bytes 2088960 | tf_op jit(solution)/shard_map/reduce_scatter | solution.py:1379
  409.7 28.0 %copy-start.2 = (f32[1,1536]{1,0:T(1,128)S(1)}, f32[1,1536]{1,0:T(1,128)}, u32[]{:S(2)}) copy-start(f32[1,1536]{1,0:T(1,128)} %get-tuple-element.102) | copy-start | bytes 18436
  546.6 106.6 %copy-start.1 = (f32[192,512]{1,0:T(8,128)S(1)}, f32[192,512]{1,0:T(8,128)}, u32[]{:S(2)}) copy-start(f32[192,512]{1,0:T(8,128)} %get-tuple-element.117) | copy-start | bytes 1179652
  546.6 107.3 %copy-start = (f32[192,1152]{1,0:T(8,128)S(1)}, f32[192,1152]{1,0:T(8,128)}, u32[]{:S(2)}) copy-start(f32[192,1152]{1,0:T(8,128)} %get-tuple-element.124) | copy-start | bytes 2654212
Sparse Core Ops, SparseCore 0:
  82.4 93.5 all-gather.1
  409.1 35.1 reduce-scatter.2
  446.5 61.1 reduce-scatter.4

commit v7 on v6

--- a/solution.py
+++ b/solution.py
@@ -1115,14 +1115,9 @@
 def finish(heads, piece, share, resid, low, high, gains, little, *rest):
     count = (len(rest) - 6) // 2
     sources, rest = rest[:count], rest[count:]
-    output, grad_gains, grad_conv, grad_bias, grad_decay, grad_blocks, *rest = rest
-    targets, sems = rest[:count], rest[count:]
-    copies = [
-        pltpu.make_async_copy(source, target, sems[0].at[i])
-        for i, (source, target) in enumerate(zip(sources, targets))
-    ]
-    for copy in copies:
-        copy.start()
+    output, grad_gains, grad_conv, grad_bias, grad_decay, grad_blocks, *targets = rest
+    for source, target in zip(sources, targets):
+        target[...] = source[...]
     half = low.shape[1]
     output[:, :half] = (resid[:, :half] + low[...].astype(f32)).astype(bf16)
     output[:, half:] = (resid[:, half:] + high[...].astype(f32)).astype(bf16)
@@ -1148,11 +1143,9 @@
                 grad_bias[k - 4, h : h + 1, :] = row
             else:
                 grad_decay[h : h + 1, :] = row
-    for copy in copies:
-        copy.wait()
-
-
-def local_call(body, outs, scratch, flops, args, late=0, held=0, far=0):
+
+
+def local_call(body, outs, scratch, flops, args, late=0, held=0):
     whole, away = pl.BlockSpec(memory_space=pltpu.VMEM), pl.BlockSpec(memory_space=pl.ANY)
     twins = list(args[len(args) - late :]) + list(outs[len(outs) - held :])
     scratch = scratch + [pltpu.VMEM(a.shape, a.dtype) for a in twins]
@@ -1165,8 +1158,8 @@
     return pl.pallas_call(
         body,
         out_shape=outs,
-        in_specs=[whole] * (len(args) - late - far) + [away] * (late + far),
-        out_specs=[whole] * (len(outs) - held - far) + [away] * (held + far),
+        in_specs=[whole] * (len(args) - late) + [away] * late,
+        out_specs=[whole] * (len(outs) - held) + [away] * held,
         scratch_shapes=scratch,
         compiler_params=pltpu.CompilerParams(vmem_limit_bytes=VMEM_MB << 20),
         cost_estimate=pl.CostEstimate(flops=flops, bytes_accessed=moved, transcendentals=0),
@@ -1424,10 +1417,9 @@
     output, grad_gains, grad_conv, grad_bias, grad_decay, grad_blocks, *copied = local_call(
         functools.partial(finish, heads, piece, share),
         outs + [shape_of(a.dtype, *a.shape) for a in copied],
-        [pltpu.SemaphoreType.DMA((5,))] if fused else [],
+        [],
         0,
         (resid, ffn_low, ffn_high, gain_own, little_own, *copied),
-        far=len(copied),
     )
     if fused:
         grad_inputs, grad_in, grad_gate, up_grad, gate_ff_grad = copied

time: 669 us -> 567 us (0.85)
  Pallas kernels: 629 us -> 528 us
    pallas_call x4, Pallas kernels: 194 us -> 92.8 us  [local_call(): pl.pallas_call(body, out_shape=outs, in_specs=[whole] * (len(args) - late...]
  transfers between devices with their start and end apart: 3 -> 3, of which waited for: 1 -> 1; matrix products, arithmetic and copies ran while one was open for 1% -> 1% of each run, Pallas kernels for 45% -> 53%
where the time goes in v7:
time: 567 us; the launch traced here: 560 us
  Pallas kernels  528 us (93%)
  between operations  14.4 us (3%)
  local copies, waits for them, and re-layouts  7.49 us (1%)
  waiting for transfers between devices  5.77 us (1%)
    pallas_call x4, Pallas kernels, line_call(): pl.pallas_call(functools.partial(body, n), out_shape=outs, in_specs=[whol...  435 us
    pallas_call x4, Pallas kernels, local_call(): pl.pallas_call(body, out_shape=outs, in_specs=[whole] * (len(args) - late...  92.8 us
  transfers between devices with their start and end apart: 3, of which 1 were waited for; matrix products, arithmetic and copies ran while one was open for 1% of the time, Pallas kernels for 53%

profile of v7, /device:TPU:0, one launch (start us, length us, event | category | flops | bytes accessed | tf_op | source)
XLA Modules:
  0.0 560.5 jit_solution(14769506852078933213)
XLA Ops:
  7.2 0.7 convert_element_type.11
  7.9 0.7 maximum_bitcast_fusion
  8.7 1.4 fusion
  10.0 0.6 pad.9.chan
  10.6 2.2 broadcast_multiply_fusion.cot
  12.8 69.4 %shard_map.255 = (bf16[1088,1536]{1,0:T(8,128)(2,1)}, bf16[1536,512]{1,0:T(8,128)(2,1)}, bf16[1536,512]{1,0:T(8,128)(2,1)}, bf16[1536,512]{1,0:T(8,128)(2,1)}, b...) custom-call(bf16[272,1536]{1,0:T(8,128)(2,1)} %x.11, f32[1,1536]{1,0:T(1,128)} %get-tuple-element.125.gain, ...), custom_call_target="tpu_custom_call" | custom-call | bytes 147251200 | tf_op jit(solution)/shard_map/pallas_call | solution.py:1102
  82.3 0.0 reduce-scatter.3.cloned.1.call-start
  82.4 0.1 reshape_squeeze.3
  82.5 0.1 copy.41
  82.6 0.7 reshape_reshape.7.orow
  83.3 1.0 reshape_reshape.8.ocol
  84.3 0.2 reduce-window_clone.1
  84.5 0.1 select_reduce_fusion
  84.5 0.1 reduce_max.12
  84.7 0.1 select_add_fusion
  84.7 0.1 copy.42
  84.8 1.0 reshape.60.pos
  85.9 23.7 %shard_map.256 = (f32[1088,512]{1,0:T(8,128)}, f32[1088,512]{1,0:T(8,128)}, f32[1088,512]{1,0:T(8,128)}, f32[1088,512]{1,0:T(8,128)}, f32[1088,512]{1,0:T(8,128)...) custom-call(bf16[1088,1536]{1,0:T(8,128)(2,1)} %get-tuple-element.70.tokens.rest_6_.rest_2_, ...), custom_call_target="tpu_custom_call" | custom-call | flops 8770289664 | bytes 26194784 | tf_op jit(solution)/shard_map/pallas_call | solution.py:1158
  109.6 145.7 %shard_map.257 = (f32[272,1536]{1,0:T(8,128)}, bf16[1088,1536]{1,0:T(8,128)(2,1)}, bf16[1536,1152]{1,0:T(8,128)(2,1)}, bf16[1536,1152]{1,0:T(8,128)(2,1)}, bf16[1536,1152]{1,0:T(8,128)(2,1)}) custom-call(bf16[272,1536]{1,0:T(8,128)(2,1)} %x.11, f32[1,1536]{1,0:T(1,128)} %get-tuple-element.126.gain, bf16[1088,1536]{1,0:T(8,128)(2,1)} %get-tuple-element.76.part, ...), custom_call_target="tpu_custom_call" | custom-call | bytes 551116800 | tf_op jit(solution)/shard_map/pallas_call | solution.py:1102
  255.3 35.9 %shard_map.258 = (bf16[1088,1536]{1,0:T(8,128)(2,1)}, bf16[1088,1152]{1,0:T(8,128)(2,1)}, bf16[1088,1152]{1,0:T(8,128)(2,1)}, bf16[1088,1152]{1,0:T(8,128)(2,1)}) custom-call(bf16[1088,1536]{1,0:T(8,128)(2,1)} %get-tuple-element.78.tokens.rest_0_, bf16[1536,1152]{1,0:T(8,128)(2,1)} %get-tuple-element.79.w_up, ...), custom_call_target="tpu_custom_call" | custom-call | flops 19251855360 | bytes 28164096 | tf_op jit(solution)/shard_map/pallas_call | solution.py:1158
  291.2 117.7 %shard_map.259 = (f32[272,1536]{1,0:T(8,128)}, f32[1,1536]{1,0:T(1,128)}, bf16[1088,1536]{1,0:T(8,128)(2,1)}, bf16[1088,768]{1,0:T(8,128)(2,1)}, bf16[1088,768]{...) custom-call(f32[272,1536]{1,0:T(8,128)} %get-tuple-element.77.resid, ...), custom_call_target="tpu_custom_call" | custom-call | bytes 2359910400 | tf_op jit(solution)/shard_map/pallas_call | solution.py:1102
  408.9 0.0 reduce-scatter.5.cloned.1.call-start
  409.0 0.7 reduce-scatter.5.cloned.1.call-update
  409.7 28.0 %shard_map.260 = (bf16[1088,1024]{1,0:T(8,128)(2,1)}, bf16[1088,1536]{1,0:T(8,128)(2,1)}, f32[128,1152]{1,0:T(8,128)}, f32[1,1536]{1,0:T(1,128)}) custom-call(bf16[1088,1536]{1,0:T(8,128)(2,1)} %get-tuple-element.88.back.rest_3_, bf16[1536,512]{1,0:T(8,128)(2,1)} %get-tuple-element.75.w_out_far.w_out, s32[1088,1]{1,0:T(8,128)} %reshape_reshape.8.ocol, ...), custom_call_target="tpu_custom_call" | custom-call | flops 8770289664 | bytes 31253344 | tf_op jit(solution)/shard_map/pallas_call | solution.py:1158
  437.7 0.7 pad_maximum_fusion
  438.4 0.1 reshape.57
  438.6 0.6 pad.10
  439.2 5.0 reduce-scatter.3.cloned.1.call-done.low
  444.2 102.3 %shard_map.261 = (bf16[272,1536]{1,0:T(8,128)(2,1)}, f32[192,512]{1,0:T(8,128)}, f32[192,512]{1,0:T(8,128)}, f32[192,512]{1,0:T(8,128)}, f32[16,1152]{1,0:T(8,128)}, /*index=5*/f32[16,128]{1,0:T(8,128)}) custom-call(bf16[272,1536]{1,0:T(8,128)(2,1)} %x.11, f32[272,1536]{1,0:T(8,128)} %get-tuple-element.98.d_resid, f32[1,1536]{1,0:T(1,128)} %get-tuple-element.125.gain, ...), custom_call_target="tpu_custom_call" | custom-call | bytes 1653760000 | tf_op jit(solution)/shard_map/pallas_call | solution.py:1102
  546.6 5.2 shard_map.262
  551.8 0.7 copy.52
  552.6 0.9 copy.53
  (21 shorter events, 0.2 us)
Async XLA Ops:
  7.2 75.2 %copy-start.3 = (s32[1,1088]{1,0:T(1,128)S(1)}, s32[1,1088]{1,0:T(1,128)}, u32[]{:S(2)}) copy-start(s32[1,1088]{1,0:T(1,128)} %param.19) | copy-start | bytes 13060
  7.2 248.1 %all-gather.2.cloned.1.call-start = ((), (), s32[]{:S(2)}) async-start(), calls=%async_computation.2 | async-start | bytes 4177920 | tf_op jit(solution)/shard_map/all_gather | solution.py:1256
  10.6 73.6 %copy-start.4 = (s32[1,4]{1,0:T(1,128)S(1)}, s32[1,4]{1,0:T(1,128)}, u32[]{:S(2)}) copy-start(s32[1,4]{1,0:T(1,128)} %param.20) | copy-start | bytes 52
  82.3 361.9 %reduce-scatter.3.cloned.1.call-start = ((), (), s32[]{:S(2)}) async-start(), calls=%async_computation.3 | async-start | bytes 2088960 | tf_op jit(solution)/shard_map/reduce_scatter | solution.py:1372
  408.9 137.6 %reduce-scatter.5.cloned.1.call-start = ((), (), s32[]{:S(2)}) async-start(), calls=%async_computation.4 | async-start | bytes 2088960 | tf_op jit(solution)/shard_map/reduce_scatter | solution.py:1372
  409.7 28.0 %copy-start.2 = (f32[1,1536]{1,0:T(1,128)S(1)}, f32[1,1536]{1,0:T(1,128)}, u32[]{:S(2)}) copy-start(f32[1,1536]{1,0:T(1,128)} %get-tuple-element.102) | copy-start | bytes 18436
  546.6 5.3 copy-start.1
  546.6 6.0 %copy-start = (f32[192,1152]{1,0:T(8,128)S(1)}, f32[192,1152]{1,0:T(8,128)}, u32[]{:S(2)}) copy-start(f32[192,1152]{1,0:T(8,128)} %get-tuple-element.124) | copy-start | bytes 2654212
Sparse Core Ops, SparseCore 0:
  82.4 93.5 all-gather.1
  409.1 35.1 reduce-scatter.2
  446.5 61.1 reduce-scatter.4

commit v8 on v7

--- a/solution.py
+++ b/solution.py
@@ -177,47 +177,6 @@
         copy.start()
     for copy in leaving:
         copy.wait()
-
-
-def ffn(tokens, w_up, w_gate_far, cot_far, w_down_far, *rest):
-    far, rest = rest[:4], rest[4:]
-    w_gate, cot, w_down, *near, late_sem, held_sem = rest
-    dnorm_ref, hidden_ref, dup_ref, dgate_ref = near
-    late = late_all([w_gate_far, cot_far, w_down_far], [w_gate, cot, w_down], late_sem)
-    blocks_of = tokens.shape[0] // ROWS
-
-    def leaving(b):
-        at = rows_of(b, ROWS)
-        return [
-            pltpu.make_async_copy(source.at[at], target.at[at], held_sem.at[i, b])
-            for i, (source, target) in enumerate(zip(near, far))
-        ]
-
-    def block(b, carry):
-        at = rows_of(b, ROWS)
-        up = dot(tokens[at, :], w_up[...])
-
-        @pl.when(b == 0)
-        def _():
-            for array in late:
-                array.copy.wait()
-
-        value, slope = gelu_both(dot(tokens[at, :], w_gate[...]))
-        hidden_ref[at, :] = (value * up).astype(bf16)
-        d_hidden = dot(cot[at, :], w_down[...])
-        d_up = (d_hidden * value).astype(bf16)
-        d_gate = (d_hidden * up * slope).astype(bf16)
-        dup_ref[at, :] = d_up
-        dgate_ref[at, :] = d_gate
-        dnorm_ref[at, :] = (dot_last(d_up, w_up[...]) + dot_last(d_gate, w_gate[...])).astype(bf16)
-        for copy in leaving(b):
-            copy.start()
-        return carry
-
-    lax.fori_loop(0, blocks_of, block, 0)
-    for b in range(blocks_of):
-        for copy in leaving(b):
-            copy.wait()
 
 
 def mixer_backward(back, w_out, ocol, orow, pos, gain, chan, blocks, *rest):
@@ -498,16 +457,18 @@
             def _():
                 self.all_copy(way, owner, k).start()
 
+    def sent(self, k):
+        for owner in range(self.n):
+            for way in range(2):
+
+                @pl.when(self.me > owner if way else self.me < owner)
+                def _():
+                    self.sum_copy(way, owner, k).wait_send()
+
     def finish(self):
         for k in range(PIECES):
             for owner in range(self.n):
                 for way in range(2):
-                    if self.part is not None:
-
-                        @pl.when(self.me > owner if way else self.me < owner)
-                        def _():
-                            self.sum_copy(way, owner, k).wait_send()
-
                     if self.whole is not None:
                         reached = self.me <= owner if way else self.me >= owner
 
@@ -524,6 +485,7 @@
                 slots[k].append((0, functools.partial(self.first, k)))
                 for stage in range(1, self.n - 1):
                     slots[k + HOP * stage].append((2, functools.partial(self.relay, k, stage)))
+                slots[done].append((3, functools.partial(self.sent, k)))
             slots[done].append((3, functools.partial(point, k)))
             if alls:
                 slots[done].append((4, functools.partial(self.spread, k)))
@@ -563,6 +525,8 @@
         self.ref = ref
         self.copy = pltpu.make_async_copy(source, ref, sem)
         self.pending = True
+
+    def begin(self):
         self.copy.start()
 
     def ready(self):
@@ -572,7 +536,10 @@
 
 
 def late_all(sources, refs, sems):
-    return [Late(source, ref, sems.at[i]) for i, (source, ref) in enumerate(zip(sources, refs))]
+    arrays = [Late(source, ref, sems.at[i]) for i, (source, ref) in enumerate(zip(sources, refs))]
+    for array in arrays:
+        array.begin()
+    return arrays
 
 
 class Plane:
@@ -757,8 +724,9 @@
         also(6, part.add_third)
 
     def finish():
-        for copy in parts[0].sent[-2:]:
-            copy.wait_send()
+        for ring in {id(part.sent): part.sent for part in parts}.values():
+            for copy in ring[-2:]:
+                copy.wait_send()
         for part in [*parts, *given]:
             part.finish()
 
@@ -918,40 +886,6 @@
     line.run(point, [idle] * 4 + [second] + [idle] * 3 + [third] + [idle] * 3 + [last])
 
 
-def sum_norm_gather(n, x, gain, part, *rest):
-    if len(rest) > 9:
-        shares, rest = rest[:3], rest[3:]
-        resid, whole, *alls = rest[:5]
-        left, right, total, ss, sr, send, recv, plane_send, plane_recv = rest[5:]
-        plane = Plane()
-    else:
-        resid, whole, left, right, total, ss, sr, send, recv = rest
-        plane = None
-    line = Line(n, x.shape[0], part, (left, right), whole, (ss, sr), (send, recv))
-    line.greet(plane)
-    tasks = []
-    if plane is not None:
-        rows = shares[0].shape[0]
-        own = pl.ds(pl.multiple_of(plane.me * rows, TILE), rows)
-        for share, array in zip(shares, alls):
-            array[own, :] = share[...]
-        items = [(row_view(array, rows), (0, 1)) for array in alls]
-        first, second, third, last = gather_tasks(plane, items, (plane_send, plane_recv))
-        tasks = [first] + [idle] * 5 + [second] + [idle] * 9 + [third] + [idle] * 6 + [last]
-
-    def point(k):
-        line.total(k, total)
-
-        def one(here, own, at):
-            v = x[own, :].astype(f32) + total[here, :]
-            resid[own, :] = v
-            whole[at, :] = (v * rms_scale(v) * gain[...]).astype(bf16)
-
-        line.tiles(k, one)
-
-    line.run(point, tasks)
-
-
 def norm_back(value, gain, grad):
     scale = rms_scale(value)
     e = gain * grad
@@ -959,65 +893,154 @@
     return scale * e - value * slope, grad * value * scale
 
 
-def sum_back_gather(n, resid, cot, gain, part, *rest):
-    if len(rest) > 10:
-        sources, rest = rest[:6], rest[6:]
-        d_resid, gain_grad, whole, low_part, high_part, *outs = rest[:8]
-        left, right, total, ss, sr, send, recv, *reduce = rest[8:]
-        reduce, refs, late_sems = reduce[:7], reduce[7:13], reduce[13]
-    else:
-        d_resid, gain_grad, whole, left, right, total, ss, sr, send, recv = rest
-        sources = ()
-    line = Line(n, resid.shape[0], part, (left, right), whole, (ss, sr), (send, recv))
-    line.greet(Plane() if sources else None)
+def middle(n, x, gain, cot, part, *rest):
+    shares, (d_resid, gain_grad, back), far, rest = rest[:3], rest[3:6], rest[6:14], rest[14:]
+    left, right, total, ss, sr, send, recv, part2, ss2, sr2, send2, recv2, csend, crecv, *rest = rest
+    up_s, value_s, grad_s, *rest = rest
+    *rest, held_sem = rest
+    near, rest = rest[-8:], rest[:-8]
+    whole, cots, resid, hidden, d_up, d_gate, low_part, high_part = near
+    plane = Plane() if rest else None
+    w_up, w_gate, w_down = weights = rest[:3] if rest else shares
+    local = x.shape[0]
+    line = Line(n, local, part, (left, right), whole, (ss, sr), (send, recv))
+    back_line = Line(n, local, part2, (left, right), back, (ss2, sr2), (send2, recv2))
+    cot_line = Line(n, local, None, None, cots, None, (csend, crecv))
+    line.greet(plane)
     gain_grad[...] = jnp.zeros_like(gain_grad)
+    leaving = [
+        pltpu.make_async_copy(source, target, held_sem.at[i])
+        for i, (source, target) in enumerate(zip(near, far))
+    ]
+
+    def keep_cot(_, own, at):
+        cots[at, :] = cot[own, :]
 
     def point(k):
         line.total(k, total)
 
         def one(here, own, at):
-            back, terms = norm_back(resid[own, :], gain[...], total[here, :])
+            v = x[own, :].astype(f32) + total[here, :]
+            resid[own, :] = v
+            whole[at, :] = (v * rms_scale(v) * gain[...]).astype(bf16)
+
+        line.tiles(k, one)
+
+    def back_point(k):
+        back_line.total(k, total)
+
+        def one(here, own, at):
+            grad, terms = norm_back(resid[own, :], gain[...], total[here, :])
             gain_grad[...] += jnp.sum(terms, axis=0, keepdims=True)
-            value = cot[own, :].astype(f32) + back
+            value = cot[own, :].astype(f32) + grad
             d_resid[own, :] = value
-            whole[at, :] = value.astype(bf16)
+            back[at, :] = value.astype(bf16)
 
         line.tiles(k, one)
 
-    if not sources:
-        line.run(point)
-        return
-    norm, cots, d_up, d_gate, hidden, w_down = late_all(sources, refs, late_sems)
-    sent = []
-    tasks, finish = reduce_tasks(
-        [
-            Reduce(i, *side, slice(None), sent, *reduce[:5], out, reduce[5:])
-            for i, (side, out) in enumerate(
-                zip(((norm, d_up), (norm, d_gate), (cots, hidden)), outs)
-            )
-        ]
-    )
-
-    def project(b):
-        w_down.ready()
-        at = pl.ds(b * ROWS, ROWS)
-        value = dot_last(hidden.ref[at, :], w_down.ref[...]).astype(bf16)
-        low_part[at, :] = value[:, : value.shape[1] // 2]
-        high_part[at, :] = value[:, value.shape[1] // 2 :]
-
-    for b in range(part.shape[0] // ROWS):
-        tasks.insert(12 + b, functools.partial(project, b))
-    line.run(point, tasks)
-    finish()
+    def pair_steps(j):
+        first = line.pieces[2 * j][0]
+        rows = line.pieces[2 * j][1] + line.pieces[2 * j + 1][1]
+        at = [pl.ds(owner * local + first, rows) for owner in range(n)]
+        here = pl.ds(0, n * rows)
+
+        def read(array):
+            return jnp.concatenate([array[rows_at, :] for rows_at in at], axis=0)
+
+        def write(array, value):
+            for owner, rows_at in enumerate(at):
+                array[rows_at, :] = value[owner * rows : (owner + 1) * rows]
+
+        def up():
+            up_s[here, :] = dot(read(whole), w_up[...])
+
+        def gate():
+            value, slope = gelu_both(dot(read(whole), w_gate[...]))
+            write(hidden, (value * up_s[here, :]).astype(bf16))
+            value_s[here, :] = value
+            up_s[here, :] = up_s[here, :] * slope
+
+        def into_hidden():
+            d_hidden = dot(read(cots), w_down[...])
+            write(d_up, (d_hidden * value_s[here, :]).astype(bf16))
+            write(d_gate, (d_hidden * up_s[here, :]).astype(bf16))
+
+        def through_up():
+            grad_s[here, :] = dot_last(read(d_up), w_up[...])
+
+        def through_gate():
+            write(part2, (grad_s[here, :] + dot_last(read(d_gate), w_gate[...])).astype(bf16))
+
+        def project():
+            value = dot_last(read(hidden), w_down[...]).astype(bf16)
+            write(low_part, value[:, : value.shape[1] // 2])
+            write(high_part, value[:, value.shape[1] // 2 :])
+
+        return up, gate, into_hidden, through_up, through_gate, project
+
+    hops = n - 1
+    slots = [[] for _ in range(PIECES + 5 * hops)]
+
+    def put(slot, order, work, *args):
+        slots[slot].append((order, functools.partial(work, *args)))
+
+    for k in range(PIECES):
+        put(k, 0, line.first, k)
+        for stage in range(1, hops):
+            put(k + stage, 2, line.relay, k, stage)
+        met = k + hops
+        put(met, 3, line.sent, k)
+        put(met, 3, point, k)
+        put(met, 3, line.spread, k)
+        given = k if 2 * k < PIECES else min(2 * k - PIECES // 2 + 1, PIECES + 2)
+        put(given, 0, cot_line.tiles, k, keep_cot)
+        put(given, 0, cot_line.spread, k)
+        for stage in range(1, n):
+            put(met + stage, 1, line.forward, k, stage)
+            put(given + stage, 1, cot_line.forward, k, stage)
+    for j in range(PIECES // 2):
+        slot = 2 * j + 2 + 2 * hops
+        steps = pair_steps(j)
+        for at, order, step in zip((0, 0, 0, 1, 1, 1), (0.5, 1.5, 2.5, 0.5, 1.5, 3.5), steps):
+            put(slot + at, order, step)
+        for k in (2 * j, 2 * j + 1):
+            begun = slot + 1 + k % 2
+            put(begun, 2 if begun == slot + 1 else 0, back_line.first, k)
+            for stage in range(1, hops):
+                put(begun + stage, 2, back_line.relay, k, stage)
+            put(begun + hops, 3, back_line.sent, k)
+            put(begun + hops, 3, back_point, k)
+            put(begun + hops, 3, back_line.spread, k)
+            for stage in range(1, n):
+                put(begun + hops + stage, 1, back_line.forward, k, stage)
+    done = PIECES + 2 * hops + 2
+    for copy in leaving:
+        put(done, 0, copy.start)
+    if plane is not None:
+        rows = shares[0].shape[0]
+        own = pl.ds(pl.multiple_of(plane.me * rows, TILE), rows)
+        for share, array in zip(shares, weights):
+            array[own, :] = share[...]
+        items = [(row_view(array, rows), (0, 1)) for array in weights]
+        stages = gather_tasks(plane, items, rest[3:])
+        for slot, stage in zip((0, 3, 6, 2 * hops + 2), stages):
+            put(slot, 0, stage)
+    for slot in slots:
+        for _, work in sorted(slot, key=lambda entry: entry[0]):
+            work()
+    for each in (line, back_line, cot_line):
+        each.finish()
+    for copy in leaving:
+        copy.wait()
 
 
 def sum_back(n, x, d_resid, gain, part, *rest):
     if len(rest) > 6:
         little, gains, *rest = rest
-        sources, rest = rest[:4], rest[4:]
-        grad_x, *outs, little_out, gains_out = rest[:6]
-        left, right, total, ss, sr, *reduce = rest[6:]
-        refs, late_sems = reduce[22:26], reduce[26]
+        sources, rest = rest[:9], rest[9:]
+        grad_x, *outs, little_out, gains_out = rest[:9]
+        left, right, total, ss, sr, *reduce = rest[9:]
+        wide, late_refs, late_sems = reduce[22:29], reduce[29:34], reduce[34]
         given = [
             Given(little, *reduce[7:11], little_out, reduce[11:13]),
             Given(gains, *reduce[13:17], gains_out, reduce[17:19]),
@@ -1041,21 +1064,42 @@
     if not sources:
         line.run(point)
         return
-    norm, back_all, cat, mixed = late_all(sources, refs, late_sems)
-    width = mixed.ref.shape[1]
-    sent = []
+    left_a, left_b, right_a, right_b, right_c = late_refs
+    across, width = sources[7].shape[1], sources[8].shape[1]
+    places = (left_a, left_b, right_a, right_b, right_c)
+    places += (left_a, left_b, right_a.at[:, pl.ds(0, across)], right_c.at[:, pl.ds(0, width)])
+    mid, cots, d_up, d_gate, hidden, norm, back_all, cat, mixed = (
+        Late(source, ref, late_sems.at[i]) for i, (source, ref) in enumerate(zip(sources, places))
+    )
+    for array in (mid, d_up, d_gate, cots, hidden):
+        array.begin()
+    every, sent, sent_wide = slice(None), [], []
+    wide_sides = ((mid, d_up, every), (mid, d_gate, every), (cots, hidden, every))
     sides = (
         (norm, cat, slice(0, width)),
         (norm, cat, slice(width, 2 * width)),
-        (back_all, mixed, slice(None)),
+        (back_all, mixed, every),
     )
-    tasks, finish = reduce_tasks(
-        [
-            Reduce(i, *side, sent, *reduce[:5], out, reduce[5:7])
-            for i, (side, out) in enumerate(zip(sides, outs))
-        ],
-        given,
-    )
+    parts = [
+        Reduce(i, *side, sent_wide, *wide[:5], out, wide[5:7])
+        for i, (side, out) in enumerate(zip(wide_sides, outs))
+    ]
+    parts += [
+        Reduce(i, *side, sent, *reduce[:5], out, reduce[5:7])
+        for i, (side, out) in enumerate(zip(sides, outs[3:]))
+    ]
+    tasks, finish = reduce_tasks(parts, given)
+
+    def then(task, *arrays):
+        def both():
+            task()
+            for array in arrays:
+                array.begin()
+
+        return both
+
+    tasks[7] = then(tasks[7], norm, cat)
+    tasks[11] = then(tasks[11], back_all, mixed)
     me = lax.axis_index("mp")
 
     def meet(away):
@@ -1083,7 +1127,7 @@
     add_gains()
 
 
-def line_call(body, n, identity, outs, sums, alls, args, more=(), late=0):
+def line_call(body, n, identity, outs, sums, alls, args, more=(), late=0, held=0):
     whole = pl.BlockSpec(memory_space=pltpu.VMEM)
     local, model = args[0].shape
     sem = pltpu.SemaphoreType.DMA((2, n, PIECES))
@@ -1095,15 +1139,16 @@
     if alls:
         scratch += [sem, sem]
     scratch += more
-    if late:
-        scratch += [pltpu.VMEM(a.shape, a.dtype) for a in args[-late:]]
-        scratch += [pltpu.SemaphoreType.DMA((late,))]
+    if held:
+        scratch += [pltpu.VMEM(o.shape, o.dtype) for o in outs[len(outs) - held :]]
+        scratch += [pltpu.SemaphoreType.DMA((held,))]
+    away = pl.BlockSpec(memory_space=pl.ANY)
     moved = sum(a.size * a.dtype.itemsize for a in args)
     return pl.pallas_call(
         functools.partial(body, n),
         out_shape=outs,
-        in_specs=[whole] * (len(args) - late) + [pl.BlockSpec(memory_space=pl.ANY)] * late,
-        out_specs=[whole] * len(outs),
+        in_specs=[whole] * (len(args) - late) + [away] * late,
+        out_specs=[whole] * (len(outs) - held) + [away] * held,
         scratch_shapes=scratch,
         compiler_params=pltpu.CompilerParams(
             vmem_limit_bytes=VMEM_MB << 20, collective_id=identity, has_side_effects=True
@@ -1252,9 +1297,6 @@
         )
     cot = cotangent * token_mask.astype(bf16)[:, None]
 
-    cot_late, norm_group = lax.optimization_barrier((cot, norm_group))
-    cot_group = lax.all_gather(cot_late, "mp", axis=0, tiled=True)
-
     wide = pltpu.VMEM((count, width), f32)
     saved = [shape_of(f32, count, width)] * 6
     gate_pre, branch, conv, gate_in, gate_rec, state, mixed, back_part = local_call(
@@ -1273,54 +1315,44 @@
         8,
     )
     shares = (w_up, w_gate_ff, down_rows)
-    resid, norm_mid_group, *ffn_weights = line_call(
-        sum_norm_gather,
+    if not fused:
+        shares = [lax.all_gather(share, "dp", axis=0, tiled=True) for share in shares]
+    hid = shape_of(bf16, count, hidden_width)
+    half = shape_of(bf16, count, model // 2)
+    pieces = cut_rows(local_rows, PIECES)
+    most = n_mp * max(pieces[k][1] + pieces[k + 1][1] for k in range(0, PIECES, 2))
+    pair = pltpu.VMEM((most, hidden_width), f32)
+    flow = pltpu.SemaphoreType.DMA((2, n_mp, PIECES))
+    plane_scratch = [pltpu.VMEM((model, hidden_width), bf16)] * 3 + [pltpu.SemaphoreType.DMA((3, 2, 7))] * 2
+    (
+        d_resid,
+        gain_mid,
+        back_group,
+        norm_mid_group,
+        cot_group,
+        resid,
+        hidden,
+        d_up,
+        d_gate_ff,
+        *ffn_parts,
+    ) = line_call(
+        middle,
         n_mp,
         1,
-        [own, tok] + [shape_of(bf16, model, hidden_width)] * (3 * fused),
+        [own, shape_of(f32, 1, model), tok, tok, tok, own, hid, hid, hid, half, half],
         True,
         True,
-        (inputs, gain_f[1:2], back_part) + (shares if fused else ()),
-        [pltpu.SemaphoreType.DMA((3, 2, 7))] * (2 * fused),
+        (inputs, gain_f[1:2], cot, back_part, *shares),
+        [pltpu.VMEM((count, model), bf16)]
+        + [flow] * 6
+        + [pair, pair, pltpu.VMEM((most, model), f32)]
+        + plane_scratch * fused,
+        held=8,
     )
-    if not fused:
-        ffn_weights = [lax.all_gather(share, "dp", axis=0, tiled=True) for share in shares]
-    full_up, full_gate_ff, full_down = ffn_weights
-
-    hid = shape_of(bf16, count, hidden_width)
-    d_norm_part, hidden, d_up, d_gate_ff = local_call(
-        ffn,
-        [tok, hid, hid, hid],
-        [],
-        10 * count * model * hidden_width,
-        (norm_mid_group, full_up, full_gate_ff, cot_group, full_down),
-        3,
-        4,
-    )
-    d_resid, gain_mid, back_group, *ffn_grads = line_call(
-        sum_back_gather,
-        n_mp,
-        2,
-        [own, shape_of(f32, 1, model), tok]
-        + ([shape_of(bf16, count, model // 2)] * 2 + [shape_of(f32, rows, hidden_width)] * 3) * fused,
-        True,
-        True,
-        (resid, cot, gain_f[1:2], d_norm_part)
-        + ((norm_mid_group, cot_group, d_up, d_gate_ff, hidden, full_down) if fused else ()),
-        reduce_scratch(3, rows, hidden_width) if fused else (),
-        6 * fused,
-    )
+
     def reduced(left, right):
         grad = dot_first(left, right).astype(bf16)
         return lax.psum_scatter(grad, "dp", scatter_dimension=0, tiled=True).astype(f32)
-
-    if fused:
-        *ffn_parts, up_grad, gate_ff_grad, down_grad = ffn_grads
-    else:
-        ffn_parts = jnp.split(dot_last(hidden, full_down).astype(bf16), 2, axis=1)
-        up_grad = reduced(norm_mid_group, d_up)
-        gate_ff_grad = reduced(norm_mid_group, d_gate_ff)
-        down_grad = reduced(cot_group, hidden)
 
     d_cat, d_norm_back, little, gain_in = local_call(
         mixer_backward,
@@ -1378,26 +1410,50 @@
         3,
         [shape_of(bf16, local_rows, model)]
         + (
-            [shape_of(f32, rows, width)] * 3
+            [shape_of(f32, rows, hidden_width)] * 3
+            + [shape_of(f32, rows, width)] * 3
             + [shape_of(f32, piece, little.shape[1]), shape_of(f32, 2 * SUB, LANE)]
         )
         * fused,
         True,
         False,
         (inputs, d_resid, gain_f[0:1], d_norm_back)
-        + ((little, gain_parts, norm_group, back_group, d_cat, mixed) if fused else ()),
+        + (
+            (
+                little,
+                gain_parts,
+                norm_mid_group,
+                cot_group,
+                d_up,
+                d_gate_ff,
+                hidden,
+                norm_group,
+                back_group,
+                d_cat,
+                mixed,
+            )
+            if fused
+            else ()
+        ),
         reduce_scratch(3, rows, width)
         + given_scratch(piece, little.shape[1])
         + given_scratch(2 * SUB, LANE)
         + [pltpu.VMEM((n_mp - 1, 2 * SUB, LANE), f32)]
         + [pltpu.SemaphoreType.DMA((n_mp - 1,))] * 2
+        + reduce_scratch(3, rows, hidden_width)
+        + [pltpu.VMEM((count, model), bf16)] * 2
+        + [pltpu.VMEM((count, hidden_width), bf16)] * 3
+        + [pltpu.SemaphoreType.DMA((9,))]
         if fused
         else (),
-        4 * fused,
+        9 * fused,
     )
     if fused:
-        *mix_grads, little_own, gain_own = mix_grads
+        up_grad, gate_ff_grad, down_grad, *mix_grads, little_own, gain_own = mix_grads
     else:
+        up_grad = reduced(norm_mid_group, d_up)
+        gate_ff_grad = reduced(norm_mid_group, d_gate_ff)
+        down_grad = reduced(cot_group, hidden)
         mix_grads = [
             reduced(norm_group, d_cat[:, :width]),
             reduced(norm_group, d_cat[:, width:]),

time: 567 us -> 529 us (0.933)
  Pallas kernels: 528 us -> 484 us
    pallas_call x4 -> x3, Pallas kernels: 92.8 us -> 56.9 us  [local_call(): pl.pallas_call(body, out_shape=outs, in_specs=[whole] * (len(args) - late...]
    pallas_call x4 -> x3, Pallas kernels: 435 us -> 427 us  [line_call(): pl.pallas_call(functools.partial(body, n), out_shape=outs, in_specs=[whol...]
  transfers between devices with their start and end apart: 3 -> 2, of which waited for: 1 -> 1; matrix products, arithmetic and copies ran while one was open for 1% -> 0% of each run, Pallas kernels for 53% -> 30%
where the time goes in v8:
time: 529 us; the launch traced here: 520 us
  Pallas kernels  484 us (91%)
  between operations  14.7 us (3%)
  waiting for transfers between devices  7.88 us (1%)
  local copies, waits for them, and re-layouts  7.48 us (1%)
  other arithmetic  5.58 us (1%)
    pallas_call x3, Pallas kernels, line_call(): pl.pallas_call(functools.partial(body, n), out_shape=outs, in_specs=[whol...  427 us
    pallas_call x3, Pallas kernels, local_call(): pl.pallas_call(body, out_shape=outs, in_specs=[whole] * (len(args) - late...  56.9 us
  transfers between devices with their start and end apart: 2, of which 1 were waited for; matrix products, arithmetic and copies ran while one was open for 0% of the time, Pallas kernels for 30%

profile of v8, /device:TPU:0, one launch (start us, length us, event | category | flops | bytes accessed | tf_op | source)
XLA Modules:
  0.0 519.5 jit_solution(7780582561510626953)
XLA Ops:
  7.2 0.0 reduce-scatter.3.cloned.1.call-start
  7.2 0.8 reduce
  8.0 0.1 reshape_squeeze.3
  8.1 0.1 copy.41
  8.2 1.0 reshape_reshape.8.ocol
  9.2 0.7 reshape_reshape.7.orow
  9.9 1.4 fusion
  11.3 0.7 convert_element_type.11
  12.0 0.7 maximum_bitcast_fusion
  12.7 0.8 reduce-window_clone.1
  13.5 0.7 subtract_bitcast_fusion.1
  14.2 0.1 select_reduce_fusion
  14.3 0.1 reduce_max.12
  14.4 0.1 select_add_fusion
  14.5 0.1 copy.42
  14.6 1.0 reshape.60.pos
  15.6 1.0 broadcast_multiply_fusion.cot
  16.6 0.6 pad.9.chan
  17.2 69.4 %shard_map.255 = (bf16[1088,1536]{1,0:T(8,128)(2,1)}, bf16[1536,512]{1,0:T(8,128)(2,1)}, bf16[1536,512]{1,0:T(8,128)(2,1)}, bf16[1536,512]{1,0:T(8,128)(2,1)}, b...) custom-call(bf16[272,1536]{1,0:T(8,128)(2,1)} %x.11, f32[1,1536]{1,0:T(1,128)} %get-tuple-element.115.gain, ...), custom_call_target="tpu_custom_call" | custom-call | bytes 147251200 | tf_op jit(solution)/shard_map/pallas_call | solution.py:1147
  86.6 23.6 %shard_map.256 = (f32[1088,512]{1,0:T(8,128)}, f32[1088,512]{1,0:T(8,128)}, f32[1088,512]{1,0:T(8,128)}, f32[1088,512]{1,0:T(8,128)}, f32[1088,512]{1,0:T(8,128)...) custom-call(bf16[1088,1536]{1,0:T(8,128)(2,1)} %get-tuple-element.64.tokens.rest_6_.rest_7_, ...), custom_call_target="tpu_custom_call" | custom-call | flops 8770289664 | bytes 26194784 | tf_op jit(solution)/shard_map/pallas_call | solution.py:1203
  110.2 228.4 %shard_map.257 = (f32[272,1536]{1,0:T(8,128)}, f32[1,1536]{1,0:T(1,128)}, bf16[1088,1536]{1,0:T(8,128)(2,1)}, bf16[1088,1536]{1,0:T(8,128)(2,1)}, bf16[1088,1536...) custom-call(bf16[272,1536]{1,0:T(8,128)(2,1)} %x.11, ...), custom_call_target="tpu_custom_call" | custom-call | bytes 634675200 | tf_op jit(solution)/shard_map/pallas_call | solution.py:1147
  338.7 0.0 reduce-scatter.5.cloned.1.call-start
  338.7 0.7 reduce-scatter.5.cloned.1.call-update
  339.4 28.0 %shard_map.258 = (bf16[1088,1024]{1,0:T(8,128)(2,1)}, bf16[1088,1536]{1,0:T(8,128)(2,1)}, f32[128,1152]{1,0:T(8,128)}, f32[1,1536]{1,0:T(1,128)}) custom-call(bf16[1088,1536]{1,0:T(8,128)(2,1)} %get-tuple-element.73.back.rest_8_, bf16[1536,512]{1,0:T(8,128)(2,1)} %get-tuple-element.69.w_out_far.w_out, s32[1088,1]{1,0:T(8,128)} %reshape_reshape.8.ocol, ...), custom_call_target="tpu_custom_call" | custom-call | flops 8770289664 | bytes 31253344 | tf_op jit(solution)/shard_map/pallas_call | solution.py:1203
  367.5 0.7 pad_maximum_fusion
  368.2 0.1 reshape.57
  368.4 0.6 pad.10
  369.0 7.2 %reduce-scatter.3.cloned.1.call-done.low = bf16[272,768]{1,0:T(8,128)(2,1)} async-done(((bf16[1088,768]{1,0:T(8,128)(2,1)}), bf16[272,768]{1,0:T(8,128)(2,1)}) %reduce-scatter.3.cloned.1.call-update) | async-done | bytes 417808 | tf_op jit(solution)/shard_map/reduce_scatter | solution.py:1404
  376.1 129.1 %shard_map.259 = (bf16[272,1536]{1,0:T(8,128)(2,1)}, f32[192,1152]{1,0:T(8,128)}, f32[192,1152]{1,0:T(8,128)}, f32[192,1152]{1,0:T(8,128)}, f32[192,512]{1,0:T(8...) custom-call(bf16[272,1536]{1,0:T(8,128)(2,1)} %x.11, ...), custom_call_target="tpu_custom_call" | custom-call | bytes 3074252800 | tf_op jit(solution)/shard_map/pallas_call | solution.py:1147
  505.3 5.2 %shard_map.260 = (bf16[272,1536]{1,0:T(8,128)(2,1)}, f32[2,48]{1,0:T(2,128)}, f32[4,4,16]{2,1,0:T(4,128)}, f32[3,4,16]{2,1,0:T(4,128)}, f32[4,16]{1,0:T(4,128)},...) custom-call(f32[272,1536]{1,0:T(8,128)} %get-tuple-element.71.resid,, ...), custom_call_target="tpu_custom_call" | custom-call | bytes 10275200 | tf_op jit(solution)/shard_map/pallas_call | solution.py:1203
  510.6 0.7 copy.52
  511.3 0.9 copy.53
  (14 shorter events, 0.1 us)
Async XLA Ops:
  7.2 8.4 %copy-start.1 = (bf16[272,1536]{1,0:T(8,128)(2,1)S(1)}, bf16[272,1536]{1,0:T(8,128)(2,1)}, u32[]{:S(2)}) copy-start(bf16[272,1536]{1,0:T(8,128)(2,1)} %param.17) | copy-start | bytes 2506756
  7.2 369.0 %reduce-scatter.3.cloned.1.call-start = ((), (), s32[]{:S(2)}) async-start(), calls=%async_computation.2 | async-start | bytes 2088960 | tf_op jit(solution)/shard_map/reduce_scatter | solution.py:1404
  338.7 166.6 %reduce-scatter.5.cloned.1.call-start = ((), (), s32[]{:S(2)}) async-start(), calls=%async_computation.3 | async-start | bytes 2088960 | tf_op jit(solution)/shard_map/reduce_scatter | solution.py:1404
  339.4 28.1 %copy-start.3 = (f32[1,1536]{1,0:T(1,128)S(1)}, f32[1,1536]{1,0:T(1,128)}, u32[]{:S(2)}) copy-start(f32[1,1536]{1,0:T(1,128)} %get-tuple-element.87) | copy-start | bytes 18436
  505.3 5.3 %copy-start.2 = (f32[192,512]{1,0:T(8,128)S(1)}, f32[192,512]{1,0:T(8,128)}, u32[]{:S(2)}) copy-start(f32[192,512]{1,0:T(8,128)} %get-tuple-element.107) | copy-start | bytes 1179652
  505.3 6.0 %copy-start = (f32[192,1152]{1,0:T(8,128)S(1)}, f32[192,1152]{1,0:T(8,128)}, u32[]{:S(2)}) copy-start(f32[192,1152]{1,0:T(8,128)} %get-tuple-element.114) | copy-start | bytes 2654212
Sparse Core Ops, SparseCore 0:
  338.8 37.2 reduce-scatter.2
  378.5 61.1 reduce-scatter.4

commit v9 on v8

--- a/solution.py
+++ b/solution.py
@@ -495,7 +495,7 @@
         tasks = iter(tasks)
         for slot in slots:
             for step, (_, work) in enumerate(sorted(slot, key=lambda entry: entry[0])):
-                if step in (0, 3):
+                if step in (0, 1, 3):
                     next(tasks, idle)()
                 work()
         for task in tasks:
@@ -894,19 +894,25 @@
 
 
 def middle(n, x, gain, cot, part, *rest):
-    shares, (d_resid, gain_grad, back), far, rest = rest[:3], rest[3:6], rest[6:14], rest[14:]
+    (*shares, cot_first), rest = rest[:4], rest[4:]
+    (d_resid, gain_grad, back, high_sum), far, rest = rest[:4], rest[4:11], rest[11:]
     left, right, total, ss, sr, send, recv, part2, ss2, sr2, send2, recv2, csend, crecv, *rest = rest
-    up_s, value_s, grad_s, *rest = rest
+    up_s, value_s, grad_s, high_part, left3, right3, total3, ss3, sr3, cot_sem, *rest = rest
     *rest, held_sem = rest
-    near, rest = rest[-8:], rest[:-8]
-    whole, cots, resid, hidden, d_up, d_gate, low_part, high_part = near
+    near, rest = rest[-7:], rest[:-7]
+    whole, cots, resid, hidden, d_up, d_gate, low_part = near
     plane = Plane() if rest else None
     w_up, w_gate, w_down = weights = rest[:3] if rest else shares
     local = x.shape[0]
     line = Line(n, local, part, (left, right), whole, (ss, sr), (send, recv))
     back_line = Line(n, local, part2, (left, right), back, (ss2, sr2), (send2, recv2))
-    cot_line = Line(n, local, None, None, cots, None, (csend, crecv))
+    early = cot_first.shape[1]
+    later = pl.ds(early, cot.shape[1] - early)
+    cot_line = Line(n, local, None, None, cots.at[:, later], None, (csend, crecv))
+    high_line = Line(n, local, high_part, (left3, right3), None, (ss3, sr3), None)
     line.greet(plane)
+    arriving = pltpu.make_async_copy(cot_first, cots.at[:, pl.ds(0, early)], cot_sem)
+    arriving.start()
     gain_grad[...] = jnp.zeros_like(gain_grad)
     leaving = [
         pltpu.make_async_copy(source, target, held_sem.at[i])
@@ -914,7 +920,7 @@
     ]
 
     def keep_cot(_, own, at):
-        cots[at, :] = cot[own, :]
+        cots[at, later] = cot[own, later]
 
     def point(k):
         line.total(k, total)
@@ -937,6 +943,11 @@
             back[at, :] = value.astype(bf16)
 
         line.tiles(k, one)
+
+    def high_point(k):
+        high_line.total(k, total3)
+        first, rows = line.pieces[k]
+        high_sum[pl.ds(first, rows), :] = total3[pl.ds(0, rows), :].astype(bf16)
 
     def pair_steps(j):
         first = line.pieces[2 * j][0]
@@ -996,8 +1007,8 @@
         put(given, 0, cot_line.tiles, k, keep_cot)
         put(given, 0, cot_line.spread, k)
         for stage in range(1, n):
-            put(met + stage, 1, line.forward, k, stage)
-            put(given + stage, 1, cot_line.forward, k, stage)
+            put(met + stage, 5, line.forward, k, stage)
+            put(given + stage, 5, cot_line.forward, k, stage)
     for j in range(PIECES // 2):
         slot = 2 * j + 2 + 2 * hops
         steps = pair_steps(j)
@@ -1012,7 +1023,14 @@
             put(begun + hops, 3, back_point, k)
             put(begun + hops, 3, back_line.spread, k)
             for stage in range(1, n):
-                put(begun + hops + stage, 1, back_line.forward, k, stage)
+                put(begun + hops + stage, 5, back_line.forward, k, stage)
+            begun += 1
+            put(begun, 4, high_line.first, k)
+            for stage in range(1, hops):
+                put(begun + stage, 4, high_line.relay, k, stage)
+            put(begun + hops, 4, high_line.sent, k)
+            put(begun + hops, 4, high_point, k)
+    put(2 * hops + 2, 0, arriving.wait)
     done = PIECES + 2 * hops + 2
     for copy in leaving:
         put(done, 0, copy.start)
@@ -1297,6 +1315,9 @@
         )
     cot = cotangent * token_mask.astype(bf16)[:, None]
 
+    cot_first, norm_group = lax.optimization_barrier((cot[:, : model // 3], norm_group))
+    cot_first = lax.all_gather(cot_first, "mp", axis=0, tiled=True)
+
     wide = pltpu.VMEM((count, width), f32)
     saved = [shape_of(f32, count, width)] * 6
     gate_pre, branch, conv, gate_in, gate_rec, state, mixed, back_part = local_call(
@@ -1319,6 +1340,7 @@
         shares = [lax.all_gather(share, "dp", axis=0, tiled=True) for share in shares]
     hid = shape_of(bf16, count, hidden_width)
     half = shape_of(bf16, count, model // 2)
+    half_twin = pltpu.VMEM(half.shape, bf16)
     pieces = cut_rows(local_rows, PIECES)
     most = n_mp * max(pieces[k][1] + pieces[k + 1][1] for k in range(0, PIECES, 2))
     pair = pltpu.VMEM((most, hidden_width), f32)
@@ -1328,26 +1350,32 @@
         d_resid,
         gain_mid,
         back_group,
+        ffn_high,
         norm_mid_group,
         cot_group,
         resid,
         hidden,
         d_up,
         d_gate_ff,
-        *ffn_parts,
+        ffn_part,
     ) = line_call(
         middle,
         n_mp,
         1,
-        [own, shape_of(f32, 1, model), tok, tok, tok, own, hid, hid, hid, half, half],
+        [own, shape_of(f32, 1, model), tok, shape_of(bf16, local_rows, model // 2)]
+        + [tok, tok, own, hid, hid, hid, half],
         True,
         True,
-        (inputs, gain_f[1:2], cot, back_part, *shares),
+        (inputs, gain_f[1:2], cot, back_part, *shares, cot_first),
         [pltpu.VMEM((count, model), bf16)]
         + [flow] * 6
         + [pair, pair, pltpu.VMEM((most, model), f32)]
+        + [half_twin] * 3
+        + [pltpu.VMEM((max(rows for _, rows in pieces), model // 2), f32), flow, flow]
+        + [pltpu.SemaphoreType.DMA(())]
         + plane_scratch * fused,
-        held=8,
+        late=1,
+        held=7,
     )
 
     def reduced(left, right):
@@ -1400,9 +1428,7 @@
     gain_parts = gain_parts.transpose(1, 2, 0, 3).reshape(n_dp, 2 * n_mp, share)
     gain_parts = jnp.pad(gain_parts, ((0, 0), (0, 2 * SUB - 2 * n_mp), (0, LANE - share)))
     gain_parts = gain_parts.reshape(2 * SUB * n_dp, LANE)
-    ffn_low, ffn_high = (
-        lax.psum_scatter(part, "mp", scatter_dimension=0, tiled=True) for part in ffn_parts
-    )
+    ffn_low = lax.psum_scatter(ffn_part, "mp", scatter_dimension=0, tiled=True)
     ffn_low, d_norm_back = lax.optimization_barrier((ffn_low, d_norm_back))
     grad_inputs, *mix_grads = line_call(
         sum_back,

time: 529 us -> 479 us (0.905)
  Pallas kernels: 484 us -> 434 us
    pallas_call x3, Pallas kernels: 427 us -> 377 us  [line_call(): pl.pallas_call(functools.partial(body, n), out_shape=outs, in_specs=[whol...]
  transfers between devices with their start and end apart: 2 -> 2, of which waited for: 1 -> 2; matrix products, arithmetic and copies ran while one was open for 0% -> 1% of each run, Pallas kernels for 30% -> 11%
where the time goes in v9:
time: 479 us; the launch traced here: 470 us
  Pallas kernels  434 us (91%)
  between operations  14.7 us (3%)
  waiting for transfers between devices  9.56 us (2%)
  local copies, waits for them, and re-layouts  8.31 us (2%)
    pallas_call x3, Pallas kernels, line_call(): pl.pallas_call(functools.partial(body, n), out_shape=outs, in_specs=[whol...  377 us
    pallas_call x3, Pallas kernels, local_call(): pl.pallas_call(body, out_shape=outs, in_specs=[whole] * (len(args) - late...  56.9 us
  transfers between devices with their start and end apart: 2, of which 2 were waited for; matrix products, arithmetic and copies ran while one was open for 1% of the time, Pallas kernels for 11%

profile of v9, /device:TPU:0, one launch (start us, length us, event | category | flops | bytes accessed | tf_op | source)
XLA Modules:
  0.0 469.6 jit_solution(9458725259624105014)
XLA Ops:
  7.2 0.0 all-gather.2.cloned.1.call-start
  7.3 1.4 fusion
  8.6 0.7 convert_element_type.11
  9.3 1.3 broadcast_multiply_fusion.cot
  10.6 0.8 slice.19
  11.5 0.6 pad.9.chan
  12.1 69.1 %shard_map.255 = (bf16[1088,1536]{1,0:T(8,128)(2,1)}, bf16[1536,512]{1,0:T(8,128)(2,1)}, bf16[1536,512]{1,0:T(8,128)(2,1)}, bf16[1536,512]{1,0:T(8,128)(2,1)}, b...) custom-call(bf16[272,1536]{1,0:T(8,128)(2,1)} %x.11, f32[1,1536]{1,0:T(1,128)} %get-tuple-element.119.gain, ...), custom_call_target="tpu_custom_call" | custom-call | bytes 147251200 | tf_op jit(solution)/shard_map/pallas_call | solution.py:1165
  81.1 0.0 all-gather.2.cloned.1.call-update
  81.1 0.0 reduce-scatter.2.cloned.1.call-start
  81.2 0.1 reshape_squeeze.3
  81.3 0.1 copy.41
  81.4 1.0 reshape_reshape.8.ocol
  82.4 0.7 reshape_reshape.7.orow
  83.1 0.2 reduce-window_clone.1
  83.3 0.1 select_reduce_fusion
  83.4 0.1 reduce_max.12
  83.5 0.1 select_add_fusion
  83.6 0.1 copy.42
  83.7 1.0 reshape.60.pos
  84.7 23.6 %shard_map.256 = (f32[1088,512]{1,0:T(8,128)}, f32[1088,512]{1,0:T(8,128)}, f32[1088,512]{1,0:T(8,128)}, f32[1088,512]{1,0:T(8,128)}, f32[1088,512]{1,0:T(8,128)...) custom-call(bf16[1088,1536]{1,0:T(8,128)(2,1)} %get-tuple-element.67.tokens.rest_6_.rest_7_, ...), custom_call_target="tpu_custom_call" | custom-call | flops 8770289664 | bytes 26194784 | tf_op jit(solution)/shard_map/pallas_call | solution.py:1221
  108.3 2.0 all-gather.2.cloned.1.call-done.rest_3_
  110.3 216.3 %shard_map.257 = (f32[272,1536]{1,0:T(8,128)}, f32[1,1536]{1,0:T(1,128)}, bf16[1088,1536]{1,0:T(8,128)(2,1)}, bf16[272,768]{1,0:T(8,128)(2,1)}, bf16[1088,1536]{...) custom-call(bf16[272,1536]{1,0:T(8,128)(2,1)} %x.11, ...), custom_call_target="tpu_custom_call" | custom-call | bytes 746086400 | tf_op jit(solution)/shard_map/pallas_call | solution.py:1165
  326.7 0.0 reduce-scatter.2.cloned.1.call-update
  326.7 28.0 %shard_map.258 = (bf16[1088,1024]{1,0:T(8,128)(2,1)}, bf16[1088,1536]{1,0:T(8,128)(2,1)}, f32[128,1152]{1,0:T(8,128)}, f32[1,1536]{1,0:T(1,128)}) custom-call(bf16[1088,1536]{1,0:T(8,128)(2,1)} %get-tuple-element.77.back.rest_8_, bf16[1536,512]{1,0:T(8,128)(2,1)} %get-tuple-element.72.w_out_far.w_out, s32[1088,1]{1,0:T(8,128)} %reshape_reshape.8.ocol, ...), custom_call_target="tpu_custom_call" | custom-call | flops 8770289664 | bytes 31253344 | tf_op jit(solution)/shard_map/pallas_call | solution.py:1221
  354.8 0.7 pad_maximum_fusion
  355.5 0.1 reshape.57
  355.6 0.6 pad.10
  356.2 7.5 %reduce-scatter.2.cloned.1.call-done.low = bf16[272,768]{1,0:T(8,128)(2,1)} async-done(((bf16[1088,768]{1,0:T(8,128)(2,1)}), bf16[272,768]{1,0:T(8,128)(2,1)}) %reduce-scatter.2.cloned.1.call-update) | async-done | bytes 417808 | tf_op jit(solution)/shard_map/reduce_scatter | solution.py:1431
  363.8 91.6 %shard_map.259 = (bf16[272,1536]{1,0:T(8,128)(2,1)}, f32[192,1152]{1,0:T(8,128)}, f32[192,1152]{1,0:T(8,128)}, f32[192,1152]{1,0:T(8,128)}, f32[192,512]{1,0:T(8...) custom-call(bf16[272,1536]{1,0:T(8,128)(2,1)} %x.11, ...), custom_call_target="tpu_custom_call" | custom-call | bytes 3074252800 | tf_op jit(solution)/shard_map/pallas_call | solution.py:1165
  455.5 5.2 %shard_map.260 = (bf16[272,1536]{1,0:T(8,128)(2,1)}, f32[2,48]{1,0:T(2,128)}, f32[4,4,16]{2,1,0:T(4,128)}, f32[3,4,16]{2,1,0:T(4,128)}, f32[4,16]{1,0:T(4,128)},...) custom-call(f32[272,1536]{1,0:T(8,128)} %get-tuple-element.75.resid,, ...), custom_call_target="tpu_custom_call" | custom-call | bytes 10275200 | tf_op jit(solution)/shard_map/pallas_call | solution.py:1221
  460.7 0.7 copy.52
  461.5 0.9 copy.53
  (25 shorter events, 0.1 us)
Async XLA Ops:
  7.2 4.2 copy-start.7
  7.2 4.2 copy-start.6
  7.2 4.2 copy-start.5
  7.2 74.0 %copy-start.4 = (s32[1,1088]{1,0:T(1,128)S(1)}, s32[1,1088]{1,0:T(1,128)}, u32[]{:S(2)}) copy-start(s32[1,1088]{1,0:T(1,128)} %param.19) | copy-start | bytes 13060
  7.2 103.1 %all-gather.2.cloned.1.call-start = ((), (), s32[]{:S(2)}) async-start(), calls=%async_computation.1 | async-start | bytes 1392640 | tf_op jit(solution)/shard_map/all_gather | solution.py:1319
  9.3 73.8 %copy-start.8 = (s32[1,4]{1,0:T(1,128)S(1)}, s32[1,4]{1,0:T(1,128)}, u32[]{:S(2)}) copy-start(s32[1,4]{1,0:T(1,128)} %param.20) | copy-start | bytes 52
  10.6 97.7 %copy-start = (bf16[272,1536]{1,0:T(8,128)(2,1)}, bf16[272,1536]{1,0:T(8,128)(2,1)S(1)}, u32[]{:S(2)}) copy-start(bf16[272,1536]{1,0:T(8,128)(2,1)S(1)} %broadcast_multiply_fusion.cot) | copy-start | bytes 2506756
  81.1 282.6 %reduce-scatter.2.cloned.1.call-start = ((), (), s32[]{:S(2)}) async-start(), calls=%async_computation.2 | async-start | bytes 2088960 | tf_op jit(solution)/shard_map/reduce_scatter | solution.py:1431
  326.7 28.1 %copy-start.3 = (f32[1,1536]{1,0:T(1,128)S(1)}, f32[1,1536]{1,0:T(1,128)}, u32[]{:S(2)}) copy-start(f32[1,1536]{1,0:T(1,128)} %get-tuple-element.91) | copy-start | bytes 18436
  455.4 5.3 %copy-start.2 = (f32[192,512]{1,0:T(8,128)S(1)}, f32[192,512]{1,0:T(8,128)}, u32[]{:S(2)}) copy-start(f32[192,512]{1,0:T(8,128)} %get-tuple-element.111) | copy-start | bytes 1179652
  455.4 6.0 %copy-start.1 = (f32[192,1152]{1,0:T(8,128)S(1)}, f32[192,1152]{1,0:T(8,128)}, u32[]{:S(2)}) copy-start(f32[192,1152]{1,0:T(8,128)} %get-tuple-element.118) | copy-start | bytes 2654212
Sparse Core Ops, SparseCore 0:
  81.3 29.0 all-gather.1
  326.8 36.9 reduce-scatter.1

commit v10 on v9

--- a/solution.py
+++ b/solution.py
@@ -535,6 +535,14 @@
         self.pending = False
 
 
+class Here:
+    def __init__(self, ref):
+        self.ref = ref
+
+    def ready(self):
+        pass
+
+
 def late_all(sources, refs, sems):
     arrays = [Late(source, ref, sems.at[i]) for i, (source, ref) in enumerate(zip(sources, refs))]
     for array in arrays:
@@ -581,8 +589,8 @@
         super().__init__()
         self.sent, self.theirs = sent, theirs
         self.index, self.left, self.right, self.lanes = index, left, right, lanes
-        self.mine, self.got = mine.at[index], got.at[index]
-        self.second, self.third, self.out = second.at[index], third.at[index], out
+        self.mine, self.got = mine, got
+        self.second, self.third, self.out = second, third, out
         self.sems = sems
         self.rows = out.shape[0]
         self.half = self.rows // 2
@@ -604,7 +612,7 @@
         x, y = self.bit(2), self.bit(4)
         block = (1 - y) * 2 + j if half else j * 2 + 1 - x
         rows = self.mine.at[block, pl.ds(half * self.half, self.half)]
-        return self.copy(rows, self.second.at[half, j], 4 + 2 * half + j, 4 if half else 2)
+        return self.copy(rows, self.second(half, j), 4 + 2 * half + j, 4 if half else 2)
 
     def third_block(self, half):
         x, y = self.bit(2), self.bit(4)
@@ -612,7 +620,7 @@
 
     def third_copy(self, half):
         rows = self.mine.at[self.third_block(half), pl.ds(half * self.half, self.half)]
-        return self.copy(rows, self.third.at[half], 8 + half, 2 if half else 4)
+        return self.copy(rows, self.third(half), 8 + half, 2 if half else 4)
 
     def product(self, t):
         def task():
@@ -651,7 +659,7 @@
             block, at = self.third_block(half), pl.ds(half * self.half, self.half)
             far = 1 - self.bit(2 if half else 4)
             self.mine[block, at] = (
-                self.mine[block, at].astype(f32) + self.second[half, far].astype(f32)
+                self.mine[block, at].astype(f32) + self.second(half, far)[...].astype(f32)
             ).astype(self.mine.dtype)
             self.third_copy(half).start()
 
@@ -663,8 +671,8 @@
             near = self.bit(2 if half else 4)
             self.out[at, :] = (
                 self.mine[own, at].astype(f32)
-                + self.second[half, near].astype(f32)
-                + self.third[half].astype(f32)
+                + self.second(half, near)[...].astype(f32)
+                + self.third(half)[...].astype(f32)
             )
 
     def finish(self):
@@ -676,7 +684,7 @@
 
 class Given(Reduce):
     def __init__(self, given, mine, got, second, third, out, sems):
-        super().__init__(0, None, None, None, None, mine, None, got, second, third, out, sems)
+        super().__init__(0, None, None, None, None, *views(0, mine, None, got, second, third), out, sems)
         self.given = given
 
     def rows_of(self, t, core):
@@ -696,6 +704,31 @@
 
     def keep(self, t):
         return self.given[self.rows_of(t, self.bit(1)), :]
+
+
+def views(index, mine, theirs, got, second, third):
+    return (
+        mine.at[index],
+        theirs,
+        got.at[index],
+        lambda half, j: second.at[index, half, j],
+        lambda half: third.at[index, half],
+    )
+
+
+def blocks_views(index, both, spare):
+    half_rows = spare.shape[1] // 2
+
+    def halves(block, j):
+        return spare.at[block, pl.ds(pl.multiple_of(j * half_rows, TILE), half_rows)]
+
+    return (
+        both.at[pl.ds(0, 4)],
+        spare.at[pl.ds(6, 2)],
+        both.at[pl.ds(4, 4)],
+        lambda half, j: halves(3 * index + half, j),
+        lambda half: halves(3 * index + 2, half),
+    )
 
 
 def reduce_tasks(parts, given=()):
@@ -895,7 +928,9 @@
 
 def middle(n, x, gain, cot, part, *rest):
     (*shares, cot_first), rest = rest[:4], rest[4:]
-    (d_resid, gain_grad, back, high_sum), far, rest = rest[:4], rest[4:11], rest[11:]
+    grads = len(rest) > 45 and 2 or 0
+    (d_resid, gain_grad, back, high_sum), rest = rest[:4], rest[4:]
+    weight_grads, far, rest = rest[:grads], rest[grads : grads + 7], rest[grads + 7 :]
     left, right, total, ss, sr, send, recv, part2, ss2, sr2, send2, recv2, csend, crecv, *rest = rest
     up_s, value_s, grad_s, high_part, left3, right3, total3, ss3, sr3, cot_sem, *rest = rest
     *rest, held_sem = rest
@@ -903,6 +938,10 @@
     whole, cots, resid, hidden, d_up, d_gate, low_part = near
     plane = Plane() if rest else None
     w_up, w_gate, w_down = weights = rest[:3] if rest else shares
+
+    def whole_of(weight):
+        return weight[...].reshape(-1, weight.shape[-1])
+
     local = x.shape[0]
     line = Line(n, local, part, (left, right), whole, (ss, sr), (send, recv))
     back_line = Line(n, local, part2, (left, right), back, (ss2, sr2), (send2, recv2))
@@ -963,27 +1002,27 @@
                 array[rows_at, :] = value[owner * rows : (owner + 1) * rows]
 
         def up():
-            up_s[here, :] = dot(read(whole), w_up[...])
+            up_s[here, :] = dot(read(whole), whole_of(w_up))
 
         def gate():
-            value, slope = gelu_both(dot(read(whole), w_gate[...]))
+            value, slope = gelu_both(dot(read(whole), whole_of(w_gate)))
             write(hidden, (value * up_s[here, :]).astype(bf16))
             value_s[here, :] = value
             up_s[here, :] = up_s[here, :] * slope
 
         def into_hidden():
-            d_hidden = dot(read(cots), w_down[...])
+            d_hidden = dot(read(cots), whole_of(w_down))
             write(d_up, (d_hidden * value_s[here, :]).astype(bf16))
             write(d_gate, (d_hidden * up_s[here, :]).astype(bf16))
 
         def through_up():
-            grad_s[here, :] = dot_last(read(d_up), w_up[...])
+            grad_s[here, :] = dot_last(read(d_up), whole_of(w_up))
 
         def through_gate():
-            write(part2, (grad_s[here, :] + dot_last(read(d_gate), w_gate[...])).astype(bf16))
+            write(part2, (grad_s[here, :] + dot_last(read(d_gate), whole_of(w_gate))).astype(bf16))
 
         def project():
-            value = dot_last(read(hidden), w_down[...]).astype(bf16)
+            value = dot_last(read(hidden), whole_of(w_down)).astype(bf16)
             write(low_part, value[:, : value.shape[1] // 2])
             write(high_part, value[:, value.shape[1] // 2 :])
 
@@ -1035,19 +1074,61 @@
     for copy in leaving:
         put(done, 0, copy.start)
     if plane is not None:
-        rows = shares[0].shape[0]
-        own = pl.ds(pl.multiple_of(plane.me * rows, TILE), rows)
+        *plane_sems, wide_send, wide_recv, free = rest[3:]
+        half_rows = shares[0].shape[0] // 2
         for share, array in zip(shares, weights):
-            array[own, :] = share[...]
-        items = [(row_view(array, rows), (0, 1)) for array in weights]
-        stages = gather_tasks(plane, items, rest[3:])
+            array[plane.me] = share[...]
+
+        def weight_view(array):
+            return lambda owner, half: array.at[owner, pl.ds(half * half_rows, half_rows)]
+
+        items = [(weight_view(array), (0, 1)) for array in weights]
+        stages = gather_tasks(plane, items, plane_sems)
         for slot, stage in zip((0, 3, 6, 2 * hops + 2), stages):
             put(slot, 0, stage)
+
+        def leave_weights():
+            for bit in plane.bits:
+                pl.semaphore_signal(
+                    free, inc=1, device_id={"dp": plane.other(bit)}, device_id_type=MESH
+                )
+
+        sent = []
+        tokens = Here(whole)
+        tasks, end = reduce_tasks(
+            [
+                Reduce(
+                    i,
+                    tokens,
+                    Here(right),
+                    slice(None),
+                    sent,
+                    *blocks_views(i, both, w_down),
+                    out,
+                    (wide_send, wide_recv),
+                )
+                for i, (right, both, out) in enumerate(
+                    zip((d_up, d_gate), (w_up, w_gate), weight_grads)
+                )
+            ]
+        )
+        put(done - 1, 4, leave_weights)
+        put(done, 0, pl.semaphore_wait, free, len(plane.bits))
+        at = [(slot, order) for slot in range(done, len(slots)) for order in (0.5, 2.5, 3.5)]
+        for (slot, order), task in zip(at, tasks):
+            put(slot, order, task)
+        rest_tasks = tasks[len(at) :]
+    else:
+        rest_tasks = []
     for slot in slots:
         for _, work in sorted(slot, key=lambda entry: entry[0]):
             work()
+    for task in rest_tasks:
+        task()
     for each in (line, back_line, cot_line):
         each.finish()
+    if plane is not None:
+        end()
     for copy in leaving:
         copy.wait()
 
@@ -1055,10 +1136,10 @@
 def sum_back(n, x, d_resid, gain, part, *rest):
     if len(rest) > 6:
         little, gains, *rest = rest
-        sources, rest = rest[:9], rest[9:]
-        grad_x, *outs, little_out, gains_out = rest[:9]
-        left, right, total, ss, sr, *reduce = rest[9:]
-        wide, late_refs, late_sems = reduce[22:29], reduce[29:34], reduce[34]
+        sources, rest = rest[:6], rest[6:]
+        grad_x, *outs, little_out, gains_out = rest[:7]
+        left, right, total, ss, sr, *reduce = rest[7:]
+        wide, late_refs, late_sems = reduce[22:29], reduce[29:35], reduce[35]
         given = [
             Given(little, *reduce[7:11], little_out, reduce[11:13]),
             Given(gains, *reduce[13:17], gains_out, reduce[17:19]),
@@ -1082,42 +1163,25 @@
     if not sources:
         line.run(point)
         return
-    left_a, left_b, right_a, right_b, right_c = late_refs
-    across, width = sources[7].shape[1], sources[8].shape[1]
-    places = (left_a, left_b, right_a, right_b, right_c)
-    places += (left_a, left_b, right_a.at[:, pl.ds(0, across)], right_c.at[:, pl.ds(0, width)])
-    mid, cots, d_up, d_gate, hidden, norm, back_all, cat, mixed = (
-        Late(source, ref, late_sems.at[i]) for i, (source, ref) in enumerate(zip(sources, places))
-    )
-    for array in (mid, d_up, d_gate, cots, hidden):
-        array.begin()
+    width = sources[5].shape[1]
+    cots, hidden, norm, back_all, cat, mixed = late_all(sources, late_refs, late_sems)
     every, sent, sent_wide = slice(None), [], []
-    wide_sides = ((mid, d_up, every), (mid, d_gate, every), (cots, hidden, every))
+    wide_sides = ((cots, hidden, every),)
     sides = (
         (norm, cat, slice(0, width)),
         (norm, cat, slice(width, 2 * width)),
         (back_all, mixed, every),
     )
     parts = [
-        Reduce(i, *side, sent_wide, *wide[:5], out, wide[5:7])
+        Reduce(i, *side, sent_wide, *views(i, *wide[:5]), out, wide[5:7])
         for i, (side, out) in enumerate(zip(wide_sides, outs))
     ]
     parts += [
-        Reduce(i, *side, sent, *reduce[:5], out, reduce[5:7])
-        for i, (side, out) in enumerate(zip(sides, outs[3:]))
+        Reduce(i, *side, sent, *views(i, *reduce[:5]), out, reduce[5:7])
+        for i, (side, out) in enumerate(zip(sides, outs[1:]))
     ]
     tasks, finish = reduce_tasks(parts, given)
 
-    def then(task, *arrays):
-        def both():
-            task()
-            for array in arrays:
-                array.begin()
-
-        return both
-
-    tasks[7] = then(tasks[7], norm, cat)
-    tasks[11] = then(tasks[11], back_all, mixed)
     me = lax.axis_index("mp")
 
     def meet(away):
@@ -1345,12 +1409,15 @@
     most = n_mp * max(pieces[k][1] + pieces[k + 1][1] for k in range(0, PIECES, 2))
     pair = pltpu.VMEM((most, hidden_width), f32)
     flow = pltpu.SemaphoreType.DMA((2, n_mp, PIECES))
-    plane_scratch = [pltpu.VMEM((model, hidden_width), bf16)] * 3 + [pltpu.SemaphoreType.DMA((3, 2, 7))] * 2
+    plane_scratch = [pltpu.VMEM((n_dp, rows, hidden_width), bf16)] * 3
+    plane_scratch += [pltpu.SemaphoreType.DMA((3, 2, 7))] * 2 + [pltpu.SemaphoreType.DMA((2, 10))] * 2
+    plane_scratch += [pltpu.SemaphoreType.REGULAR]
     (
         d_resid,
         gain_mid,
         back_group,
         ffn_high,
+        *ffn_grads,
         norm_mid_group,
         cot_group,
         resid,
@@ -1363,6 +1430,7 @@
         n_mp,
         1,
         [own, shape_of(f32, 1, model), tok, shape_of(bf16, local_rows, model // 2)]
+        + [shape_of(f32, rows, hidden_width)] * (2 * fused)
         + [tok, tok, own, hid, hid, hid, half],
         True,
         True,
@@ -1436,7 +1504,7 @@
         3,
         [shape_of(bf16, local_rows, model)]
         + (
-            [shape_of(f32, rows, hidden_width)] * 3
+            [shape_of(f32, rows, hidden_width)]
             + [shape_of(f32, rows, width)] * 3
             + [shape_of(f32, piece, little.shape[1]), shape_of(f32, 2 * SUB, LANE)]
         )
@@ -1448,10 +1516,7 @@
             (
                 little,
                 gain_parts,
-                norm_mid_group,
                 cot_group,
-                d_up,
-                d_gate_ff,
                 hidden,
                 norm_group,
                 back_group,
@@ -1466,16 +1531,16 @@
         + given_scratch(2 * SUB, LANE)
         + [pltpu.VMEM((n_mp - 1, 2 * SUB, LANE), f32)]
         + [pltpu.SemaphoreType.DMA((n_mp - 1,))] * 2
-        + reduce_scratch(3, rows, hidden_width)
-        + [pltpu.VMEM((count, model), bf16)] * 2
-        + [pltpu.VMEM((count, hidden_width), bf16)] * 3
-        + [pltpu.SemaphoreType.DMA((9,))]
+        + reduce_scratch(1, rows, hidden_width)
+        + [pltpu.VMEM(a.shape, a.dtype) for a in (cot_group, hidden, norm_group, back_group, d_cat, mixed)]
+        + [pltpu.SemaphoreType.DMA((6,))]
         if fused
         else (),
-        9 * fused,
+        6 * fused,
     )
     if fused:
-        up_grad, gate_ff_grad, down_grad, *mix_grads, little_own, gain_own = mix_grads
+        up_grad, gate_ff_grad = ffn_grads
+        down_grad, *mix_grads, little_own, gain_own = mix_grads
     else:
         up_grad = reduced(norm_mid_group, d_up)
         gate_ff_grad = reduced(norm_mid_group, d_gate_ff)

time: 479 us -> 463 us (0.967)
  Pallas kernels: 434 us -> 420 us
    pallas_call x3, Pallas kernels: 377 us -> 363 us  [line_call(): pl.pallas_call(functools.partial(body, n), out_shape=outs, in_specs=[whol...]
where the time goes in v10:
time: 463 us; the launch traced here: 455 us
  Pallas kernels  420 us (91%)
  between operations  14.7 us (3%)
  local copies, waits for them, and re-layouts  8.3 us (2%)
  waiting for transfers between devices  8.03 us (2%)
    pallas_call x3, Pallas kernels, line_call(): pl.pallas_call(functools.partial(body, n), out_shape=outs, in_specs=[whol...  363 us
    pallas_call x3, Pallas kernels, local_call(): pl.pallas_call(body, out_shape=outs, in_specs=[whole] * (len(args) - late...  57 us
  transfers between devices with their start and end apart: 2, of which 2 were waited for; matrix products, arithmetic and copies ran while one was open for 1% of the time, Pallas kernels for 11%

profile of v10, /device:TPU:0, one launch (start us, length us, event | category | flops | bytes accessed | tf_op | source)
XLA Modules:
  0.0 454.5 jit_solution(2817823059524936862)
XLA Ops:
  7.2 0.0 all-gather.2.cloned.1.call-start
  7.2 0.7 convert_element_type.11
  7.9 0.7 maximum_bitcast_fusion
  8.7 1.4 fusion
  10.0 1.3 broadcast_multiply_fusion.cot
  11.3 0.8 slice.19
  12.1 0.6 pad.9.chan
  12.7 69.1 %shard_map.255 = (bf16[1088,1536]{1,0:T(8,128)(2,1)}, bf16[1536,512]{1,0:T(8,128)(2,1)}, bf16[1536,512]{1,0:T(8,128)(2,1)}, bf16[1536,512]{1,0:T(8,128)(2,1)}, b...) custom-call(bf16[272,1536]{1,0:T(8,128)(2,1)} %x.11, f32[1,1536]{1,0:T(1,128)} %get-tuple-element.113.gain, ...), custom_call_target="tpu_custom_call" | custom-call | bytes 147251200 | tf_op jit(solution)/shard_map/pallas_call | solution.py:1229
  81.8 0.0 all-gather.2.cloned.1.call-update
  81.8 0.0 reduce-scatter.2.cloned.1.call-start
  81.9 0.1 reshape_squeeze.3
  82.0 0.1 copy.41
  82.1 0.7 reshape_reshape.7.orow
  82.8 1.0 reshape_reshape.8.ocol
  83.8 0.2 reduce-window_clone.1
  84.0 0.1 select_reduce_fusion
  84.1 0.1 reduce_max.12
  84.2 0.1 select_add_fusion
  84.3 0.1 copy.42
  84.4 1.0 reshape.60.pos
  85.4 23.7 %shard_map.256 = (f32[1088,512]{1,0:T(8,128)}, f32[1088,512]{1,0:T(8,128)}, f32[1088,512]{1,0:T(8,128)}, f32[1088,512]{1,0:T(8,128)}, f32[1088,512]{1,0:T(8,128)...) custom-call(bf16[1088,1536]{1,0:T(8,128)(2,1)} %get-tuple-element.64.tokens.rest_6_.rest_4_, ...), custom_call_target="tpu_custom_call" | custom-call | flops 8770289664 | bytes 26194784 | tf_op jit(solution)/shard_map/pallas_call | solution.py:1285
  109.1 1.9 all-gather.2.cloned.1.call-done.rest_3_
  111.0 220.5 %shard_map.257 = (f32[272,1536]{1,0:T(8,128)}, f32[1,1536]{1,0:T(1,128)}, bf16[1088,1536]{1,0:T(8,128)(2,1)}, bf16[272,768]{1,0:T(8,128)(2,1)}, f32[192,1152]{1,...) custom-call(bf16[272,1536]{1,0:T(8,128)(2,1)} %x.11, ...), custom_call_target="tpu_custom_call" | custom-call | bytes 746086400 | tf_op jit(solution)/shard_map/pallas_call | solution.py:1229
  331.6 28.0 %shard_map.258 = (bf16[1088,1024]{1,0:T(8,128)(2,1)}, bf16[1088,1536]{1,0:T(8,128)(2,1)}, f32[128,1152]{1,0:T(8,128)}, f32[1,1536]{1,0:T(1,128)}) custom-call(bf16[1088,1536]{1,0:T(8,128)(2,1)} %get-tuple-element.74.back.rest_5_, bf16[1536,512]{1,0:T(8,128)(2,1)} %get-tuple-element.69.w_out_far.w_out, s32[1088,1]{1,0:T(8,128)} %reshape_reshape.8.ocol, ...), custom_call_target="tpu_custom_call" | custom-call | flops 8770289664 | bytes 31253344 | tf_op jit(solution)/shard_map/pallas_call | solution.py:1285
  359.6 0.7 pad_maximum_fusion
  360.3 0.1 reshape.57
  360.5 0.6 pad.10
  361.1 6.1 %reduce-scatter.2.cloned.1.call-done.low = bf16[272,768]{1,0:T(8,128)(2,1)} async-done(((bf16[1088,768]{1,0:T(8,128)(2,1)}), bf16[272,768]{1,0:T(8,128)(2,1)}) %reduce-scatter.2.cloned.1.call-update) | async-done | bytes 417808 | tf_op jit(solution)/shard_map/reduce_scatter | solution.py:1499
  367.3 73.1 %shard_map.259 = (bf16[272,1536]{1,0:T(8,128)(2,1)}, f32[192,1152]{1,0:T(8,128)}, f32[192,512]{1,0:T(8,128)}, f32[192,512]{1,0:T(8,128)}, f32[192,512]{1,0:T(8,1...) custom-call(bf16[272,1536]{1,0:T(8,128)(2,1)} %x.11, f32[272,1536]{1,0:T(8,128)} %get-tuple-element.84.d_resid, ...), custom_call_target="tpu_custom_call" | custom-call | bytes 2238668800 | tf_op jit(solution)/shard_map/pallas_call | solution.py:1229
  440.4 5.2 %shard_map.260 = (bf16[272,1536]{1,0:T(8,128)(2,1)}, f32[2,48]{1,0:T(2,128)}, f32[4,4,16]{2,1,0:T(4,128)}, f32[3,4,16]{2,1,0:T(4,128)}, f32[4,16]{1,0:T(4,128)},...) custom-call(f32[272,1536]{1,0:T(8,128)} %get-tuple-element.72.resid,, ...), custom_call_target="tpu_custom_call" | custom-call | bytes 10275200 | tf_op jit(solution)/shard_map/pallas_call | solution.py:1285
  445.6 0.7 copy.52
  446.4 0.9 copy.53
  (19 shorter events, 0.1 us)
Async XLA Ops:
  7.2 74.7 %copy-start.4 = (s32[1,1088]{1,0:T(1,128)S(1)}, s32[1,1088]{1,0:T(1,128)}, u32[]{:S(2)}) copy-start(s32[1,1088]{1,0:T(1,128)} %param.19) | copy-start | bytes 13060
  7.2 103.8 %all-gather.2.cloned.1.call-start = ((), (), s32[]{:S(2)}) async-start(), calls=%async_computation.1 | async-start | bytes 1392640 | tf_op jit(solution)/shard_map/all_gather | solution.py:1383
  10.0 73.8 %copy-start.5 = (s32[1,4]{1,0:T(1,128)S(1)}, s32[1,4]{1,0:T(1,128)}, u32[]{:S(2)}) copy-start(s32[1,4]{1,0:T(1,128)} %param.20) | copy-start | bytes 52
  11.3 97.8 %copy-start = (bf16[272,1536]{1,0:T(8,128)(2,1)}, bf16[272,1536]{1,0:T(8,128)(2,1)S(1)}, u32[]{:S(2)}) copy-start(bf16[272,1536]{1,0:T(8,128)(2,1)S(1)} %broadcast_multiply_fusion.cot) | copy-start | bytes 2506756
  81.8 285.4 %reduce-scatter.2.cloned.1.call-start = ((), (), s32[]{:S(2)}) async-start(), calls=%async_computation.2 | async-start | bytes 2088960 | tf_op jit(solution)/shard_map/reduce_scatter | solution.py:1499
  331.6 28.1 %copy-start.3 = (f32[1,1536]{1,0:T(1,128)S(1)}, f32[1,1536]{1,0:T(1,128)}, u32[]{:S(2)}) copy-start(f32[1,1536]{1,0:T(1,128)} %get-tuple-element.88) | copy-start | bytes 18436
  440.3 5.3 %copy-start.2 = (f32[192,512]{1,0:T(8,128)S(1)}, f32[192,512]{1,0:T(8,128)}, u32[]{:S(2)}) copy-start(f32[192,512]{1,0:T(8,128)} %get-tuple-element.105) | copy-start | bytes 1179652
  440.3 6.0 %copy-start.1 = (f32[192,1152]{1,0:T(8,128)S(1)}, f32[192,1152]{1,0:T(8,128)}, u32[]{:S(2)}) copy-start(f32[192,1152]{1,0:T(8,128)} %get-tuple-element.112) | copy-start | bytes 2654212
Sparse Core Ops, SparseCore 0:
  81.9 29.0 all-gather.1
  331.7 35.5 reduce-scatter.1

commit v11 on v10

--- a/solution.py
+++ b/solution.py
@@ -180,10 +180,18 @@
 
 
 def mixer_backward(back, w_out, ocol, orow, pos, gain, chan, blocks, *rest):
-    far, (dcat_ref, dnorm_ref, little_ref, dgain_ref), rest = rest[:9], rest[9:13], rest[13:]
+    more = 2 if len(rest) > 36 else 0
+    far, rest = rest[: 9 + more], rest[9 + more :]
+    (dcat_ref, dnorm_ref, little_ref, dgain_ref), rest = rest[:4], rest[4:]
+    passed_on, rest = rest[:more], rest[more:]
     dmix_arr, dmix, adj, prod, after, before, low, small_ref, dblocks_ref, *rest = rest
-    gate_ref, grec_ref, state_ref, conv_ref, gin_ref, branch_ref, norm, w_in, w_gate, late_sem = rest
-    late = late_all(far, rest[:9], late_sem)
+    gate_ref, grec_ref, state_ref, conv_ref, gin_ref, branch_ref, norm, w_in, w_gate, *extra = rest[: 9 + more]
+    late_sem = rest[9 + 2 * more]
+    late = late_all(far, rest[: 9 + more], late_sem)
+    leaving = [
+        pltpu.make_async_copy(source, target, rest[-1].at[i, 0])
+        for i, (source, target) in enumerate(zip(extra, passed_on))
+    ]
     count, _ = back.shape
     width = w_in.shape[1]
     steps = count // SUB
@@ -212,6 +220,8 @@
     lax.fori_loop(0, blocks_of, pack, 0)
     for array in late:
         array.ready()
+    for copy in leaving:
+        copy.start()
 
     def scan(i, carry):
         held, passed, following = carry
@@ -339,6 +349,8 @@
 
     lax.fori_loop(0, blocks_of, leave, 0)
     dgain_ref[...] = dgain_ref[...] / gain[...]
+    for copy in leaving:
+        copy.wait()
 
 
 MESH = pl.DeviceIdType.MESH
@@ -851,12 +863,17 @@
     w_out,
     blocks,
     chan,
+    order,
+    lengths,
     whole,
     all_in,
     all_gate,
     all_out,
     all_blocks,
     all_chan,
+    ocol,
+    orow,
+    pos,
     send,
     recv,
     raw,
@@ -915,8 +932,29 @@
 
         line.tiles(k, one)
 
+    def indices():
+        count = whole.shape[0]
+        steps = count // SUB
+        tokens = order[...].astype(f32)
+        across = lax.broadcasted_iota(jnp.int32, (ROWS, count), 1)
+        line_total = jnp.zeros((1, count), f32)
+        for b in range(count // ROWS):
+            row = lax.broadcasted_iota(jnp.int32, (ROWS, 1), 0) + b * ROWS
+            token = lax.rem(row, SUB) * steps + lax.div(row, SUB)
+            picked = jnp.sum(jnp.where(across == token, tokens, 0.0), axis=1, keepdims=True)
+            ocol[pl.ds(b * ROWS, ROWS), :] = picked.astype(jnp.int32)
+            line_total += jnp.sum(jnp.where(across == row, picked, 0.0), axis=0, keepdims=True)
+        orow[...] = line_total.astype(jnp.int32)
+        row = lax.broadcasted_iota(jnp.int32, pos.shape, 0)
+        token = lax.rem(row, SUB) * steps + lax.div(row, SUB)
+        start, own_start = jnp.zeros((1, 1), jnp.int32), jnp.zeros(pos.shape, jnp.int32)
+        for k in range(lengths.shape[1]):
+            own_start = jnp.where(token >= start, start, own_start)
+            start = start + lengths[:, k : k + 1]
+        pos[...] = jnp.where(token >= count, -1, token - own_start)
+
     first()
-    line.run(point, [idle] * 4 + [second] + [idle] * 3 + [third] + [idle] * 3 + [last])
+    line.run(point, [idle] * 4 + [second, indices] + [idle] * 2 + [third] + [idle] * 3 + [last])
 
 
 def norm_back(value, gain, grad):
@@ -1023,8 +1061,8 @@
 
         def project():
             value = dot_last(read(hidden), whole_of(w_down)).astype(bf16)
-            write(low_part, value[:, : value.shape[1] // 2])
-            write(high_part, value[:, value.shape[1] // 2 :])
+            write(low_part, value[:, : low_part.shape[1]])
+            write(high_part, value[:, low_part.shape[1] :])
 
         return up, gate, into_hidden, through_up, through_gate, project
 
@@ -1328,30 +1366,18 @@
     lines = jnp.concatenate([conv_weight, chan_bias, decay[None]], axis=0).transpose(1, 0, 2)
     lines = lines.reshape(SUB * heads, piece)
 
-    steps = count // SUB
-    ends = jnp.cumsum(lengths[0], dtype=jnp.int32)
-    starts = ends - lengths[0]
-    places = jnp.arange(count, dtype=jnp.int32)
-    own_start = jnp.max(
-        jnp.where(places[:, None] >= starts[None, :], starts[None, :], 0), axis=1
-    )
-    pos = (places - own_start).reshape(SUB, steps).T
-    wrap = jnp.concatenate([pos[: TAIL // SUB, 1:], jnp.full((TAIL // SUB, 1), -1, jnp.int32)], axis=1)
-    pos_col = jnp.concatenate([pos, wrap], axis=0).reshape(count + TAIL, 1)
-    order_int = order[0].reshape(SUB, steps).T.reshape(count)
-    ocol, orow = order_int.reshape(count, 1), order_int.reshape(1, count)
-
     gain_f = gains.astype(f32)
     n_mp = lax.axis_size("mp")
     tok = shape_of(bf16, count, model)
     own = shape_of(f32, local_rows, model)
     if fused:
         grown = shape_of(bf16, model, width)
-        norm_group, full_in, full_gate, full_out, blocks, chan = line_call(
+        norm_group, full_in, full_gate, full_out, blocks, chan, ocol, orow, pos_col = line_call(
             gather_weights,
             n_mp,
             0,
-            [tok, grown, grown, grown, shape_of(bf16, 2 * heads, LANE, LANE), shape_of(f32, 16, width)],
+            [tok, grown, grown, grown, shape_of(bf16, 2 * heads, LANE, LANE), shape_of(f32, 16, width)]
+            + [shape_of(jnp.int32, *at) for at in ((count, 1), (1, count), (count + TAIL, 1))],
             False,
             True,
             (
@@ -1362,10 +1388,24 @@
                 out_rows,
                 gate_blocks.reshape(2 * heads, piece, LANE),
                 jnp.pad(lines, ((0, 0), (0, LANE - piece))),
+                order,
+                lengths,
             ),
             [pltpu.VMEM((n_dp * SUB * heads, LANE), bf16)] + [pltpu.SemaphoreType.DMA((5, 2, 7))] * 2,
         )
     else:
+        steps = count // SUB
+        ends = jnp.cumsum(lengths[0], dtype=jnp.int32)
+        starts = ends - lengths[0]
+        places = jnp.arange(count, dtype=jnp.int32)
+        own_start = jnp.max(
+            jnp.where(places[:, None] >= starts[None, :], starts[None, :], 0), axis=1
+        )
+        pos = (places - own_start).reshape(SUB, steps).T
+        wrap = jnp.concatenate([pos[: TAIL // SUB, 1:], jnp.full((TAIL // SUB, 1), -1, jnp.int32)], axis=1)
+        pos_col = jnp.concatenate([pos, wrap], axis=0).reshape(count + TAIL, 1)
+        order_int = order[0].reshape(SUB, steps).T.reshape(count)
+        ocol, orow = order_int.reshape(count, 1), order_int.reshape(1, count)
         (norm_group,) = line_call(gather_norm, n_mp, 0, [tok], False, True, (inputs, gain_f[0:1]))
         full_in = lax.all_gather(w_in, "dp", axis=0, tiled=True)
         full_gate = lax.all_gather(w_gate, "dp", axis=0, tiled=True)
@@ -1403,8 +1443,9 @@
     if not fused:
         shares = [lax.all_gather(share, "dp", axis=0, tiled=True) for share in shares]
     hid = shape_of(bf16, count, hidden_width)
-    half = shape_of(bf16, count, model // 2)
-    half_twin = pltpu.VMEM(half.shape, bf16)
+    low_width = model * 5 // 12
+    low_shape = shape_of(bf16, count, low_width)
+    high_twin = pltpu.VMEM((count, model - low_width), bf16)
     pieces = cut_rows(local_rows, PIECES)
     most = n_mp * max(pieces[k][1] + pieces[k + 1][1] for k in range(0, PIECES, 2))
     pair = pltpu.VMEM((most, hidden_width), f32)
@@ -1429,17 +1470,17 @@
         middle,
         n_mp,
         1,
-        [own, shape_of(f32, 1, model), tok, shape_of(bf16, local_rows, model // 2)]
+        [own, shape_of(f32, 1, model), tok, shape_of(bf16, local_rows, model - low_width)]
         + [shape_of(f32, rows, hidden_width)] * (2 * fused)
-        + [tok, tok, own, hid, hid, hid, half],
+        + [tok, tok, own, hid, hid, hid, low_shape],
         True,
         True,
         (inputs, gain_f[1:2], cot, back_part, *shares, cot_first),
         [pltpu.VMEM((count, model), bf16)]
         + [flow] * 6
         + [pair, pair, pltpu.VMEM((most, model), f32)]
-        + [half_twin] * 3
-        + [pltpu.VMEM((max(rows for _, rows in pieces), model // 2), f32), flow, flow]
+        + [high_twin] * 3
+        + [pltpu.VMEM((max(rows for _, rows in pieces), model - low_width), f32), flow, flow]
         + [pltpu.SemaphoreType.DMA(())]
         + plane_scratch * fused,
         late=1,
@@ -1450,14 +1491,15 @@
         grad = dot_first(left, right).astype(bf16)
         return lax.psum_scatter(grad, "dp", scatter_dimension=0, tiled=True).astype(f32)
 
-    d_cat, d_norm_back, little, gain_in = local_call(
+    d_cat, d_norm_back, little, gain_in, *ffn_grads = local_call(
         mixer_backward,
         [
             shape_of(bf16, count, 2 * width),
             tok,
             shape_of(f32, LANE, 2 * width + LANE),
             shape_of(f32, 1, model),
-        ],
+        ]
+        + [shape_of(f32, *a.shape) for a in ffn_grads],
         [
             pltpu.VMEM((count, width), bf16),
             wide,
@@ -1488,8 +1530,10 @@
             norm_group,
             full_in,
             full_gate,
+            *ffn_grads,
         ),
-        9,
+        9 + len(ffn_grads),
+        len(ffn_grads),
     )
     share = model // (n_dp * n_mp)
     gain_parts = jnp.concatenate([gain_in, gain_mid], axis=0).reshape(2, n_dp, n_mp, share)
@@ -1560,7 +1604,7 @@
         shape_of(f32, heads, piece),
         shape_of(f32, 2, heads, piece, LANE),
     ]
-    copied = [grad_inputs, mix_grads[0], mix_grads[1], up_grad, gate_ff_grad] if fused else []
+    copied = [grad_inputs, mix_grads[0], mix_grads[1]] if fused else []
     output, grad_gains, grad_conv, grad_bias, grad_decay, grad_blocks, *copied = local_call(
         functools.partial(finish, heads, piece, share),
         outs + [shape_of(a.dtype, *a.shape) for a in copied],
@@ -1569,7 +1613,7 @@
         (resid, ffn_low, ffn_high, gain_own, little_own, *copied),
     )
     if fused:
-        grad_inputs, grad_in, grad_gate, up_grad, gate_ff_grad = copied
+        grad_inputs, grad_in, grad_gate = copied
     else:
         grad_in, grad_gate, _ = mix_grads
     return (

time: 463 us -> 462 us (level)
  Pallas kernels: 420 us -> 426 us
    pallas_call x3, Pallas kernels: 363 us -> 369 us  [line_call(): pl.pallas_call(functools.partial(body, n), out_shape=outs, in_specs=[whol...]
    reduce_scatter x1, waiting for transfers between devices: 6.14 us -> 0.71 us  [shards(): ffn_low = lax.psum_scatter(ffn_part, 'mp', scatter_dimension=0, tiled=True)]
  transfers between devices with their start and end apart: 2 -> 2, of which waited for: 2 -> 2; matrix products, arithmetic and copies ran while one was open for 1% -> 0% of each run, Pallas kernels for 11% -> 12%
where the time goes in v11:
time: 462 us; the launch traced here: 454 us
  Pallas kernels  426 us (92%)
  between operations  14.4 us (3%)
  waiting for transfers between devices  5.45 us (1%)
  local copies, waits for them, and re-layouts  5.24 us (1%)
    pallas_call x3, Pallas kernels, line_call(): pl.pallas_call(functools.partial(body, n), out_shape=outs, in_specs=[whol...  369 us
    pallas_call x3, Pallas kernels, local_call(): pl.pallas_call(body, out_shape=outs, in_specs=[whole] * (len(args) - late...  57 us
  transfers between devices with their start and end apart: 2, of which 2 were waited for; matrix products, arithmetic and copies ran while one was open for 0% of the time, Pallas kernels for 12%

profile of v11, /device:TPU:0, one launch (start us, length us, event | category | flops | bytes accessed | tf_op | source)
XLA Modules:
  0.0 454.2 jit_solution(8509703324951880958)
XLA Ops:
  7.2 0.0 all-gather.2.cloned.1.call-start
  7.2 0.7 convert_element_type.11
  7.9 0.7 maximum_bitcast_fusion
  8.7 1.4 fusion
  10.0 1.3 broadcast_multiply_fusion.cot
  11.3 0.0 copy-start
  11.3 0.8 slice.15
  12.1 0.6 pad.8.chan
  12.7 70.4 %shard_map.255 = (bf16[1088,1536]{1,0:T(8,128)(2,1)}, bf16[1536,512]{1,0:T(8,128)(2,1)}, bf16[1536,512]{1,0:T(8,128)(2,1)}, bf16[1536,512]{1,0:T(8,128)(2,1)}, b...) custom-call(bf16[272,1536]{1,0:T(8,128)(2,1)} %x.9, ...), custom_call_target="tpu_custom_call" | custom-call | bytes 147688000 | tf_op jit(solution)/shard_map/pallas_call | solution.py:1267
  83.1 0.0 all-gather.2.cloned.1.call-update
  83.2 0.0 reduce-scatter.2.cloned.1.call-start
  83.2 23.7 %shard_map.256 = (f32[1088,512]{1,0:T(8,128)}, f32[1088,512]{1,0:T(8,128)}, f32[1088,512]{1,0:T(8,128)}, f32[1088,512]{1,0:T(8,128)}, f32[1088,512]{1,0:T(8,128)...) custom-call(bf16[1088,1536]{1,0:T(8,128)(2,1)} %get-tuple-element.67.tokens.rest_6_.rest_4_, ...), custom_call_target="tpu_custom_call" | custom-call | flops 8770289664 | bytes 26194784 | tf_op jit(solution)/shard_map/pallas_call | solution.py:1323
  106.9 0.0 copy-done
  106.9 4.7 %all-gather.2.cloned.1.call-done.rest_3_ = bf16[1088,512]{1,0:T(8,128)(2,1)} async-done(((bf16[272,512]{1,0:T(8,128)(2,1)}), bf16[1088,512]{1,0:T(8,128)(2,1)}) %all-gather.2.cloned.1.call-update) | async-done | bytes 1114128 | tf_op jit(solution)/shard_map/all_gather | solution.py:1423
  111.6 224.4 %shard_map.257 = (f32[272,1536]{1,0:T(8,128)}, f32[1,1536]{1,0:T(1,128)}, bf16[1088,1536]{1,0:T(8,128)(2,1)}, bf16[272,896]{1,0:T(8,128)(2,1)}, f32[192,1152]{1,...) custom-call(bf16[272,1536]{1,0:T(8,128)(2,1)} %x.9, ...), custom_call_target="tpu_custom_call" | custom-call | bytes 746086400 | tf_op jit(solution)/shard_map/pallas_call | solution.py:1267
  336.0 0.0 reduce-scatter.2.cloned.1.call-update
  336.0 0.0 copy-start.3
  336.0 29.3 %shard_map.258 = (bf16[1088,1024]{1,0:T(8,128)(2,1)}, bf16[1088,1536]{1,0:T(8,128)(2,1)}, f32[128,1152]{1,0:T(8,128)}, f32[1,1536]{1,0:T(1,128)}, f32[192,1152]{1,0:T(8,128)}, /*index=5*/f32[192,1152]{1,0:T(8,128)}) custom-call(bf16[1088,1536]{1,0:T(8,128)(2,1)} %get-tuple-element.80.back.rest_5_, bf16[1536,512]{1,0:T(8,128)(2,1)} %get-tuple-element.75.w_out_far.w_out, ...), custom_call_target="tpu_custom_call" | custom-call | flops 8770289664 | bytes 34792288 | tf_op jit(solution)/shard_map/pallas_call | solution.py:1323
  365.4 0.0 copy-done.3
  365.4 0.7 pad_maximum_fusion
  366.1 0.1 reshape.44
  366.2 0.6 pad.9
  366.8 0.7 reduce-scatter.2.cloned.1.call-done.low
  367.6 74.0 %shard_map.259 = (bf16[272,1536]{1,0:T(8,128)(2,1)}, f32[192,1152]{1,0:T(8,128)}, f32[192,512]{1,0:T(8,128)}, f32[192,512]{1,0:T(8,128)}, f32[192,512]{1,0:T(8,1...) custom-call(bf16[272,1536]{1,0:T(8,128)(2,1)} %x.9, f32[272,1536]{1,0:T(8,128)} %get-tuple-element.92.d_resid, ...), custom_call_target="tpu_custom_call" | custom-call | bytes 2238668800 | tf_op jit(solution)/shard_map/pallas_call | solution.py:1267
  441.5 0.0 copy-start.2
  441.5 0.0 copy-start.1
  441.5 4.0 shard_map.260
  445.5 0.0 copy-done.2
  445.5 0.7 copy.35
  446.3 0.0 copy-done.1
  446.3 0.9 copy.36
  (2 shorter events, 0.0 us)
Async XLA Ops:
  7.2 104.5 %all-gather.2.cloned.1.call-start = ((), (), s32[]{:S(2)}) async-start(), calls=%async_computation.1 | async-start | bytes 1392640 | tf_op jit(solution)/shard_map/all_gather | solution.py:1423
  11.3 95.6 %copy-start = (bf16[272,1536]{1,0:T(8,128)(2,1)}, bf16[272,1536]{1,0:T(8,128)(2,1)S(1)}, u32[]{:S(2)}) copy-start(bf16[272,1536]{1,0:T(8,128)(2,1)S(1)} %broadcast_multiply_fusion.cot) | copy-start | bytes 2506756
  83.2 284.4 %reduce-scatter.2.cloned.1.call-start = ((), (), s32[]{:S(2)}) async-start(), calls=%async_computation.2 | async-start | bytes 1740800 | tf_op jit(solution)/shard_map/reduce_scatter | solution.py:1543
  336.0 29.3 %copy-start.3 = (f32[1,1536]{1,0:T(1,128)S(1)}, f32[1,1536]{1,0:T(1,128)}, u32[]{:S(2)}) copy-start(f32[1,1536]{1,0:T(1,128)} %get-tuple-element.96) | copy-start | bytes 18436
  441.5 4.0 copy-start.2
  441.5 4.8 %copy-start.1 = (f32[192,1152]{1,0:T(8,128)S(1)}, f32[192,1152]{1,0:T(8,128)}, u32[]{:S(2)}) copy-start(f32[192,1152]{1,0:T(8,128)} %get-tuple-element.118) | copy-start | bytes 2654212
Sparse Core Ops, SparseCore 0:
  83.3 28.3 all-gather.1
  336.1 31.3 reduce-scatter.1

commit v12 on v11

--- a/solution.py
+++ b/solution.py
@@ -865,6 +865,8 @@
     chan,
     order,
     lengths,
+    cotangent,
+    mask,
     whole,
     all_in,
     all_gate,
@@ -874,6 +876,8 @@
     ocol,
     orow,
     pos,
+    cot,
+    cot_first,
     send,
     recv,
     raw,
@@ -953,8 +957,18 @@
             start = start + lengths[:, k : k + 1]
         pos[...] = jnp.where(token >= count, -1, token - own_start)
 
+    def masked():
+        count = cotangent.shape[0]
+        row = lax.broadcasted_iota(jnp.int32, (count, count), 0)
+        column = lax.broadcasted_iota(jnp.int32, (count, count), 1)
+        kept = jnp.where(row == column, mask[...].astype(f32), 0.0)
+        kept = jnp.sum(kept, axis=1, keepdims=True)
+        value = (cotangent[...].astype(f32) * kept).astype(bf16)
+        cot[...] = value
+        cot_first[...] = value[:, : cot_first.shape[1]]
+
     first()
-    line.run(point, [idle] * 4 + [second, indices] + [idle] * 2 + [third] + [idle] * 3 + [last])
+    line.run(point, [idle] * 4 + [second, indices, masked, idle, third] + [idle] * 3 + [last])
 
 
 def norm_back(value, gain, grad):
@@ -1080,7 +1094,7 @@
         put(met, 3, line.sent, k)
         put(met, 3, point, k)
         put(met, 3, line.spread, k)
-        given = k if 2 * k < PIECES else min(2 * k - PIECES // 2 + 1, PIECES + 2)
+        given = max(k - 2, 0) if 2 * k <= PIECES else min(2 * k - 3, PIECES + 2)
         put(given, 0, cot_line.tiles, k, keep_cot)
         put(given, 0, cot_line.spread, k)
         for stage in range(1, n):
@@ -1101,7 +1115,7 @@
             put(begun + hops, 3, back_line.spread, k)
             for stage in range(1, n):
                 put(begun + hops + stage, 5, back_line.forward, k, stage)
-            begun += 1
+            begun += hops
             put(begun, 4, high_line.first, k)
             for stage in range(1, hops):
                 put(begun + stage, 4, high_line.relay, k, stage)
@@ -1372,12 +1386,14 @@
     own = shape_of(f32, local_rows, model)
     if fused:
         grown = shape_of(bf16, model, width)
-        norm_group, full_in, full_gate, full_out, blocks, chan, ocol, orow, pos_col = line_call(
+        norm_group, full_in, full_gate, full_out, blocks, chan, ocol, orow, pos_col, cot, cot_first = (
+            line_call(
             gather_weights,
             n_mp,
             0,
             [tok, grown, grown, grown, shape_of(bf16, 2 * heads, LANE, LANE), shape_of(f32, 16, width)]
-            + [shape_of(jnp.int32, *at) for at in ((count, 1), (1, count), (count + TAIL, 1))],
+            + [shape_of(jnp.int32, *at) for at in ((count, 1), (1, count), (count + TAIL, 1))]
+            + [shape_of(bf16, local_rows, model), shape_of(bf16, local_rows, model // 3)],
             False,
             True,
             (
@@ -1390,8 +1406,11 @@
                 jnp.pad(lines, ((0, 0), (0, LANE - piece))),
                 order,
                 lengths,
+                cotangent,
+                token_mask.reshape(1, -1),
             ),
             [pltpu.VMEM((n_dp * SUB * heads, LANE), bf16)] + [pltpu.SemaphoreType.DMA((5, 2, 7))] * 2,
+        )
         )
     else:
         steps = count // SUB
@@ -1417,9 +1436,10 @@
         chan = jnp.concatenate(
             [params[:7], jax.nn.softplus(decay_row)] + [jax.nn.sigmoid(decay_row)] * SUB, axis=0
         )
-    cot = cotangent * token_mask.astype(bf16)[:, None]
-
-    cot_first, norm_group = lax.optimization_barrier((cot[:, : model // 3], norm_group))
+
+    if not fused:
+        cot = cotangent * token_mask.astype(bf16)[:, None]
+        cot_first = cot[:, : model // 3]
     cot_first = lax.all_gather(cot_first, "mp", axis=0, tiled=True)
 
     wide = pltpu.VMEM((count, width), f32)

time: 462 us -> 458 us (level)
  no operation moved by 1% of the time
where the time goes in v12:
time: 458 us; the launch traced here: 450 us
  Pallas kernels  423 us (92%)
  between operations  14.3 us (3%)
  local copies, waits for them, and re-layouts  5.66 us (1%)
  waiting for transfers between devices  5.13 us (1%)
    pallas_call x3, Pallas kernels, line_call(): pl.pallas_call(functools.partial(body, n), out_shape=outs, in_specs=[whol...  366 us
    pallas_call x3, Pallas kernels, local_call(): pl.pallas_call(body, out_shape=outs, in_specs=[whole] * (len(args) - late...  57 us
  transfers between devices with their start and end apart: 2, of which 2 were waited for; matrix products, arithmetic and copies ran while one was open for 0% of the time, Pallas kernels for 12%

profile of v12, /device:TPU:0, one launch (start us, length us, event | category | flops | bytes accessed | tf_op | source)
XLA Modules:
  0.0 450.0 jit_solution(14331074236862104874)
XLA Ops:
  7.2 0.0 all-gather.2.cloned.1.call-start
  7.2 1.2 reshape.46.mask
  8.5 0.7 maximum_bitcast_fusion
  9.2 1.4 fusion
  10.6 0.6 pad.8.chan
  11.2 70.9 %shard_map.255 = (bf16[1088,1536]{1,0:T(8,128)(2,1)}, bf16[1536,512]{1,0:T(8,128)(2,1)}, bf16[1536,512]{1,0:T(8,128)(2,1)}, bf16[1536,512]{1,0:T(8,128)(2,1)}, b...) custom-call(bf16[272,1536]{1,0:T(8,128)(2,1)} %x.9, ...), custom_call_target="tpu_custom_call" | custom-call | bytes 231355200 | tf_op jit(solution)/shard_map/pallas_call | solution.py:1281
  82.1 0.0 all-gather.2.cloned.1.call-update
  82.1 0.0 reduce-scatter.2.cloned.1.call-start
  82.2 23.7 %shard_map.256 = (f32[1088,512]{1,0:T(8,128)}, f32[1088,512]{1,0:T(8,128)}, f32[1088,512]{1,0:T(8,128)}, f32[1088,512]{1,0:T(8,128)}, f32[1088,512]{1,0:T(8,128)...) custom-call(bf16[1088,1536]{1,0:T(8,128)(2,1)} %get-tuple-element.67.tokens.rest_6_.rest_4_, ...), custom_call_target="tpu_custom_call" | custom-call | flops 8770289664 | bytes 26194784 | tf_op jit(solution)/shard_map/pallas_call | solution.py:1337
  105.9 4.7 %all-gather.2.cloned.1.call-done.rest_3_ = bf16[1088,512]{1,0:T(8,128)(2,1)} async-done(((bf16[272,512]{1,0:T(8,128)(2,1)}), bf16[1088,512]{1,0:T(8,128)(2,1)}) %all-gather.2.cloned.1.call-update) | async-done | bytes 1114128 | tf_op jit(solution)/shard_map/all_gather | solution.py:1443
  110.6 221.6 %shard_map.257 = (f32[272,1536]{1,0:T(8,128)}, f32[1,1536]{1,0:T(1,128)}, bf16[1088,1536]{1,0:T(8,128)(2,1)}, bf16[272,896]{1,0:T(8,128)(2,1)}, f32[192,1152]{1,...) custom-call(bf16[272,1536]{1,0:T(8,128)(2,1)} %x.9, ...), custom_call_target="tpu_custom_call" | custom-call | bytes 746086400 | tf_op jit(solution)/shard_map/pallas_call | solution.py:1281
  332.2 0.0 reduce-scatter.2.cloned.1.call-update
  332.2 0.0 copy-start.2
  332.2 29.3 %shard_map.258 = (bf16[1088,1024]{1,0:T(8,128)(2,1)}, bf16[1088,1536]{1,0:T(8,128)(2,1)}, f32[128,1152]{1,0:T(8,128)}, f32[1,1536]{1,0:T(1,128)}, f32[192,1152]{1,0:T(8,128)}, /*index=5*/f32[192,1152]{1,0:T(8,128)}) custom-call(bf16[1088,1536]{1,0:T(8,128)(2,1)} %get-tuple-element.80.back.rest_5_, bf16[1536,512]{1,0:T(8,128)(2,1)} %get-tuple-element.75.w_out_far.w_out, ...), custom_call_target="tpu_custom_call" | custom-call | flops 8770289664 | bytes 34792288 | tf_op jit(solution)/shard_map/pallas_call | solution.py:1337
  361.5 0.0 copy-done.2
  361.5 0.7 pad_maximum_fusion
  362.2 0.1 reshape.47
  362.4 0.6 pad.9
  363.0 0.4 reduce-scatter.2.cloned.1.call-done.low
  363.4 73.9 %shard_map.259 = (bf16[272,1536]{1,0:T(8,128)(2,1)}, f32[192,1152]{1,0:T(8,128)}, f32[192,512]{1,0:T(8,128)}, f32[192,512]{1,0:T(8,128)}, f32[192,512]{1,0:T(8,1...) custom-call(bf16[272,1536]{1,0:T(8,128)(2,1)} %x.9, f32[272,1536]{1,0:T(8,128)} %get-tuple-element.92.d_resid, ...), custom_call_target="tpu_custom_call" | custom-call | bytes 2238668800 | tf_op jit(solution)/shard_map/pallas_call | solution.py:1281
  437.3 0.0 copy-start.1
  437.3 0.0 copy-start
  437.3 4.0 shard_map.260
  441.3 0.0 copy-done.1
  441.3 0.7 copy.35
  442.1 0.0 copy-done
  442.1 0.9 copy.36
  (2 shorter events, 0.0 us)
Async XLA Ops:
  7.2 103.4 %all-gather.2.cloned.1.call-start = ((), (), s32[]{:S(2)}) async-start(), calls=%async_computation.1 | async-start | bytes 1392640 | tf_op jit(solution)/shard_map/all_gather | solution.py:1443
  82.1 281.3 %reduce-scatter.2.cloned.1.call-start = ((), (), s32[]{:S(2)}) async-start(), calls=%async_computation.2 | async-start | bytes 1740800 | tf_op jit(solution)/shard_map/reduce_scatter | solution.py:1563
  332.2 29.3 %copy-start.2 = (f32[1,1536]{1,0:T(1,128)S(1)}, f32[1,1536]{1,0:T(1,128)}, u32[]{:S(2)}) copy-start(f32[1,1536]{1,0:T(1,128)} %get-tuple-element.96) | copy-start | bytes 18436
  437.3 4.0 copy-start.1
  437.3 4.8 %copy-start = (f32[192,1152]{1,0:T(8,128)S(1)}, f32[192,1152]{1,0:T(8,128)}, u32[]{:S(2)}) copy-start(f32[192,1152]{1,0:T(8,128)} %get-tuple-element.118) | copy-start | bytes 2654212
Sparse Core Ops, SparseCore 0:
  82.2 28.3 all-gather.1
  332.3 31.0 reduce-scatter.1

commit v13 on v12

--- a/solution.py
+++ b/solution.py
@@ -1393,7 +1393,7 @@
             0,
             [tok, grown, grown, grown, shape_of(bf16, 2 * heads, LANE, LANE), shape_of(f32, 16, width)]
             + [shape_of(jnp.int32, *at) for at in ((count, 1), (1, count), (count + TAIL, 1))]
-            + [shape_of(bf16, local_rows, model), shape_of(bf16, local_rows, model // 3)],
+            + [shape_of(bf16, local_rows, model), shape_of(bf16, local_rows, model // 4)],
             False,
             True,
             (
@@ -1439,7 +1439,7 @@
 
     if not fused:
         cot = cotangent * token_mask.astype(bf16)[:, None]
-        cot_first = cot[:, : model // 3]
+        cot_first = cot[:, : model // 4]
     cot_first = lax.all_gather(cot_first, "mp", axis=0, tiled=True)
 
     wide = pltpu.VMEM((count, width), f32)

time: 458 us -> 475 us (1.037)
  blocking collectives: 0 us -> 19.1 us
    all_gather x0 -> x1, blocking collectives: none -> 19.1 us  [shards(): cot_first = lax.all_gather(cot_first, 'mp', axis=0, tiled=True)]
  transfers between devices with their start and end apart: 2 -> 1, of which waited for: 2 -> 1; matrix products, arithmetic and copies ran while one was open for 0% -> 0% of each run, Pallas kernels for 12% -> 6%
where the time goes in v13:
time: 475 us; the launch traced here: 467 us
  Pallas kernels  426 us (90%)
  blocking collectives  19.1 us (4%)
  between operations  14.3 us (3%)
  local copies, waits for them, and re-layouts  5.66 us (1%)
    pallas_call x3, Pallas kernels, line_call(): pl.pallas_call(functools.partial(body, n), out_shape=outs, in_specs=[whol...  369 us
    pallas_call x3, Pallas kernels, local_call(): pl.pallas_call(body, out_shape=outs, in_specs=[whole] * (len(args) - late...  57 us
    all_gather x1, blocking collectives, shards(): cot_first = lax.all_gather(cot_first, 'mp', axis=0, tiled=True)  19.1 us
  transfers between devices with their start and end apart: 1, of which 1 were waited for; matrix products, arithmetic and copies ran while one was open for 0% of the time, Pallas kernels for 6%

profile of v13, /device:TPU:0, one launch (start us, length us, event | category | flops | bytes accessed | tf_op | source)
XLA Modules:
  0.0 467.1 jit_solution(595665114712232577)
XLA Ops:
  7.2 0.0 reduce-scatter.2.cloned.1.call-start
  7.2 1.2 reshape.46.mask
  8.5 0.7 maximum_bitcast_fusion
  9.2 1.4 fusion
  10.6 0.6 pad.8.chan
  11.2 70.9 %shard_map.255 = (bf16[1088,1536]{1,0:T(8,128)(2,1)}, bf16[1536,512]{1,0:T(8,128)(2,1)}, bf16[1536,512]{1,0:T(8,128)(2,1)}, bf16[1536,512]{1,0:T(8,128)(2,1)}, b...) custom-call(bf16[272,1536]{1,0:T(8,128)(2,1)} %x.9, ...), custom_call_target="tpu_custom_call" | custom-call | bytes 231355200 | tf_op jit(solution)/shard_map/pallas_call | solution.py:1281
  82.1 19.1 %all_gather.3.rest_3_ = bf16[1088,384]{1,0:T(8,128)(2,1)} all-gather(bf16[272,384]{1,0:T(8,128)(2,1)} %get-tuple-element.77), channel_id=1, replica_groups=mesh['dp'=8,'mp'=4] {'mp'}, dimensions={0}, use_global_device_ids=true | all-gather | bytes 1044480 | tf_op jit(solution)/shard_map/all_gather | solution.py:1443
  101.2 23.7 %shard_map.256 = (f32[1088,512]{1,0:T(8,128)}, f32[1088,512]{1,0:T(8,128)}, f32[1088,512]{1,0:T(8,128)}, f32[1088,512]{1,0:T(8,128)}, f32[1088,512]{1,0:T(8,128)...) custom-call(bf16[1088,1536]{1,0:T(8,128)(2,1)} %get-tuple-element.67.tokens.rest_6_.rest_4_, ...), custom_call_target="tpu_custom_call" | custom-call | flops 8770289664 | bytes 26194784 | tf_op jit(solution)/shard_map/pallas_call | solution.py:1337
  124.9 224.3 %shard_map.257 = (f32[272,1536]{1,0:T(8,128)}, f32[1,1536]{1,0:T(1,128)}, bf16[1088,1536]{1,0:T(8,128)(2,1)}, bf16[272,896]{1,0:T(8,128)(2,1)}, f32[192,1152]{1,...) custom-call(bf16[272,1536]{1,0:T(8,128)(2,1)} %x.9, ...), custom_call_target="tpu_custom_call" | custom-call | bytes 718233600 | tf_op jit(solution)/shard_map/pallas_call | solution.py:1281
  349.2 0.0 reduce-scatter.2.cloned.1.call-update
  349.2 0.0 copy-start.2
  349.2 29.3 %shard_map.258 = (bf16[1088,1024]{1,0:T(8,128)(2,1)}, bf16[1088,1536]{1,0:T(8,128)(2,1)}, f32[128,1152]{1,0:T(8,128)}, f32[1,1536]{1,0:T(1,128)}, f32[192,1152]{1,0:T(8,128)}, /*index=5*/f32[192,1152]{1,0:T(8,128)}) custom-call(bf16[1088,1536]{1,0:T(8,128)(2,1)} %get-tuple-element.80.back.rest_5_, bf16[1536,512]{1,0:T(8,128)(2,1)} %get-tuple-element.75.w_out_far.w_out, ...), custom_call_target="tpu_custom_call" | custom-call | flops 8770289664 | bytes 34792288 | tf_op jit(solution)/shard_map/pallas_call | solution.py:1337
  378.5 0.0 copy-done.2
  378.6 0.7 pad_maximum_fusion
  379.3 0.1 reshape.47
  379.4 0.6 pad.9
  380.0 0.4 reduce-scatter.2.cloned.1.call-done.low
  380.4 73.9 %shard_map.259 = (bf16[272,1536]{1,0:T(8,128)(2,1)}, f32[192,1152]{1,0:T(8,128)}, f32[192,512]{1,0:T(8,128)}, f32[192,512]{1,0:T(8,128)}, f32[192,512]{1,0:T(8,1...) custom-call(bf16[272,1536]{1,0:T(8,128)(2,1)} %x.9, f32[272,1536]{1,0:T(8,128)} %get-tuple-element.92.d_resid, ...), custom_call_target="tpu_custom_call" | custom-call | bytes 2238668800 | tf_op jit(solution)/shard_map/pallas_call | solution.py:1281
  454.4 0.0 copy-start.1
  454.4 0.0 copy-start
  454.4 4.0 shard_map.260
  458.4 0.0 copy-done.1
  458.4 0.7 copy.35
  459.1 0.0 copy-done
  459.1 0.9 copy.36
  (2 shorter events, 0.0 us)
Async XLA Ops:
  7.2 373.2 %reduce-scatter.2.cloned.1.call-start = ((), (), s32[]{:S(2)}) async-start(), calls=%async_computation.1 | async-start | bytes 1740800 | tf_op jit(solution)/shard_map/reduce_scatter | solution.py:1563
  349.2 29.3 %copy-start.2 = (f32[1,1536]{1,0:T(1,128)S(1)}, f32[1,1536]{1,0:T(1,128)}, u32[]{:S(2)}) copy-start(f32[1,1536]{1,0:T(1,128)} %get-tuple-element.96) | copy-start | bytes 18436
  454.4 4.0 copy-start.1
  454.4 4.8 %copy-start = (f32[192,1152]{1,0:T(8,128)S(1)}, f32[192,1152]{1,0:T(8,128)}, u32[]{:S(2)}) copy-start(f32[192,1152]{1,0:T(8,128)} %get-tuple-element.118) | copy-start | bytes 2654212
Sparse Core Ops, SparseCore 0:
  349.3 31.0 reduce-scatter.1
